TPU v7x, 32 devices: a whole 2x2x4 slice. The times are simulated.
32 devices in a mesh: rep: 8 (over y, x, core), shard: 4 (over z).
Axes of the slice: x: 2, y: 2, z: 4, core: 2. Of those that a mesh axis runs over, the one named last changes fastest.
Arguments:
- tokens: bfloat16 [8192, 1024], P(('rep', 'shard')), may hold values from -6 to 6
- sequence_start: int32 [8192], P(('rep', 'shard')), may hold values from 0 to 255, as said below
- routes: int32 [8192, 8], P(('rep', 'shard')), may hold values from 0 to 15, all different within a row; in each aligned block of 256 rows (0 to 255, 256 to 511, ...) at most 160 rows name the same one
- route_weights: float32 [8192, 8], P(('rep', 'shard')), may hold values from 0.05 to 0.3
- cotangent: bfloat16 [8192, 1024], P(('rep', 'shard')), may hold values from -6 to 6
- query_proj: bfloat16 [1024, 1024], P('shard'), may hold values from -0.1875 to 0.1875
- key_proj: bfloat16 [1024, 512], P('shard'), may hold values from -0.1875 to 0.1875
- value_proj: bfloat16 [1024, 512], P('shard'), may hold values from -0.1875 to 0.1875
- out_proj: bfloat16 [1024, 1024], P('shard'), may hold values from -1.5 to 1.5
- prenorm: bfloat16 [1024], P('shard'), may hold values from 0.5 to 1.5
- midnorm: bfloat16 [1024], P('shard'), may hold values from 0.5 to 1.5
- gate_proj: bfloat16 [16, 1024, 512], P('shard'), may hold values from -0.1875 to 0.1875
- up_proj: bfloat16 [16, 1024, 512], P('shard'), may hold values from -0.1875 to 0.1875
- down_proj: bfloat16 [16, 512, 1024], P('shard'), may hold values from -0.25 to 0.25
- query_moment: float32 [1024, 1024], P('shard'), may hold values from -640 to 640
- key_moment: float32 [1024, 512], P('shard'), may hold values from -640 to 640
- value_moment: float32 [1024, 512], P('shard'), may hold values from -640 to 640
- out_moment: float32 [1024, 1024], P('shard'), may hold values from -640 to 640
- prenorm_moment: float32 [1024], P('shard'), may hold values from -1792 to 1792
- midnorm_moment: float32 [1024], P('shard'), may hold values from -320 to 320
- gate_moment: float32 [16, 1024, 512], P('shard'), may hold values from -128 to 128
- up_moment: float32 [16, 1024, 512], P('shard'), may hold values from -128 to 128
- down_moment: float32 [16, 512, 1024], P('shard'), may hold values from -128 to 128
Outputs:
- mixed: bfloat16 [8192, 1024], P(('rep', 'shard'))
- grad_tokens: float32 [8192, 1024], P(('rep', 'shard'))
- query_grad: float32 [1024, 1024], P('shard')
- query_next: float32 [1024, 1024], P('shard')
- query_update: float32 [1024, 1024], P('shard')
- key_grad: float32 [1024, 512], P('shard')
- key_next: float32 [1024, 512], P('shard')
- key_update: float32 [1024, 512], P('shard')
- value_grad: float32 [1024, 512], P('shard')
- value_next: float32 [1024, 512], P('shard')
- value_update: float32 [1024, 512], P('shard')
- out_grad: float32 [1024, 1024], P('shard')
- out_next: float32 [1024, 1024], P('shard')
- out_update: float32 [1024, 1024], P('shard')
- prenorm_grad: float32 [1024], P('shard')
- prenorm_next: float32 [1024], P('shard')
- prenorm_update: float32 [1024], P('shard')
- midnorm_grad: float32 [1024], P('shard')
- midnorm_next: float32 [1024], P('shard')
- midnorm_update: float32 [1024], P('shard')
- gate_grad: float32 [16, 1024, 512], P('shard')
- gate_next: float32 [16, 1024, 512], P('shard')
- gate_update: float32 [16, 1024, 512], P('shard')
- up_grad: float32 [16, 1024, 512], P('shard')
- up_next: float32 [16, 1024, 512], P('shard')
- up_update: float32 [16, 1024, 512], P('shard')
- down_grad: float32 [16, 512, 1024], P('shard')
- down_next: float32 [16, 512, 1024], P('shard')
- down_update: float32 [16, 512, 1024], P('shard')
Inputs may be any that keep to these rules, and one draw needn't show every extreme that they name: `sequence_start`: within each device's block of 256 tokens, sequences are contiguous runs; every token holds the block-local index of its run's first token, which holds its own index. Some block is one sequence of all 256 tokens. `routes`: each token names 8 different experts. Among the rows of one device no expert is named by more than 160 rows, and in some device one expert is named by exactly 160.
All inputs are finite; a program needn't handle non-finite values.
Results may differ from a plain program's by a relative error of at most 0.011.
The roundings to bfloat16 on the way count: a program that leaves them out, or rounds other values in their place, can miss the bound.
Values may be sent and summed in bfloat16 or wider, within the bound.
A program may use at most 320 MiB of HBM per device.

v0:
```python
import functools
import math

import jax
import jax.numpy as jnp
from jax import lax
from jax.experimental import pallas as pl
from jax.experimental.pallas import tpu as pltpu
from jax.sharding import PartitionSpec as P

NHEADS = 16
KVHEADS = 8
HEAD = 64
EXPERTS = 16
NS_ITERS = 2
BLOCK = 256


norm_epsilon = 1e-06
rotary_base = 10000.0
momentum_keep = 0.9
rate_matrix = 0.5
rate_gain = 0.0002
newton_first = 3.4445
newton_second = -4.775
newton_third = 2.0315
masked_score = -1e30


def root_scale(values):
    inverse = lax.rsqrt(jnp.mean(values * values, axis=-1, keepdims=True) + norm_epsilon)
    return (values * inverse, inverse)


def root_back(grad_normed, scaling, scaled, inverse):
    grad_scaled = grad_normed * scaling
    inner_mean = jnp.mean(grad_scaled * scaled, axis=-1, keepdims=True)
    return (inverse * (grad_scaled - scaled * inner_mean), jnp.sum(grad_normed * scaled, axis=0))


def rotary_tables(positions):
    half_size = HEAD // 2
    frequency = rotary_base ** (-(jnp.arange(half_size, dtype=jnp.float32) * 2.0) / HEAD)
    angles = positions.astype(jnp.float32)[:, None] * frequency[None, :]
    angles = jnp.concatenate([angles, angles], axis=-1)
    return (jnp.cos(angles)[:, None, :], jnp.sin(angles)[:, None, :])


def rotate_half(values):
    half_size = values.shape[-1] // 2
    return jnp.concatenate([-values[..., half_size:], values[..., :half_size]], axis=-1)


def rotate_back(values):
    half_size = values.shape[-1] // 2
    return jnp.concatenate([values[..., half_size:], -values[..., :half_size]], axis=-1)


def block_scores(query_block, rotated_keys, start_block, sequence_start, offset):
    scores = jnp.einsum(
        "qkgd,tkd->kgqt", query_block, rotated_keys, preferred_element_type=jnp.float32
    ) * (1.0 / math.sqrt(HEAD))
    key_places = jnp.arange(rotated_keys.shape[0], dtype=jnp.int32)
    query_places = offset + jnp.arange(query_block.shape[0], dtype=jnp.int32)
    allowed = (start_block[:, None] == sequence_start[None, :]) & (
        key_places[None, :] <= query_places[:, None]
    )
    return jnp.where(allowed, scores, masked_score)


def attend_forward(queries, rotated_keys, values, sequence_start):
    block_count = queries.shape[0] // BLOCK

    def one_block(pieces):
        query_block, start_block, offset = pieces
        scores = block_scores(query_block, rotated_keys, start_block, sequence_start, offset)
        row_max = jnp.max(scores, axis=-1, keepdims=True)
        exponents = jnp.exp(scores - row_max)
        totals = jnp.sum(exponents, axis=-1, keepdims=True)
        softmax_low = (exponents / totals).astype(jnp.bfloat16)
        attended = jnp.einsum(
            "kgqt,tkd->qkgd", softmax_low, values, preferred_element_type=jnp.float32
        )
        return (attended, row_max + jnp.log(totals))

    shaped = queries.reshape((block_count, BLOCK) + queries.shape[1:])
    offsets = jnp.arange(block_count, dtype=jnp.int32) * BLOCK
    attended, log_total = lax.map(
        one_block, (shaped, sequence_start.reshape(block_count, BLOCK), offsets)
    )
    return (attended.reshape(queries.shape[0], -1), log_total)


def attend_backward(queries, rotated_keys, values, sequence_start, log_total, grad_heads):
    block_count = queries.shape[0] // BLOCK
    score_scale = 1.0 / math.sqrt(HEAD)

    def one_block(running, pieces):
        grad_keys, grad_values = running
        query_block, start_block, offset, log_block, grad_block = pieces
        scores = block_scores(query_block, rotated_keys, start_block, sequence_start, offset)
        softmax_full = jnp.exp(scores - log_block)
        grad_softmax = jnp.einsum(
            "qkgd,tkd->kgqt", grad_block, values, preferred_element_type=jnp.float32
        )
        inner_sum = jnp.sum(softmax_full * grad_softmax, axis=-1, keepdims=True)
        grad_scores = (softmax_full * (grad_softmax - inner_sum)).astype(jnp.bfloat16)
        grad_query = (
            jnp.einsum(
                "kgqt,tkd->qkgd", grad_scores, rotated_keys, preferred_element_type=jnp.float32
            )
            * score_scale
        )
        grad_keys = (
            grad_keys
            + jnp.einsum(
                "kgqt,qkgd->tkd", grad_scores, query_block, preferred_element_type=jnp.float32
            )
            * score_scale
        )
        grad_values = grad_values + jnp.einsum(
            "kgqt,qkgd->tkd",
            softmax_full.astype(jnp.bfloat16),
            grad_block,
            preferred_element_type=jnp.float32,
        )
        return ((grad_keys, grad_values), grad_query)

    shaped = queries.reshape((block_count, BLOCK) + queries.shape[1:])
    grad_shaped = grad_heads.reshape((block_count, BLOCK) + queries.shape[1:])
    offsets = jnp.arange(block_count, dtype=jnp.int32) * BLOCK
    key_zeros = jnp.zeros(rotated_keys.shape, jnp.float32)
    finals, grad_queries = lax.scan(
        one_block,
        (key_zeros, key_zeros),
        (shaped, sequence_start.reshape(block_count, BLOCK), offsets, log_total, grad_shaped),
    )
    return (grad_queries.reshape(queries.shape), finals[0], finals[1])


def newton_parts(grams):
    a, b, c = newton_first, newton_second, newton_third

    def times(left, right):
        return jnp.dot(left, right, preferred_element_type=jnp.float32)

    lows = [gram.astype(jnp.bfloat16) for gram in grams]
    firsts = [b * gram + c * times(low, low) for gram, low in zip(grams, lows)]
    first_lows = [first.astype(jnp.bfloat16) for first in firsts]
    mixes = [times(low, first) for low, first in zip(lows, first_lows)]
    nexts = [
        (a * a) * gram + (2.0 * a) * mix + times(mix.astype(jnp.bfloat16), first)
        for gram, mix, first in zip(grams, mixes, first_lows)
    ]
    next_lows = [gram.astype(jnp.bfloat16) for gram in nexts]
    seconds = [b * gram + c * times(low, low) for gram, low in zip(nexts, next_lows)]
    second_lows = [second.astype(jnp.bfloat16) for second in seconds]
    return list(zip(firsts, first_lows, seconds, second_lows))


def expert_update_kernel(kinds, scale, *refs):
    a = newton_first
    grads_ref = refs[0]
    moments = refs[1 : 1 + len(kinds)]
    outs = refs[1 + len(kinds) :]
    half = grads_ref.shape[3]
    states = []
    for index in range(len(kinds)):
        for e in range(grads_ref.shape[0]):
            grad = grads_ref[e, index].astype(jnp.float32)
            tall = kinds[index] < 2
            if not tall:
                grad = jnp.concatenate([grad[:half], grad[half:]], axis=1)
            moment = momentum_keep * moments[index][e] + grad
            outs[3 * index][e] = grad
            outs[3 * index + 1][e] = moment
            inverse = 1.0 / (jnp.sqrt(jnp.sum(moment * moment)) + 1e-07)
            low = (moment * inverse).astype(jnp.bfloat16)
            sides = (((0,), (0,)), ((), ())) if tall else (((1,), (1,)), ((), ()))
            gram = lax.dot_general(low, low, sides, preferred_element_type=jnp.float32)
            states.append((index, e, tall, inverse, low, gram))
    parts = newton_parts([state[-1] for state in states])
    for (index, e, tall, inverse, low, _), (first, first_low, second, second_low) in zip(
        states, parts
    ):
        rest = a * (first + second) + jnp.dot(
            first_low, second_low, preferred_element_type=jnp.float32
        )
        rest = (-scale * rest).astype(jnp.bfloat16)
        if tall:
            step = jnp.dot(low, rest, preferred_element_type=jnp.float32)
        else:
            step = jnp.dot(rest, low, preferred_element_type=jnp.float32)
        outs[3 * index + 2][e] = (-scale * a * a * inverse) * outs[3 * index + 1][e] + step


def expert_update(grads, kinds, moments):
    count, rows, columns = moments[0].shape
    group = 2 // len(kinds)
    scale = rate_matrix * math.sqrt(max(1.0, columns / rows))
    block = pl.BlockSpec((group, rows, columns), lambda i: (i, 0, 0))
    place = kinds[0] // len(kinds)
    taken = pl.BlockSpec((group, len(kinds)) + grads.shape[2:], lambda i: (i, place, 0, 0))
    shape = jax.ShapeDtypeStruct(moments[0].shape, jnp.float32)
    return pl.pallas_call(
        functools.partial(expert_update_kernel, kinds, scale),
        grid=(count // group,),
        in_specs=[taken] + [block] * len(kinds),
        out_specs=[block] * (3 * len(kinds)),
        out_shape=[shape] * (3 * len(kinds)),
        compiler_params=pltpu.CompilerParams(vmem_limit_bytes=60 * 1024 * 1024),
        name="expert_update",
        cost_estimate=pl.CostEstimate(
            flops=count * len(kinds) * 2500000000,
            bytes_accessed=moments[0].size * len(kinds) * 18,
            transcendentals=0,
        ),
    )(grads, *moments)


def dense_update_kernel(layout, place_ref, grads_ref, moments_ref, *refs):
    a = newton_first
    amount = len(layout)
    own_moments = refs[:amount]
    outs = refs[amount : 4 * amount]
    whole, own_grads = refs[4 * amount :]
    blocks, count, block_rows, width = grads_ref.shape
    part = width // 3
    me = place_ref[0]
    start = pl.multiple_of(me * block_rows, block_rows)
    for block in range(blocks):
        for index in range(3):
            columns = slice(8 * part * index + block * part, 8 * part * index + (block + 1) * part)
            inner = slice(index * part, (index + 1) * part)
            outer = slice(block * part, (block + 1) * part)
            grads = grads_ref[block, :, :, inner].reshape(count * block_rows, part)
            moments = moments_ref[index, :, :, outer].reshape(count * block_rows, part)
            whole[:, columns] = (
                momentum_keep * moments.astype(jnp.float32) + grads.astype(jnp.float32)
            ).astype(jnp.bfloat16)
            own_grads[:, columns] = grads_ref[block, me, :, inner].astype(jnp.float32)
    for group in ((0, 1), (2, 3)):
        states = []
        for index in group:
            begin, size = layout[index]
            grad_out, next_out, _ = outs[3 * index : 3 * index + 3]
            columns = slice(begin, begin + size)
            grad = own_grads[:, columns]
            grad_out[...] = grad
            next_out[...] = momentum_keep * own_moments[index][...] + grad
            matrix = whole[:, columns].astype(jnp.float32)
            inverse = 1.0 / (jnp.sqrt(jnp.sum(matrix * matrix)) + 1e-07)
            low = (matrix * inverse).astype(jnp.bfloat16)
            gram = lax.dot_general(
                low, low, (((0,), (0,)), ((), ())), preferred_element_type=jnp.float32
            )
            own = whole[pl.ds(start, block_rows), columns].astype(jnp.float32) * inverse
            states.append((index, size, own, gram))
        parts = newton_parts([state[-1] for state in states])
        for (index, size, own, _), (_, first_low, _, second_low) in zip(states, parts):
            scale = rate_matrix * math.sqrt(max(1.0, size / (count * block_rows)))
            once = a * own + jnp.dot(
                own.astype(jnp.bfloat16), first_low, preferred_element_type=jnp.float32
            )
            outs[3 * index + 2][...] = (-scale) * (
                a * once
                + jnp.dot(
                    once.astype(jnp.bfloat16), second_low, preferred_element_type=jnp.float32
                )
            )


def dense_update(grads, gathered, own_moments, layout, shard_index):
    _, count, block_rows, width = gathered.shape
    moments = pl.BlockSpec((3, count, block_rows, width), lambda i: (1, 0, 0, 0))
    whole = lambda shape: pl.BlockSpec(shape, lambda i: (0,) * len(shape))
    shapes = []
    for _, size in layout:
        shapes += [jax.ShapeDtypeStruct((block_rows, size), jnp.float32)] * 3
    return pl.pallas_call(
        functools.partial(dense_update_kernel, layout),
        grid=(1,),
        in_specs=[pl.BlockSpec(memory_space=pltpu.SMEM), whole(grads.shape), moments]
        + [whole(moment.shape) for moment in own_moments],
        out_specs=[whole(shape.shape) for shape in shapes],
        out_shape=shapes,
        scratch_shapes=[
            pltpu.VMEM((count * block_rows, 3 * width), jnp.bfloat16),
            pltpu.VMEM((block_rows, 3 * width), jnp.float32),
        ],
        compiler_params=pltpu.CompilerParams(vmem_limit_bytes=63 * 1024 * 1024),
        name="dense_update",
        cost_estimate=pl.CostEstimate(
            flops=28000000000, bytes_accessed=24 * width * width, transcendentals=0
        ),
    )(shard_index.reshape(1).astype(jnp.int32), grads, gathered, *own_moments)


LAYOUT = ((0, 1024), (1024, 512), (1536, 512), (2048, 1024))


MESH = pl.DeviceIdType.MESH


def flip(index, bit):
    return index + bit - 2 * bit * ((index // bit) % 2)


def greet(peers):
    barrier = pltpu.get_barrier_semaphore()
    for peer in peers:
        pl.semaphore_signal(barrier, inc=1, device_id=peer, device_id_type=MESH)
    pl.semaphore_wait(barrier, len(peers))


def stream_plan(rep, bits, base, size):
    stages = []
    starts = [base, base + size]
    for step in range(len(bits)):
        size = size // 2
        stage = []
        for stream in range(2):
            bit = bits[(step + stream) % len(bits)]
            side = (rep // bit) % 2
            keep = starts[stream] + side * size
            send = starts[stream] + (1 - side) * size
            starts[stream] = keep
            stage.append((bit, stream, keep, send, size))
        stages.append(stage)
    return stages


def rows_of(start, size):
    return pl.ds(pl.multiple_of(start, 16), size)


def moe_kernel(
    count,
    bits,
    own_ref,
    cot_ref,
    weight_ref,
    gate_hbm,
    up_hbm,
    down_hbm,
    out_ref,
    back_ref,
    share_ref,
    tok,
    turned,
    mats,
    hid,
    gate_delta,
    up_delta,
    stage_back,
    stage_out,
    got_back,
    got_out,
    *rest,
):
    landing = rest[: 1 + 2 * len(bits)]
    (
        load_sem,
        right_sem,
        left_sem,
        arrive_sem,
        back_send,
        back_recv,
        out_send,
        out_recv,
        sum_send,
        sum_recv,
    ) = rest[1 + 2 * len(bits) :]
    rep = lax.axis_index("rep")
    me = lax.axis_index("shard")
    experts = mats.shape[0]
    tokens = own_ref.shape[0]
    half = mats.shape[2] // 2
    core = rep % 2

    loads = [
        pltpu.make_async_copy(gate_hbm, mats.at[:, 0], load_sem.at[0]),
        pltpu.make_async_copy(up_hbm, mats.at[:, 1], load_sem.at[1]),
        pltpu.make_async_copy(
            down_hbm.at[:, :, pl.ds(0, half)], mats.at[:, 2, pl.ds(0, half)], load_sem.at[2]
        ),
        pltpu.make_async_copy(
            down_hbm.at[:, :, pl.ds(half, half)], mats.at[:, 2, pl.ds(half, half)], load_sem.at[3]
        ),
    ]
    for load in loads:
        load.start()
    peers = [(rep, lax.rem(me + k, count)) for k in range(1, count)]
    peers += [(flip(rep, bit), me) for bit in (1,) + bits]
    greet(peers)

    right_peer = (rep, jnp.minimum(me + 1, count - 1))
    left_peer = (rep, jnp.maximum(me - 1, 0))

    def hand_on(block, to_right):
        return pltpu.make_async_remote_copy(
            src_ref=tok.at[block],
            dst_ref=tok.at[block],
            send_sem=(right_sem if to_right else left_sem).at[block],
            recv_sem=arrive_sem.at[block],
            device_id=right_peer if to_right else left_peer,
            device_id_type=MESH,
        )

    def returning(stage, got, send_sem, recv_sem, block):
        return pltpu.make_async_remote_copy(
            src_ref=stage.at[block],
            dst_ref=got.at[me],
            send_sem=send_sem.at[block],
            recv_sem=recv_sem.at[me],
            device_id=(rep, block),
            device_id_type=MESH,
        )

    tok[me] = own_ref[...]

    @pl.when(me < count - 1)
    def _():
        hand_on(me, True).start()

    @pl.when(me > 0)
    def _():
        hand_on(me, False).start()

    for load in loads:
        load.wait()

    margin = jnp.minimum(me, count - 1 - me)
    longer = jnp.where(me < count - 1 - me, 1, -1)
    inward = jnp.where(2 * me < count, 1, -1)
    nt = (((1,), (1,)), ((), ()))

    def dot(left, right):
        return jnp.dot(left, right, preferred_element_type=jnp.float32)

    def dot_nt(left, right):
        return lax.dot_general(left, right, nt, preferred_element_type=jnp.float32)

    def visit(j, carry):
        lower = me - j
        upper = me + j

        @pl.when((j > 0) & (lower >= 0))
        def _():
            hand_on(jnp.maximum(lower, 0), True).wait_recv()

            @pl.when(me < count - 1)
            def _():
                hand_on(jnp.maximum(lower, 0), True).start()

        @pl.when((j > 0) & (upper < count))
        def _():
            hand_on(jnp.minimum(upper, count - 1), False).wait_recv()

            @pl.when(me > 0)
            def _():
                hand_on(jnp.minimum(upper, count - 1), False).start()

        near = (j + 1) // 2
        alternating = me + near - 2 * near * (j % 2)
        block = jnp.where(j <= 2 * margin, alternating, me + longer * (j - margin))
        places = pl.ds(pl.multiple_of(block * tokens, tokens), tokens)
        rows = tok[block]
        grads = cot_ref[block]
        turned[:, places] = rows.T
        hiddens = []
        for e in range(experts):
            weight = weight_ref[block, :, e : e + 1]
            u = dot(rows, mats[e, 0])
            w = dot(rows, mats[e, 1])
            gate = 1.0 / (1.0 + jnp.exp(-u))
            act = u * gate
            hidden = (weight * (act * w)).astype(jnp.bfloat16)
            hid[e, :, places] = hidden.T
            hiddens.append(hidden)
            pulled = weight * (
                dot_nt(grads[:, :half], mats[e, 2, :half])
                + dot_nt(grads[:, half:], mats[e, 2, half:])
            )
            gate_delta[e, places] = (pulled * w * (gate + act * (1.0 - gate))).astype(jnp.bfloat16)
            up_delta[e, places] = (pulled * act).astype(jnp.bfloat16)
        for side in range(2):
            part = slice(side * half, (side + 1) * half)
            total_back = None
            total_out = None
            for e in range(experts):
                back = dot_nt(gate_delta[e, places], mats[e, 0, part]) + dot_nt(
                    up_delta[e, places], mats[e, 1, part]
                )
                out = dot(hiddens[e], mats[e, 2, part])
                total_back = back if e == 0 else total_back + back
                total_out = out if e == 0 else total_out + out
            stage_back[block, :, part] = total_back.astype(jnp.bfloat16)
            stage_out[block, :, part] = total_out.astype(jnp.bfloat16)

        @pl.when((j > 0) & ((block - me) * inward > 0))
        def _():
            returning(stage_back, got_back, back_send, back_recv, block).start()

        return carry

    lax.fori_loop(0, count, visit, 0)
    for block in range(count):

        @pl.when((block - me) * inward < 0)
        def _():
            returning(stage_back, got_back, back_send, back_recv, block).start()

    for k in range(1, count):
        returning(stage_out, got_out, out_send, out_recv, lax.rem(me + k, count)).start()

    plan = stream_plan(rep, bits, core * half, half // 2)

    def sum_copy(stage, slot, e, start, size, bit):
        return pltpu.make_async_remote_copy(
            src_ref=mats.at[e, :, rows_of(start, size)],
            dst_ref=landing[slot].at[e],
            send_sem=sum_send.at[slot, e],
            recv_sem=sum_recv.at[slot, e],
            device_id=(flip(rep, bit), me),
            device_id_type=MESH,
        )

    def copies(stage, e):
        if stage == 0:
            return [(sum_copy(0, 0, e, (1 - core) * half, half, 1), 0, core * half, half)]
        return [
            (
                sum_copy(stage, 1 + 2 * (stage - 1) + stream, e, send, size, bit),
                1 + 2 * (stage - 1) + stream,
                keep,
                size,
            )
            for bit, stream, keep, send, size in plan[stage - 1]
        ]

    def finish(stage, e):
        for copy, slot, keep, size in copies(stage, e):
            copy.wait_recv()
            place = rows_of(keep, size)
            for kind in range(3):
                mats[e, kind, place] = (
                    mats[e, kind, place].astype(jnp.float32)
                    + landing[slot][e, kind].astype(jnp.float32)
                ).astype(jnp.bfloat16)

    stages = 1 + len(bits)
    for turn in range(experts + stages):
        if turn < experts:
            e = turn
            for side in range(2):
                part = slice(side * half, (side + 1) * half)
                mats[e, 0, part] = dot(turned[part], gate_delta[e]).astype(jnp.bfloat16)
                mats[e, 1, part] = dot(turned[part], up_delta[e]).astype(jnp.bfloat16)
                mats[e, 2, part] = dot(hid[e], cot_ref[:, :, part].reshape(count * tokens, half)).astype(jnp.bfloat16)
            copies(0, e)[0][0].start()
        for stage in range(stages):
            e = turn - 1 - stage
            if 0 <= e < experts:
                finish(stage, e)
                if stage + 1 < stages:
                    for copy, _, _, _ in copies(stage + 1, e):
                        copy.start()
                else:
                    for _, stream, keep, _, size in plan[-1]:
                        share_ref[e, :, stream] = mats[e, :, rows_of(keep, size)]

    total = stage_back[me].astype(jnp.float32)
    for k in range(1, count):
        source = lax.rem(me + k, count)
        pltpu.make_async_remote_copy(
            src_ref=stage_back.at[source],
            dst_ref=got_back.at[source],
            send_sem=back_send.at[source],
            recv_sem=back_recv.at[source],
            device_id=(rep, source),
            device_id_type=MESH,
        ).wait_recv()
        total = total + got_back[source].astype(jnp.float32)
    back_ref[...] = total
    total = stage_out[me].astype(jnp.float32)
    for k in range(1, count):
        source = lax.rem(me + k, count)
        pltpu.make_async_remote_copy(
            src_ref=stage_out.at[source],
            dst_ref=got_out.at[source],
            send_sem=out_send.at[source],
            recv_sem=out_recv.at[source],
            device_id=(rep, source),
            device_id_type=MESH,
        ).wait_recv()
        total = total + got_out[source].astype(jnp.float32)
    out_ref[...] = total

    for k in range(1, count):
        block = lax.rem(me + k, count)
        returning(stage_back, got_back, back_send, back_recv, block).wait_send()
        returning(stage_out, got_out, out_send, out_recv, block).wait_send()
    for e in range(experts):
        for stage in range(stages):
            for copy, _, _, _ in copies(stage, e):
                copy.wait_send()
    for block in range(count):

        @pl.when((block <= me) & (me < count - 1))
        def _():
            hand_on(block, True).wait_send()

        @pl.when((block >= me) & (me > 0))
        def _():
            hand_on(block, False).wait_send()


def moe(normed, cotangents, weights, gate_proj, up_proj, down_proj, bits, count):
    tokens, width = normed.shape
    experts, _, hidden = gate_proj.shape
    half = width // 2
    low = jnp.bfloat16
    final = (half // 2) >> len(bits)
    vmem = pl.BlockSpec(memory_space=pltpu.VMEM)
    anywhere = pl.BlockSpec(memory_space=pl.ANY)
    landings = [pltpu.VMEM((experts, 3, half, hidden), low)]
    for step in range(len(bits)):
        size = (half // 2) >> (step + 1)
        landings += [pltpu.VMEM((experts, 3, size, hidden), low)] * 2
    slots = len(landings)
    dma = pltpu.SemaphoreType.DMA
    return pl.pallas_call(
        functools.partial(moe_kernel, count, bits),
        in_specs=[vmem, vmem, vmem, anywhere, anywhere, anywhere],
        out_specs=[vmem, vmem, vmem],
        out_shape=[
            jax.ShapeDtypeStruct((tokens, width), jnp.float32),
            jax.ShapeDtypeStruct((tokens, width), jnp.float32),
            jax.ShapeDtypeStruct((experts, 3, 2, final, hidden), low),
        ],
        scratch_shapes=[
            pltpu.VMEM((count, tokens, width), low),
            pltpu.VMEM((width, count * tokens), low),
            pltpu.VMEM((experts, 3, width, hidden), low),
            pltpu.VMEM((experts, hidden, count * tokens), low),
            pltpu.VMEM((experts, count * tokens, hidden), low),
            pltpu.VMEM((experts, count * tokens, hidden), low),
            pltpu.VMEM((count, tokens, width), low),
            pltpu.VMEM((count, tokens, width), low),
            pltpu.VMEM((count, tokens, width), low),
            pltpu.VMEM((count, tokens, width), low),
        ]
        + landings
        + [
            dma((4,)),
            dma((count,)),
            dma((count,)),
            dma((count,)),
            dma((count,)),
            dma((count,)),
            dma((count,)),
            dma((count,)),
            dma((slots, experts)),
            dma((slots, experts)),
        ],
        compiler_params=pltpu.CompilerParams(
            collective_id=1, has_side_effects=True, vmem_limit_bytes=63 * 1024 * 1024
        ),
        name="moe",
        cost_estimate=pl.CostEstimate(
            flops=39000000000, bytes_accessed=20000000, transcendentals=2000000
        ),
    )(normed, cotangents, weights, gate_proj, up_proj, down_proj)


def rep_bits(rep_count):
    bits = []
    bit = 2
    while bit < rep_count:
        bits.append(bit)
        bit = bit * 2
    return tuple(bits)


def spread_kernel(
    count,
    bits,
    share_ref,
    normed_ref,
    delta_ref,
    head_ref,
    branch_ref,
    gains_ref,
    experts_out,
    dense_out,
    gains_out,
    dense_ref,
    total,
    land_core,
    land_first,
    *rest,
):
    later = len(bits) - 1
    land_later = rest[:later]
    (
        piece_send,
        piece_land,
        piece,
        gains_send,
        gains_land,
        gains_all,
        local_sem,
        core_send,
        core_recv,
        half_send,
        half_recv,
        shard_send,
        shard_recv,
        grow_send,
        grow_recv,
        line_send,
        line_recv,
        join_send,
        join_recv,
        expert_send,
        expert_recv,
        gain_send,
        gain_recv,
        gain_line_send,
        gain_line_recv,
    ) = rest[later:]
    rep = lax.axis_index("rep")
    me = lax.axis_index("shard")
    core = rep % 2
    rows = dense_ref.shape[2]
    expert_rows = experts_out.shape[2]
    steps = len(bits)
    streams = range(2)

    def remote(source, target, send_sem, recv_sem, peer):
        return pltpu.make_async_remote_copy(
            src_ref=source,
            dst_ref=target,
            send_sem=send_sem,
            recv_sem=recv_sem,
            device_id=peer,
            device_id_type=MESH,
        )

    def across(bit):
        return (flip(rep, bit), me)

    def order(stream):
        return [bits[(step + stream) % steps] for step in range(steps)]

    def side(bit):
        return (rep // bit) % 2

    plan = stream_plan(rep, bits, core * (expert_rows // 2), expert_rows // 4)
    base = [(core * (expert_rows // 2)) + stream * (expert_rows // 4) for stream in streams]

    def expert_copy(level, stream):
        if level == steps:
            place = rows_of(base[stream], expert_rows // 4)
            peer = across(1)
        else:
            bit, _, keep, _, size = plan[steps - 1 - level][stream]
            place = rows_of(keep, size)
            peer = across(bit)
        source = experts_out.at[:, :, place]
        if level == 0:
            source = share_ref.at[:, :, stream]
        return remote(
            source,
            experts_out.at[:, :, place],
            expert_send.at[level, stream],
            expert_recv.at[level, stream],
            peer,
        )

    def own_copy(stream):
        _, _, keep, _, size = plan[-1][stream]
        return pltpu.make_async_copy(
            share_ref.at[:, :, stream],
            experts_out.at[:, :, rows_of(keep, size)],
            local_sem.at[stream],
        )

    for stream in streams:
        own_copy(stream).start()
    peers = [(rep, lax.rem(me + k, count)) for k in range(1, count)]
    peers += [across(bit) for bit in (1,) + bits]
    greet(peers)

    def core_copy(block):
        return remote(
            dense_ref.at[4 * (1 - core) + block],
            land_core.at[block],
            core_send.at[block],
            core_recv.at[block],
            across(1),
        )

    gain_bits = (1,) + bits

    def gain_copy(stage):
        return remote(
            gains_send.at[stage],
            gains_land.at[stage],
            gain_send.at[stage],
            gain_recv.at[stage],
            across(gain_bits[stage]),
        )

    gains_send[0] = gains_ref[...]
    gain_copy(0).start()
    for stream in streams:
        expert_copy(0, stream).start()

    part = dense_ref.shape[3] // 3
    normed_turned = normed_ref[...].T
    head_turned = head_ref[...].T

    def make_block(block):
        def columns(ref, offset):
            return ref[:, pl.ds(pl.multiple_of(offset + block * part, part), part)]

        pair = jnp.concatenate([columns(delta_ref, 0), columns(delta_ref, 8 * part)], axis=1)
        left = jnp.dot(normed_turned, pair, preferred_element_type=jnp.float32)
        right = jnp.dot(head_turned, columns(branch_ref, 0), preferred_element_type=jnp.float32)
        for line in range(count):
            place = slice(line * rows, (line + 1) * rows)
            dense_ref[block, line, :, : 2 * part] = left[place].astype(jnp.bfloat16)
            dense_ref[block, line, :, 2 * part :] = right[place].astype(jnp.bfloat16)

    for block in range(4):
        make_block(4 * (1 - core) + block)
        core_copy(block).start()
    for block in range(4):
        make_block(4 * core + block)

    def gain_step(stage):
        gain_copy(stage).wait_recv()
        gains_send[stage + 1] = gains_send[stage] + gains_land[stage]
        if stage + 1 < len(gain_bits):
            gain_copy(stage + 1).start()

    first = [side(order(stream)[0]) for stream in streams]
    held = [2 * stream + first[stream] for stream in streams]
    given = [2 * stream + 1 - first[stream] for stream in streams]

    def first_copy(stream):
        return remote(
            total.at[given[stream]],
            land_first.at[stream],
            half_send.at[0, stream],
            half_recv.at[0, stream],
            across(order(stream)[0]),
        )

    def add_core(block):
        for line in range(count):
            total[block, line] = (
                dense_ref[4 * core + block, line].astype(jnp.float32)
                + land_core[block, line].astype(jnp.float32)
            ).astype(jnp.bfloat16)

    for block in range(4):
        core_copy(block).wait_recv()
    for stream in streams:
        add_core(given[stream])
        first_copy(stream).start()
    for stream in streams:
        add_core(held[stream])
    gain_step(0)

    starts = []
    for stream in streams:
        start, size, line = 0, rows, []
        for step in range(1, steps):
            size = size // 2
            near = side(order(stream)[step])
            line.append((start + near * size, start + (1 - near) * size, size))
            start = start + near * size
        starts.append((start, size, line))

    def later_copy(step, stream):
        keep, send, size = starts[stream][2][step - 1]
        return remote(
            total.at[held[stream], :, rows_of(send, size)],
            land_later[step - 1].at[stream],
            half_send.at[step, stream],
            half_recv.at[step, stream],
            across(order(stream)[step]),
        )

    for stream in streams:
        first_copy(stream).wait_recv()
        for line in range(count):
            total[held[stream], line] = (
                total[held[stream], line].astype(jnp.float32)
                + land_first[stream, line].astype(jnp.float32)
            ).astype(jnp.bfloat16)
        if steps > 1:
            later_copy(1, stream).start()
    gain_step(1)

    for stream in streams:
        own_copy(stream).wait()
        expert_copy(0, stream).wait_recv()
        if steps > 1:
            expert_copy(1, stream).start()

    for step in range(1, steps):
        for stream in streams:
            later_copy(step, stream).wait_recv()
            keep, _, size = starts[stream][2][step - 1]
            for line in range(count):
                place = rows_of(keep, size)
                total[held[stream], line, place] = (
                    total[held[stream], line, place].astype(jnp.float32)
                    + land_later[step - 1][stream, line].astype(jnp.float32)
                ).astype(jnp.bfloat16)
            if step + 1 < steps:
                later_copy(step + 1, stream).start()
        gain_step(step + 1)

    last = starts[0][1]
    places = [rows_of(starts[stream][0], last) for stream in streams]
    for stream in streams:
        for line in range(count):
            piece_send[line, stream] = total[held[stream], line, places[stream]]

    def shard_copy(k):
        target = lax.rem(me + k, count)
        return remote(
            piece_send.at[target],
            piece_land.at[me],
            shard_send.at[target],
            shard_recv.at[me],
            (rep, target),
        )

    def shard_arrival(source):
        return remote(
            piece_send.at[source],
            piece_land.at[source],
            shard_send.at[source],
            shard_recv.at[source],
            (rep, source),
        )

    def gain_line(k):
        target = lax.rem(me + k, count)
        return remote(
            gains_send.at[len(gain_bits)],
            gains_all.at[me],
            gain_line_send.at[target],
            gain_line_recv.at[me],
            (rep, target),
        )

    def gain_arrival(source):
        return remote(
            gains_send.at[len(gain_bits)],
            gains_all.at[source],
            gain_line_send.at[source],
            gain_line_recv.at[source],
            (rep, source),
        )

    for k in range(1, count):
        shard_copy(k).start()
        gain_line(k).start()
    summed = piece_send[me].astype(jnp.float32)
    for k in range(1, count):
        source = lax.rem(me + k, count)
        shard_arrival(source).wait_recv()
        summed = summed + piece_land[source].astype(jnp.float32)
    piece[...] = summed.astype(jnp.bfloat16)

    def line_copy(k, stream):
        target = lax.rem(me + k, count)
        return remote(
            piece.at[stream],
            dense_out.at[4 * core + held[stream], me, places[stream]],
            line_send.at[stream, target],
            line_recv.at[stream, me],
            (rep, target),
        )

    def line_arrival(source, stream):
        return remote(
            piece.at[stream],
            dense_out.at[4 * core + held[stream], source, places[stream]],
            line_send.at[stream, source],
            line_recv.at[stream, source],
            (rep, source),
        )

    def own_piece(stream):
        return pltpu.make_async_copy(
            piece.at[stream],
            dense_out.at[4 * core + held[stream], me, places[stream]],
            local_sem.at[2 + stream],
        )

    for stream in streams:
        own_piece(stream).start()
        for k in range(1, count):
            line_copy(k, stream).start()
    gained = gains_send[len(gain_bits)]
    for k in range(1, count):
        source = lax.rem(me + k, count)
        gain_arrival(source).wait_recv()
        gained = gained + gains_all[source]
    gains_out[...] = gained

    for level in range(1, steps):
        for stream in streams:
            expert_copy(level, stream).wait_recv()
            expert_copy(level + 1, stream).start()
    if steps == 1:
        for stream in streams:
            expert_copy(1, stream).start()

    def grow_copy(step, stream):
        if step == 0:
            place = dense_out.at[4 * core + held[stream]]
        else:
            keep, _, size = starts[stream][2][step - 1]
            place = dense_out.at[4 * core + held[stream], :, rows_of(keep, size)]
        return remote(
            place,
            place,
            grow_send.at[step, stream],
            grow_recv.at[step, stream],
            across(order(stream)[step]),
        )

    for stream in streams:
        own_piece(stream).wait()
        for k in range(1, count):
            line_arrival(lax.rem(me + k, count), stream).wait_recv()
        grow_copy(steps - 1, stream).start()
    for step in reversed(range(steps)):
        for stream in streams:
            grow_copy(step, stream).wait_recv()
            if step > 0:
                grow_copy(step - 1, stream).start()

    def join_copy(stream):
        place = dense_out.at[pl.ds(4 * core + 2 * stream, 2)]
        return remote(place, place, join_send.at[stream], join_recv.at[stream], across(1))

    for stream in streams:
        join_copy(stream).start()
    for stream in streams:
        join_copy(stream).wait()
        expert_copy(steps, stream).wait()
        for level in range(steps):
            expert_copy(level, stream).wait_send()
        first_copy(stream).wait_send()
        for step in range(1, steps):
            later_copy(step, stream).wait_send()
        for k in range(1, count):
            line_copy(k, stream).wait_send()
        for step in range(steps):
            grow_copy(step, stream).wait_send()
    for block in range(4):
        core_copy(block).wait_send()
    for stage in range(len(gain_bits)):
        gain_copy(stage).wait_send()
    for k in range(1, count):
        shard_copy(k).wait_send()
        gain_line(k).wait_send()


def spread(share, normed, deltas, head_low, branch, gains, bits, count):
    experts, _, _, final, hidden = share.shape
    rows = normed.shape[1] // count
    width = 3 * normed.shape[1] // 8
    dense_shape = (8, count, rows, width)
    steps = len(bits)
    last = rows >> (steps - 1)
    low = jnp.bfloat16
    vmem = pl.BlockSpec(memory_space=pltpu.VMEM)
    dma = pltpu.SemaphoreType.DMA
    return pl.pallas_call(
        functools.partial(spread_kernel, count, bits),
        in_specs=[vmem] * 6,
        out_specs=[vmem, vmem, vmem],
        out_shape=[
            jax.ShapeDtypeStruct((experts, 3, 4 * (final << steps), hidden), low),
            jax.ShapeDtypeStruct(dense_shape, low),
            jax.ShapeDtypeStruct(gains.shape, jnp.float32),
        ],
        scratch_shapes=[
            pltpu.VMEM(dense_shape, low),
            pltpu.VMEM((4, count, rows, width), low),
            pltpu.VMEM((4, count, rows, width), low),
            pltpu.VMEM((2, count, rows, width), low),
        ]
        + [pltpu.VMEM((2, count, rows >> step, width), low) for step in range(1, steps)]
        + [
            pltpu.VMEM((count, 2, last, width), low),
            pltpu.VMEM((count, 2, last, width), low),
            pltpu.VMEM((2, last, width), low),
            pltpu.VMEM((steps + 2,) + gains.shape, jnp.float32),
            pltpu.VMEM((steps + 1,) + gains.shape, jnp.float32),
            pltpu.VMEM((count,) + gains.shape, jnp.float32),
            dma((4,)),
            dma((4,)),
            dma((4,)),
            dma((steps, 2)),
            dma((steps, 2)),
            dma((count,)),
            dma((count,)),
            dma((steps, 2)),
            dma((steps, 2)),
            dma((2, count)),
            dma((2, count)),
            dma((2,)),
            dma((2,)),
            dma((steps + 1, 2)),
            dma((steps + 1, 2)),
            dma((steps + 1,)),
            dma((steps + 1,)),
            dma((count,)),
            dma((count,)),
        ],
        compiler_params=pltpu.CompilerParams(
            collective_id=2, has_side_effects=True, vmem_limit_bytes=60 * 1024 * 1024
        ),
        name="spread",
    )(share, normed, deltas, head_low, branch, gains)


def gather_kernel(
    count,
    bits,
    own_ref,
    small_ref,
    full_out,
    small_out,
    local_sem,
    line_send,
    line_recv,
    grow_send,
    grow_recv,
    join_send,
    join_recv,
    small_send,
    small_recv,
):
    rep = lax.axis_index("rep")
    me = lax.axis_index("shard")
    core = rep % 2
    steps = len(bits)
    streams = range(2)
    rows = own_ref.shape[1]
    half = own_ref.shape[2] // 2
    fine = half // 4
    groups = 2
    depth = own_ref.shape[0] // groups
    others = [lax.rem(me + k, count) for k in range(1, count)]

    def columns_of(start, size):
        return pl.ds(pl.multiple_of(start, 128), size)

    def order(stream):
        return [bits[(step + stream) % steps] for step in range(steps)]

    def side(bit):
        return (rep // bit) % 2

    own_copy = pltpu.make_async_copy(own_ref, full_out.at[:, me], local_sem.at[0])
    own_copy.start()
    own_small = pltpu.make_async_copy(small_ref, small_out.at[me], local_sem.at[1])
    own_small.start()
    peers = [(rep, other) for other in others]
    peers += [(flip(rep, bit), me) for bit in (1,) + bits]
    greet(peers)

    regions = []
    for stream in streams:
        column = core * half + stream * 2 * fine
        narrow = columns_of(column + side(order(stream)[0]) * fine, fine)
        start, size = 0, rows
        held = [(pl.ds(0, rows), narrow)]
        for step in range(1, steps):
            size = size // 2
            start = start + side(order(stream)[step]) * size
            held.append((rows_of(start, size), narrow))
        regions.append((held, columns_of(column, 2 * fine)))

    def remote(source, target, send_sem, recv_sem, peer):
        return pltpu.make_async_remote_copy(
            src_ref=source,
            dst_ref=target,
            send_sem=send_sem,
            recv_sem=recv_sem,
            device_id=peer,
            device_id_type=MESH,
        )

    def slab(group):
        return pl.ds(group * depth, depth)

    def line_copy(group, stream, source, peer):
        place, columns = regions[stream][0][-1]
        return remote(
            own_ref.at[slab(group), place, columns],
            full_out.at[slab(group), source, place, columns],
            line_send.at[group, stream, peer],
            line_recv.at[group, stream, source],
            (rep, peer),
        )

    def grow_copy(step, group, stream, source):
        place, columns = regions[stream][0][step]
        part = full_out.at[slab(group), source, place, columns]
        return remote(
            part,
            part,
            grow_send.at[step, group, stream, source],
            grow_recv.at[step, group, stream, source],
            (flip(rep, order(stream)[step]), me),
        )

    def join_copy(group, stream, source):
        part = full_out.at[slab(group), source, :, regions[stream][1]]
        return remote(
            part,
            part,
            join_send.at[group, stream, source],
            join_recv.at[group, stream, source],
            (flip(rep, 1), me),
        )

    def small_copy(source, peer):
        return remote(
            small_ref,
            small_out.at[source],
            small_send.at[peer],
            small_recv.at[source],
            (rep, peer),
        )

    for other in others:
        small_copy(me, other).start()
    for group in range(groups):
        for other in others:
            for stream in streams:
                line_copy(group, stream, me, other).start()

    def advance(level, group):
        for other in others:
            for stream in streams:
                if level == 0:
                    line_copy(group, stream, other, other).wait_recv()
                else:
                    grow_copy(steps - level, group, stream, other).wait_recv()
                if level < steps:
                    grow_copy(steps - 1 - level, group, stream, other).start()
                else:
                    join_copy(group, stream, other).start()

    for level in range(steps + 2):
        if level <= steps:
            advance(level, 0)
        if level > 0:
            advance(level - 1, 1)
    for group in range(groups):
        for other in others:
            for stream in streams:
                join_copy(group, stream, other).wait()
                line_copy(group, stream, me, other).wait_send()
                for step in range(steps):
                    grow_copy(step, group, stream, other).wait_send()
    for other in others:
        small_copy(other, other).wait_recv()
        small_copy(me, other).wait_send()
    own_copy.wait()
    own_small.wait()


def gather(own, small, bits, count):
    depth, rows, columns = own.shape
    steps = len(bits)
    vmem = pl.BlockSpec(memory_space=pltpu.VMEM)
    dma = pltpu.SemaphoreType.DMA
    return pl.pallas_call(
        functools.partial(gather_kernel, count, bits),
        in_specs=[vmem, vmem],
        out_specs=[vmem, vmem],
        out_shape=[
            jax.ShapeDtypeStruct((depth, count, rows, columns), own.dtype),
            jax.ShapeDtypeStruct((count,) + small.shape, small.dtype),
        ],
        scratch_shapes=[
            dma((2,)),
            dma((2, 2, count)),
            dma((2, 2, count)),
            dma((steps, 2, 2, count)),
            dma((steps, 2, 2, count)),
            dma((2, 2, count)),
            dma((2, 2, count)),
            dma((count,)),
            dma((count,)),
        ],
        compiler_params=pltpu.CompilerParams(
            collective_id=3, has_side_effects=True, vmem_limit_bytes=32 * 1024 * 1024
        ),
        name="gather",
    )(own, small)


def local(
    tokens,
    sequence_start,
    routes,
    route_weights,
    cotangent,
    query_proj,
    key_proj,
    value_proj,
    out_proj,
    prenorm,
    midnorm,
    gate_proj,
    up_proj,
    down_proj,
    query_moment,
    key_moment,
    value_moment,
    out_moment,
    prenorm_moment,
    midnorm_moment,
    gate_moment,
    up_moment,
    down_moment,
):
    shard_index = lax.axis_index("shard")
    rep_count = lax.axis_size("rep")
    shard_count = lax.axis_size("shard")
    row_block, width = query_proj.shape
    bits = rep_bits(rep_count)
    experts_here = gate_proj.shape[0]
    low = jnp.bfloat16
    own_rows = jnp.stack(
        [
            query_proj,
            jnp.concatenate([key_proj, value_proj], axis=1),
            out_proj,
            query_moment.astype(low),
            jnp.concatenate([key_moment.astype(low), value_moment.astype(low)], axis=1),
            out_moment.astype(low),
        ]
    )
    dense_weights = jnp.sum(
        jnp.where(
            routes.T[None, :, :] == jnp.arange(EXPERTS, dtype=jnp.int32)[:, None, None],
            route_weights.T[None, :, :],
            0.0,
        ),
        axis=1,
    )
    gain_rows = jnp.pad(
        jnp.stack([prenorm, midnorm]).astype(jnp.float32),
        ((0, 6), (0, tokens.shape[0] - row_block)),
    )
    cotangent_all = lax.all_gather(cotangent, "shard", axis=0)
    gathered, small = gather(
        own_rows, jnp.concatenate([dense_weights, gain_rows], axis=0), bits, shard_count
    )
    full_query = gathered[0].reshape(width, width)
    full_pair = gathered[1].reshape(width, width)
    full_out = gathered[2].reshape(width, width)
    full_key = full_pair[:, : width // 2]
    full_value = full_pair[:, width // 2 :]
    gain_before = small[:, EXPERTS, :row_block].reshape(width)
    gain_after = small[:, EXPERTS + 1, :row_block].reshape(width)
    expert_weights = lax.dynamic_slice_in_dim(
        small, shard_index * experts_here, experts_here, 1
    ).transpose(0, 2, 1)
    group_size = NHEADS // KVHEADS
    token_count = tokens.shape[0]
    inputs = tokens.astype(jnp.float32)
    scaled_first, inverse_first = root_scale(inputs)
    normed_first = (scaled_first * gain_before).astype(jnp.bfloat16)
    query_linear = jnp.dot(normed_first, full_query, preferred_element_type=jnp.float32).reshape(
        token_count, NHEADS, HEAD
    )
    key_linear = jnp.dot(normed_first, full_key, preferred_element_type=jnp.float32).reshape(
        token_count, KVHEADS, HEAD
    )
    values = (
        jnp.dot(normed_first, full_value, preferred_element_type=jnp.float32)
        .astype(jnp.bfloat16)
        .reshape(token_count, KVHEADS, HEAD)
    )
    cosine_table, sine_table = rotary_tables(
        jnp.arange(token_count, dtype=jnp.int32) - sequence_start
    )
    queries = (
        (query_linear * cosine_table + rotate_half(query_linear) * sine_table)
        .astype(jnp.bfloat16)
        .reshape(token_count, KVHEADS, group_size, HEAD)
    )
    rotated_keys = (key_linear * cosine_table + rotate_half(key_linear) * sine_table).astype(
        jnp.bfloat16
    )
    head_out, log_total = attend_forward(queries, rotated_keys, values, sequence_start)
    head_low = head_out.astype(jnp.bfloat16)
    middle = inputs + jnp.dot(head_low, full_out, preferred_element_type=jnp.float32)
    scaled_second, inverse_second = root_scale(middle)
    normed_second = (scaled_second * gain_after).astype(jnp.bfloat16)
    returned, grad_second, expert_share = moe(
        normed_second,
        cotangent_all,
        expert_weights,
        gate_proj,
        up_proj,
        down_proj,
        bits,
        shard_count,
    )
    mixed = middle + returned
    grad_mixed = cotangent.astype(jnp.float32)
    middle_extra, midnorm_part = root_back(grad_second, gain_after, scaled_second, inverse_second)
    grad_middle = grad_mixed + middle_extra
    grad_branch = grad_middle.astype(jnp.bfloat16)
    grad_heads = (
        jnp.einsum("td,qd->tq", grad_branch, full_out, preferred_element_type=jnp.float32)
        .astype(jnp.bfloat16)
        .reshape(queries.shape)
    )
    grad_queries, grad_keys, grad_values = attend_backward(
        queries, rotated_keys, values, sequence_start, log_total, grad_heads
    )
    grad_queries = grad_queries.reshape(token_count, NHEADS, HEAD)
    query_delta = (
        (grad_queries * cosine_table + rotate_back(grad_queries * sine_table))
        .astype(jnp.bfloat16)
        .reshape(token_count, -1)
    )
    key_delta = (
        (grad_keys * cosine_table + rotate_back(grad_keys * sine_table))
        .astype(jnp.bfloat16)
        .reshape(token_count, -1)
    )
    value_delta = grad_values.astype(jnp.bfloat16).reshape(token_count, -1)
    grad_first = (
        jnp.einsum("tq,dq->td", query_delta, full_query, preferred_element_type=jnp.float32)
        + jnp.einsum("tq,dq->td", key_delta, full_key, preferred_element_type=jnp.float32)
        + jnp.einsum("tq,dq->td", value_delta, full_value, preferred_element_type=jnp.float32)
    )
    input_extra, prenorm_part = root_back(grad_first, gain_before, scaled_first, inverse_first)
    grad_tokens = grad_middle + input_extra
    deltas = jnp.concatenate([query_delta, key_delta, value_delta], axis=1)
    gains_local = jnp.concatenate(
        [jnp.stack([prenorm_part, midnorm_part]), jnp.zeros((6, prenorm_part.shape[0]))], axis=0
    )
    expert_grads, dense_grads, gains_grad = spread(
        expert_share,
        normed_first,
        deltas,
        head_low,
        grad_branch,
        gains_local,
        bits,
        shard_count,
    )
    gains_here = lax.dynamic_slice_in_dim(gains_grad, shard_index * row_block, row_block, 1)
    prenorm_grad = gains_here[0]
    midnorm_grad = gains_here[1]
    prenorm_next = momentum_keep * prenorm_moment + prenorm_grad
    midnorm_next = momentum_keep * midnorm_moment + midnorm_grad
    prenorm_update = -rate_gain * prenorm_next
    midnorm_update = -rate_gain * midnorm_next
    (
        query_grad,
        query_next,
        query_update,
        key_grad,
        key_next,
        key_update,
        value_grad,
        value_next,
        value_update,
        out_grad,
        out_next,
        out_update,
    ) = dense_update(
        dense_grads,
        gathered,
        (query_moment, key_moment, value_moment, out_moment),
        LAYOUT,
        shard_index,
    )
    gate_grad, gate_next, gate_update, up_grad, up_next, up_update = expert_update(
        expert_grads, (0, 1), (gate_moment, up_moment)
    )
    down_grad, down_next, down_update = expert_update(expert_grads, (2,), (down_moment,))
    return (
        mixed.astype(jnp.bfloat16),
        grad_tokens,
        query_grad,
        query_next,
        query_update,
        key_grad,
        key_next,
        key_update,
        value_grad,
        value_next,
        value_update,
        out_grad,
        out_next,
        out_update,
        prenorm_grad,
        prenorm_next,
        prenorm_update,
        midnorm_grad,
        midnorm_next,
        midnorm_update,
        gate_grad,
        gate_next,
        gate_update,
        up_grad,
        up_next,
        up_update,
        down_grad,
        down_next,
        down_update,
    )


def solution(mesh):
    return jax.shard_map(
        local,
        mesh=mesh,
        in_specs=(
            P(("rep", "shard"), None),
            P(("rep", "shard")),
            P(("rep", "shard"), None),
            P(("rep", "shard"), None),
            P(("rep", "shard"), None),
            P("shard", None),
            P("shard", None),
            P("shard", None),
            P("shard", None),
            P("shard"),
            P("shard"),
            P("shard", None, None),
            P("shard", None, None),
            P("shard", None, None),
            P("shard", None),
            P("shard", None),
            P("shard", None),
            P("shard", None),
            P("shard"),
            P("shard"),
            P("shard", None, None),
            P("shard", None, None),
            P("shard", None, None),
        ),
        out_specs=(
            P(("rep", "shard"), None),
            P(("rep", "shard"), None),
            P("shard", None),
            P("shard", None),
            P("shard", None),
            P("shard", None),
            P("shard", None),
            P("shard", None),
            P("shard", None),
            P("shard", None),
            P("shard", None),
            P("shard", None),
            P("shard", None),
            P("shard", None),
            P("shard"),
            P("shard"),
            P("shard"),
            P("shard"),
            P("shard"),
            P("shard"),
            P("shard", None, None),
            P("shard", None, None),
            P("shard", None, None),
            P("shard", None, None),
            P("shard", None, None),
            P("shard", None, None),
            P("shard", None, None),
            P("shard", None, None),
            P("shard", None, None),
        ),
        check_vma=False,
    )
```

profile of v0, /device:TPU:0, one launch (start us, length us, event | category | flops | bytes accessed | tf_op | source)
XLA Modules:
  0.0 553.0 jit_solution(3542258939763298282)
XLA Ops:
  9.3 1.1 convert_element_type.93
  10.4 1.2 convert_element_type.94
  11.6 1.1 bitcast_dynamic-update-slice_fusion.3
  13.2 86.4 %gather.1 = (bf16[6,4,256,1024]{3,2,1,0:T(8,128)(2,1)S(1)}, f32[4,24,256]{2,1,0:T(8,128)S(1)}) custom-call(bf16[6,256,1024]{2,1,0:T(8,128)(2,1)S(1)} %bitcast_dynamic-update-slice_fusion.own_ref, f32[24,256]{1,0:T(8,128)S(1)} %pad_maximum_fusion.3.small_ref), custom_call_target="tpu_custom_call" | custom-call | tf_op jit(solution)/shard_map/gather/pallas_call | solution.py:1294
  99.6 4.5 copy-done
  104.7 1.0 copy.90
  105.9 5.1 fusion.52
  111.3 1.7 convolution_convert_fusion.1
  113.0 1.3 fusion.32
  114.4 0.8 broadcast_multiply_fusion.2
  115.2 1.1 mul.259
  116.3 2.5 copy.96
  118.8 1.1 copy.86
  119.9 2.0 slice_negate_fusion.3
  121.9 2.5 copy.88
  124.4 2.4 fusion.41
  127.4 0.8 fusion.57
  128.8 1.1 copy-done.42
  129.9 1.7 fusion.13
  131.6 2.2 copy.100.head_ref
  134.4 2.0 dynamic-slice_bitcast_fusion.weight_ref
  136.4 1.9 multiply_reduce_fusion.2
  138.3 0.9 copy-done.3
  139.3 0.9 multiply_convert_fusion.own_ref
  140.2 126.7 %moe.1 = (f32[256,1024]{1,0:T(8,128)}, f32[256,1024]{1,0:T(8,128)}, bf16[4,3,2,64,512]{4,3,2,1,0:T(8,128)(2,1)}) custom-call(bf16[256,1024]{1,0:T(8,128)(2,1)} %multiply_convert_fusion.own_ref, bf16[4,256,1024]{2,1,0:T(8,128)(2,1)} %bitcast.162, f32[4,256,4]{2,1,0:T(8,128)} %dynamic-slice_bitcast_fusion.weight_ref, bf16[4,1024,512]{2,1,0:T(8,128)(2,1)} %gate_hbm.1, ...), custom_call_target="tpu_custom_call" | custom-call | flops 38999998464 | bytes 20000000 | tf_op jit(solution)/shard_map/moe/pallas_call | solution.py:633
  266.9 2.1 multiply_reduce_fusion
  269.0 2.0 fusion.51.branch_ref
  271.0 0.8 copy-done.24
  271.8 0.7 convolution_convert_fusion
  272.8 3.1 fusion.17
  276.3 3.0 fusion
  279.2 0.8 copy.99
  280.1 4.4 fusion.2
  285.3 0.8 broadcast_multiply_fusion
  286.2 0.8 copy.98
  287.3 1.3 pad_maximum_fusion
  288.6 2.5 copy.97
  291.2 1.9 fusion.58
  293.7 1.7 fusion.25
  295.4 1.3 copy.95
  297.4 1.4 add_convert_fusion
  298.8 1.1 pad_maximum_fusion.1.delta_ref
  299.9 139.4 %spread.1 = (bf16[4,3,1024,512]{3,2,1,0:T(8,128)(2,1)}, bf16[8,4,256,384]{3,2,1,0:T(8,128)(2,1)}, f32[8,1024]{1,0:T(8,128)}) custom-call(bf16[4,3,2,64,512]{4,3,2,1,0:T(8,128)(2,1)} %get-tuple-element.119.share_ref, bf16[256,1024]{1,0:T(8,128)(2,1)} %copy-done.16, bf16[256,2048]{1,0:T(8,128)(2,1)} %pad_maximum_fusion.1.delta_ref, ...), custom_call_target="tpu_custom_call" | custom-call | tf_op jit(solution)/shard_map/spread/pallas_call | solution.py:1090
  439.3 46.8 %dense_update.1 = (f32[256,1024]{1,0:T(8,128)}, f32[256,1024]{1,0:T(8,128)}, f32[256,1024]{1,0:T(8,128)}, f32[256,512]{1,0:T(8,128)}, f32[256,512]{1,0:T(8,128)}...) custom-call(s32[1]{0:T(128)} %bitcast.46.place_ref, ...), custom_call_target="tpu_custom_call" | custom-call | flops 28000000000 | bytes 25165824 | tf_op jit(solution)/shard_map/dense_update/pallas_call | solution.py:280
  486.1 19.0 %expert_update.3 = (f32[4,512,1024]{2,1,0:T(8,128)}, f32[4,512,1024]{2,1,0:T(8,128)}, f32[4,512,1024]{2,1,0:T(8,128)}) custom-call(bf16[4,3,1024,512]{3,2,1,0:T(8,128)(2,1)} %get-tuple-element.134.refs_0_, f32[4,512,1024]{2,1,0:T(8,128)} %refs_1_.5), custom_call_target="tpu_custom_call" | custom-call | flops 10000000000 | bytes 37748736 | tf_op jit(solution)/shard_map/expert_update/pallas_call | solution.py:205
  505.1 35.9 %expert_update.2 = (f32[4,1024,512]{2,1,0:T(8,128)}, f32[4,1024,512]{2,1,0:T(8,128)}, f32[4,1024,512]{2,1,0:T(8,128)}, f32[4,1024,512]{2,1,0:T(8,128)}, f32[4,10...) custom-call(bf16[4,3,1024,512]{3,2,1,0:T(8,128)(2,1)} %get-tuple-element.134.refs_0_, f32[4,1024,512]{2,1,0:T(8,128)} %refs_1_.4, ...), custom_call_target="tpu_custom_call" | custom-call | flops 20000000000 | bytes 75497472 | tf_op jit(solution)/shard_map/expert_update/pallas_call | solution.py:205
  541.1 3.2 fusion.24
  544.3 0.8 fusion.56
  (148 shorter events, 8.9 us)
Async XLA Ops:
  7.2 5.5 copy-start.49
  7.2 5.5 copy-start.50
  7.2 5.6 %copy-start.35 = (bf16[256,512]{1,0:T(8,128)(2,1)S(1)}, bf16[256,512]{1,0:T(8,128)(2,1)}, u32[]{:S(2)}) copy-start(bf16[256,512]{1,0:T(8,128)(2,1)} %param.30) | copy-start | bytes 786436
  7.2 5.6 %copy-start.36 = (bf16[256,512]{1,0:T(8,128)(2,1)S(1)}, bf16[256,512]{1,0:T(8,128)(2,1)}, u32[]{:S(2)}) copy-start(bf16[256,512]{1,0:T(8,128)(2,1)} %param.29) | copy-start | bytes 786436
  7.2 5.6 %copy-start.33 = (bf16[256,1024]{1,0:T(8,128)(2,1)S(1)}, bf16[256,1024]{1,0:T(8,128)(2,1)}, u32[]{:S(2)}) copy-start(bf16[256,1024]{1,0:T(8,128)(2,1)} %param.31) | copy-start | bytes 1572868
  7.3 5.7 %copy-start.27 = (f32[256,1024]{1,0:T(8,128)S(1)}, f32[256,1024]{1,0:T(8,128)}, u32[]{:S(2)}) copy-start(f32[256,1024]{1,0:T(8,128)} %refs_0_.1) | copy-start | bytes 3145732
  7.3 132.9 %all-gather.3.cloned.1.call-start = ((), (), s32[]{:S(2)}) async-start(), calls=%async_computation | async-start | bytes 2621440 | tf_op jit(solution)/shard_map/all_gather | solution.py:1374
  10.4 2.7 copy-start.28
  13.0 92.7 %copy-start.7 = (bf16[256,1024]{1,0:T(8,128)(2,1)S(1)}, bf16[256,1024]{1,0:T(8,128)(2,1)}, u32[]{:S(2)}) copy-start(bf16[256,1024]{1,0:T(8,128)(2,1)} %param.23) | copy-start | bytes 1572868
  99.6 4.6 copy-start
  104.7 6.3 %copy-start.40 = (f32[4,1,256]{2,1,0:T(1,128)}, f32[4,1,256]{2,1,0:T(1,128)S(1)}, u32[]{:S(2)}) copy-start(f32[4,1,256]{2,1,0:T(1,128)S(1)} %get-tuple-element.168) | copy-start | bytes 12292
  105.9 5.2 copy-start.46
  111.1 1.9 copy-start.11
  111.1 10.8 %copy-start.5 = (bf16[1,4,256,1024]{3,2,1,0:T(8,128)(2,1)}, bf16[1,4,256,1024]{3,2,1,0:T(8,128)(2,1)S(1)}, u32[]{:S(2)}) copy-start(bf16[1,4,256,1024]{3,2,1,0:T(8,128)(2,1)S(1)} %get-tuple-element.153) | copy-start | bytes 6291460
  111.1 3.3 copy-start.48
  111.3 13.1 %copy-start.16 = (bf16[256,1024]{1,0:T(8,128)(2,1)}, bf16[256,1024]{1,0:T(8,128)(2,1)S(1)}, u32[]{:S(2)}) copy-start(bf16[256,1024]{1,0:T(8,128)(2,1)S(1)} %fusion.20.normed_ref) | copy-start | bytes 1572868
  119.9 9.0 %copy-start.25 = (bf16[256,512]{0,1:T(8,128)(2,1)}, bf16[256,512]{0,1:T(8,128)(2,1)S(1)}, u32[]{:S(2)}) copy-start(bf16[256,512]{0,1:T(8,128)(2,1)S(1)} %copy.86) | copy-start | bytes 786436
  124.4 2.4 copy-start.23
  124.4 2.5 copy-start.29
  124.4 2.5 copy-start.30
  128.2 3.4 copy-start.1
  131.6 4.8 copy-start.13
  131.6 6.7 %copy-start.43 = (f32[8,2,256]{2,1,0:T(2,128)S(1)}, f32[8,2,256]{2,1,0:T(2,128)}, u32[]{:S(2)}) copy-start(f32[8,2,256]{2,1,0:T(2,128)} %copy-done.42) | copy-start | bytes 49156
  131.6 7.7 %copy-start.38 = (f32[4,1,256]{2,1,0:T(1,128)S(1)}, f32[4,1,256]{2,1,0:T(1,128)}, u32[]{:S(2)}) copy-start(f32[4,1,256]{2,1,0:T(1,128)} %get-tuple-element.167) | copy-start | bytes 12292
  138.3 130.7 %copy-start.44 = (f32[256]{0:T(256)}, f32[256]{0:T(256)S(1)}, u32[]{:S(2)}) copy-start(f32[256]{0:T(256)S(1)} %add_rsqrt_fusion) | copy-start | bytes 3076
  266.9 4.9 copy-start.14
  272.6 3.3 copy-start.26
  272.8 3.5 copy-start.2
  280.1 4.4 copy-start.20
  287.3 3.9 copy-start.6
  291.1 2.0 copy-start.12
  291.1 2.0 copy-start.22
  291.1 2.5 copy-start.8
  291.2 2.5 copy-start.41
  291.2 2.5 copy-start.47
  293.7 3.0 copy-start.55
  293.7 3.7 copy-start.17
  293.7 3.7 copy-start.18
  295.4 3.5 copy-start.31
  296.7 2.2 copy-start.32
  505.1 35.9 %copy-start.4 = (f32[256,1024]{1,0:T(8,128)S(1)}, f32[256,1024]{1,0:T(8,128)}, u32[]{:S(2)}) copy-start(f32[256,1024]{1,0:T(8,128)} %copy-done.3) | copy-start | bytes 3145732
  505.1 35.9 %copy-start.9 = (bf16[256,1024]{1,0:T(8,128)(2,1)S(1)}, bf16[256,1024]{1,0:T(8,128)(2,1)}, u32[]{:S(2)}) copy-start(bf16[256,1024]{1,0:T(8,128)(2,1)} %param.23) | copy-start | bytes 1572868
  505.1 35.9 %copy-start.10 = (f32[256,1024]{1,0:T(8,128)S(1)}, f32[256,1024]{1,0:T(8,128)}, u32[]{:S(2)}) copy-start(f32[256,1024]{1,0:T(8,128)} %get-tuple-element.118) | copy-start | bytes 3145732
  505.1 35.9 %copy-start.15 = (bf16[256,1024]{1,0:T(8,128)(2,1)S(1)}, bf16[256,1024]{1,0:T(8,128)(2,1)}, u32[]{:S(2)}) copy-start(bf16[256,1024]{1,0:T(8,128)(2,1)} %param.27) | copy-start | bytes 1572868
  505.1 35.9 %copy-start.39 = (f32[4,1,256]{2,1,0:T(1,128)S(1)}, f32[4,1,256]{2,1,0:T(1,128)}, u32[]{:S(2)}) copy-start(f32[4,1,256]{2,1,0:T(1,128)} %get-tuple-element.167) | copy-start | bytes 12292
  505.1 35.9 %copy-start.45 = (f32[256]{0:T(256)S(1)}, f32[256]{0:T(256)}, u32[]{:S(2)}) copy-start(f32[256]{0:T(256)} %copy-done.44) | copy-start | bytes 3076
  541.0 4.1 copy-start.53
  541.1 4.1 copy-start.54
  (9 other events, 8.3 us)
Sparse Core Ops, SparseCore 0:
  9.7 79.3 all-gather.2
where the time goes:
time: 561 us; the launch traced here: 553 us
  Pallas kernels  454 us (81%)
  local copies, waits for them, and re-layouts  36 us (6%)
  other arithmetic  24.9 us (4%)
  matrix products  21.9 us (4%)
  between operations  15.4 us (3%)
    pallas_call x1, Pallas kernels, spread(): pl.pallas_call(functools.partial(spread_kernel, count, bits), in_specs=[v...  139 us
    pallas_call x1, Pallas kernels, moe(): pl.pallas_call(functools.partial(moe_kernel, count, bits), in_specs=[vmem...  127 us
    pallas_call x1, Pallas kernels, gather(): pl.pallas_call(functools.partial(gather_kernel, count, bits), in_specs=[v...  86.4 us
    pallas_call x2, Pallas kernels, expert_update(): pl.pallas_call(functools.partial(expert_update_kernel, kinds, scale), gri...  54.8 us
    pallas_call x1, Pallas kernels, dense_update(): pl.pallas_call(functools.partial(dense_update_kernel, layout), grid=(1,),...  46.8 us
  transfers between devices with their start and end apart: 1, of which 0 were waited for; matrix products, arithmetic and copies ran while one was open for 7% of the time, Pallas kernels for 16%

commit v1 on v0

--- a/solution.py
+++ b/solution.py
@@ -13,7 +13,6 @@
 HEAD = 64
 EXPERTS = 16
 NS_ITERS = 2
-BLOCK = 256
 
 
 norm_epsilon = 1e-06
@@ -27,115 +26,159 @@
 masked_score = -1e30
 
 
-def root_scale(values):
+def normalize(values):
     inverse = lax.rsqrt(jnp.mean(values * values, axis=-1, keepdims=True) + norm_epsilon)
     return (values * inverse, inverse)
 
 
-def root_back(grad_normed, scaling, scaled, inverse):
+def normalize_back(grad_normed, scaling, scaled, inverse):
     grad_scaled = grad_normed * scaling
     inner_mean = jnp.mean(grad_scaled * scaled, axis=-1, keepdims=True)
-    return (inverse * (grad_scaled - scaled * inner_mean), jnp.sum(grad_normed * scaled, axis=0))
+    return (
+        inverse * (grad_scaled - scaled * inner_mean),
+        jnp.sum(grad_normed * scaled, axis=0, keepdims=True),
+    )
+
+
+def dot_nn(left, right):
+    return jnp.dot(left, right, preferred_element_type=jnp.float32)
+
+
+def dot_nt(left, right):
+    return lax.dot_general(
+        left, right, (((1,), (1,)), ((), ())), preferred_element_type=jnp.float32
+    )
+
+
+def dot_tn(left, right):
+    return lax.dot_general(
+        left, right, (((0,), (0,)), ((), ())), preferred_element_type=jnp.float32
+    )
+
+
+def rotate(values, table_ref, sign):
+    return (
+        values * table_ref[0]
+        + sign * pltpu.roll(values, 96, 1) * table_ref[1]
+        + sign * pltpu.roll(values, 32, 1) * table_ref[2]
+    )
+
+
+def lane_low(shape):
+    return lax.broadcasted_iota(jnp.int32, shape, 1) < HEAD
+
+
+def twice(pair, upper):
+    wide = pair.astype(jnp.float32)
+    turned = pltpu.roll(wide, HEAD, 1)
+    first = lane_low(pair.shape)
+    return jnp.where(first != upper, wide, turned).astype(pair.dtype)
+
+
+def stacked(pair):
+    first = lane_low(pair.shape)
+    zero = jnp.zeros_like(pair)
+    return jnp.concatenate([jnp.where(first, pair, zero), jnp.where(first, zero, pair)], axis=0)
+
+
+def unstacked(rows):
+    half = rows.shape[0] // 2
+    return jnp.where(lane_low((half, rows.shape[1])), rows[:half], rows[half:])
+
+
+def allowed_pairs(start_column, start_row):
+    shape = (start_column.shape[0], start_row.shape[1])
+    query_places = lax.broadcasted_iota(jnp.int32, shape, 0)
+    key_places = lax.broadcasted_iota(jnp.int32, shape, 1)
+    one = (start_column == start_row) & (key_places <= query_places)
+    return jnp.where(jnp.concatenate([one, one], axis=0), 0.0, masked_score)
+
+
+def block_lanes(ref, block):
+    return ref[:, block * 2 * HEAD : (block + 1) * 2 * HEAD]
+
+
+def attend_pair(block, query_ref, pair_ref, bias):
+    key = twice(block_lanes(pair_ref, block // 2), block % 2 == 1)
+    value = twice(block_lanes(pair_ref, KVHEADS // 2 + block // 2), block % 2 == 1)
+    queries = stacked(block_lanes(query_ref, block))
+    scores = dot_nt(queries, key) * (1.0 / math.sqrt(HEAD)) + bias
+    return (queries, key, value, scores)
+
+
+def project_inputs(normed, weights, query_ref, pair_ref, table_ref):
+    queries = dot_nn(normed, weights(0))
+    for block in range(NHEADS // 2):
+        lanes = slice(block * 2 * HEAD, (block + 1) * 2 * HEAD)
+        query_ref[:, lanes] = rotate(queries[:, lanes], table_ref, 1.0).astype(jnp.bfloat16)
+    pairs = dot_nn(normed, weights(1))
+    for block in range(KVHEADS):
+        lanes = slice(block * 2 * HEAD, (block + 1) * 2 * HEAD)
+        value = pairs[:, lanes]
+        if block < KVHEADS // 2:
+            value = rotate(value, table_ref, 1.0)
+        pair_ref[:, lanes] = value.astype(jnp.bfloat16)
+
+
+def attend_forward(blocks, query_ref, pair_ref, bias, head_ref, total_ref):
+    for block in blocks:
+        _, _, value, scores = attend_pair(block, query_ref, pair_ref, bias)
+        row_max = jnp.max(scores, axis=-1, keepdims=True)
+        exponents = jnp.exp(scores - row_max)
+        totals = jnp.sum(exponents, axis=-1, keepdims=True)
+        softmax_low = (exponents * (1.0 / totals)).astype(jnp.bfloat16)
+        head_ref[:, block * 2 * HEAD : (block + 1) * 2 * HEAD] = unstacked(
+            dot_nn(softmax_low, value)
+        ).astype(jnp.bfloat16)
+        total_ref[:, block : block + 1] = row_max + jnp.log(totals)
+
+
+def attend_backward(query_ref, pair_ref, bias, total_ref, grad_ref, table_ref, delta_ref):
+    folded = []
+    for block in range(KVHEADS):
+        queries, key, value, scores = attend_pair(block, query_ref, pair_ref, bias)
+        grads = stacked(block_lanes(grad_ref, block))
+        softmax_full = jnp.exp(scores - total_ref[:, block : block + 1])
+        grad_softmax = dot_nt(grads, value)
+        inner = jnp.sum(softmax_full * grad_softmax, axis=-1, keepdims=True)
+        grad_scores = (softmax_full * (grad_softmax - inner)).astype(jnp.bfloat16)
+        scale = 1.0 / math.sqrt(HEAD)
+        grad_query = unstacked(dot_nn(grad_scores, key)) * scale
+        lanes = slice(block * 2 * HEAD, (block + 1) * 2 * HEAD)
+        delta_ref[:, lanes] = rotate(grad_query, table_ref, -1.0).astype(jnp.bfloat16)
+        grad_key = dot_tn(grad_scores, queries) * scale
+        grad_value = dot_tn(softmax_full.astype(jnp.bfloat16), grads)
+        folded.append(
+            (
+                grad_key + pltpu.roll(grad_key, HEAD, 1),
+                grad_value + pltpu.roll(grad_value, HEAD, 1),
+            )
+        )
+        if block % 2 == 1:
+            first = lane_low(grad_key.shape)
+            both = [jnp.where(first, low, high) for low, high in zip(*folded)]
+            folded = []
+            base = NHEADS * HEAD + (block // 2) * 2 * HEAD
+            delta_ref[:, base : base + 2 * HEAD] = rotate(both[0], table_ref, -1.0).astype(
+                jnp.bfloat16
+            )
+            base = base + KVHEADS * HEAD
+            delta_ref[:, base : base + 2 * HEAD] = both[1].astype(jnp.bfloat16)
 
 
 def rotary_tables(positions):
     half_size = HEAD // 2
     frequency = rotary_base ** (-(jnp.arange(half_size, dtype=jnp.float32) * 2.0) / HEAD)
     angles = positions.astype(jnp.float32)[:, None] * frequency[None, :]
-    angles = jnp.concatenate([angles, angles], axis=-1)
-    return (jnp.cos(angles)[:, None, :], jnp.sin(angles)[:, None, :])
-
-
-def rotate_half(values):
-    half_size = values.shape[-1] // 2
-    return jnp.concatenate([-values[..., half_size:], values[..., :half_size]], axis=-1)
-
-
-def rotate_back(values):
-    half_size = values.shape[-1] // 2
-    return jnp.concatenate([values[..., half_size:], -values[..., :half_size]], axis=-1)
-
-
-def block_scores(query_block, rotated_keys, start_block, sequence_start, offset):
-    scores = jnp.einsum(
-        "qkgd,tkd->kgqt", query_block, rotated_keys, preferred_element_type=jnp.float32
-    ) * (1.0 / math.sqrt(HEAD))
-    key_places = jnp.arange(rotated_keys.shape[0], dtype=jnp.int32)
-    query_places = offset + jnp.arange(query_block.shape[0], dtype=jnp.int32)
-    allowed = (start_block[:, None] == sequence_start[None, :]) & (
-        key_places[None, :] <= query_places[:, None]
-    )
-    return jnp.where(allowed, scores, masked_score)
-
-
-def attend_forward(queries, rotated_keys, values, sequence_start):
-    block_count = queries.shape[0] // BLOCK
-
-    def one_block(pieces):
-        query_block, start_block, offset = pieces
-        scores = block_scores(query_block, rotated_keys, start_block, sequence_start, offset)
-        row_max = jnp.max(scores, axis=-1, keepdims=True)
-        exponents = jnp.exp(scores - row_max)
-        totals = jnp.sum(exponents, axis=-1, keepdims=True)
-        softmax_low = (exponents / totals).astype(jnp.bfloat16)
-        attended = jnp.einsum(
-            "kgqt,tkd->qkgd", softmax_low, values, preferred_element_type=jnp.float32
-        )
-        return (attended, row_max + jnp.log(totals))
-
-    shaped = queries.reshape((block_count, BLOCK) + queries.shape[1:])
-    offsets = jnp.arange(block_count, dtype=jnp.int32) * BLOCK
-    attended, log_total = lax.map(
-        one_block, (shaped, sequence_start.reshape(block_count, BLOCK), offsets)
-    )
-    return (attended.reshape(queries.shape[0], -1), log_total)
-
-
-def attend_backward(queries, rotated_keys, values, sequence_start, log_total, grad_heads):
-    block_count = queries.shape[0] // BLOCK
-    score_scale = 1.0 / math.sqrt(HEAD)
-
-    def one_block(running, pieces):
-        grad_keys, grad_values = running
-        query_block, start_block, offset, log_block, grad_block = pieces
-        scores = block_scores(query_block, rotated_keys, start_block, sequence_start, offset)
-        softmax_full = jnp.exp(scores - log_block)
-        grad_softmax = jnp.einsum(
-            "qkgd,tkd->kgqt", grad_block, values, preferred_element_type=jnp.float32
-        )
-        inner_sum = jnp.sum(softmax_full * grad_softmax, axis=-1, keepdims=True)
-        grad_scores = (softmax_full * (grad_softmax - inner_sum)).astype(jnp.bfloat16)
-        grad_query = (
-            jnp.einsum(
-                "kgqt,tkd->qkgd", grad_scores, rotated_keys, preferred_element_type=jnp.float32
-            )
-            * score_scale
-        )
-        grad_keys = (
-            grad_keys
-            + jnp.einsum(
-                "kgqt,qkgd->tkd", grad_scores, query_block, preferred_element_type=jnp.float32
-            )
-            * score_scale
-        )
-        grad_values = grad_values + jnp.einsum(
-            "kgqt,qkgd->tkd",
-            softmax_full.astype(jnp.bfloat16),
-            grad_block,
-            preferred_element_type=jnp.float32,
-        )
-        return ((grad_keys, grad_values), grad_query)
-
-    shaped = queries.reshape((block_count, BLOCK) + queries.shape[1:])
-    grad_shaped = grad_heads.reshape((block_count, BLOCK) + queries.shape[1:])
-    offsets = jnp.arange(block_count, dtype=jnp.int32) * BLOCK
-    key_zeros = jnp.zeros(rotated_keys.shape, jnp.float32)
-    finals, grad_queries = lax.scan(
-        one_block,
-        (key_zeros, key_zeros),
-        (shaped, sequence_start.reshape(block_count, BLOCK), offsets, log_total, grad_shaped),
-    )
-    return (grad_queries.reshape(queries.shape), finals[0], finals[1])
+    cosine, sine = (jnp.cos(angles), jnp.sin(angles))
+    zero = jnp.zeros_like(sine)
+    return jnp.stack(
+        [
+            jnp.concatenate([cosine] * 4, axis=1),
+            jnp.concatenate([-sine, zero] * 2, axis=1),
+            jnp.concatenate([zero, sine] * 2, axis=1),
+        ]
+    )
 
 
 def newton_parts(grams):
@@ -270,9 +313,8 @@
             )
 
 
-def dense_update(grads, gathered, own_moments, layout, shard_index):
-    _, count, block_rows, width = gathered.shape
-    moments = pl.BlockSpec((3, count, block_rows, width), lambda i: (1, 0, 0, 0))
+def dense_update(grads, moments, own_moments, layout, shard_index):
+    _, count, block_rows, width = moments.shape
     whole = lambda shape: pl.BlockSpec(shape, lambda i: (0,) * len(shape))
     shapes = []
     for _, size in layout:
@@ -280,7 +322,7 @@
     return pl.pallas_call(
         functools.partial(dense_update_kernel, layout),
         grid=(1,),
-        in_specs=[pl.BlockSpec(memory_space=pltpu.SMEM), whole(grads.shape), moments]
+        in_specs=[pl.BlockSpec(memory_space=pltpu.SMEM), whole(grads.shape), whole(moments.shape)]
         + [whole(moment.shape) for moment in own_moments],
         out_specs=[whole(shape.shape) for shape in shapes],
         out_shape=shapes,
@@ -293,7 +335,7 @@
         cost_estimate=pl.CostEstimate(
             flops=28000000000, bytes_accessed=24 * width * width, transcendentals=0
         ),
-    )(shard_index.reshape(1).astype(jnp.int32), grads, gathered, *own_moments)
+    )(shard_index.reshape(1).astype(jnp.int32), grads, moments, *own_moments)
 
 
 LAYOUT = ((0, 1024), (1024, 512), (1536, 512), (2048, 1024))
@@ -338,6 +380,7 @@
     count,
     bits,
     own_ref,
+    middle_ref,
     cot_ref,
     weight_ref,
     gate_hbm,
@@ -595,7 +638,7 @@
             device_id_type=MESH,
         ).wait_recv()
         total = total + got_out[source].astype(jnp.float32)
-    out_ref[...] = total
+    out_ref[...] = (middle_ref[...] + total).astype(out_ref.dtype)
 
     for k in range(1, count):
         block = lax.rem(me + k, count)
@@ -616,7 +659,7 @@
             hand_on(block, False).wait_send()
 
 
-def moe(normed, cotangents, weights, gate_proj, up_proj, down_proj, bits, count):
+def moe(normed, middle, cotangents, weights, gate_proj, up_proj, down_proj, bits, count):
     tokens, width = normed.shape
     experts, _, hidden = gate_proj.shape
     half = width // 2
@@ -632,10 +675,10 @@
     dma = pltpu.SemaphoreType.DMA
     return pl.pallas_call(
         functools.partial(moe_kernel, count, bits),
-        in_specs=[vmem, vmem, vmem, anywhere, anywhere, anywhere],
+        in_specs=[vmem, vmem, vmem, vmem, anywhere, anywhere, anywhere],
         out_specs=[vmem, vmem, vmem],
         out_shape=[
-            jax.ShapeDtypeStruct((tokens, width), jnp.float32),
+            jax.ShapeDtypeStruct((tokens, width), low),
             jax.ShapeDtypeStruct((tokens, width), jnp.float32),
             jax.ShapeDtypeStruct((experts, 3, 2, final, hidden), low),
         ],
@@ -671,7 +714,7 @@
         cost_estimate=pl.CostEstimate(
             flops=39000000000, bytes_accessed=20000000, transcendentals=2000000
         ),
-    )(normed, cotangents, weights, gate_proj, up_proj, down_proj)
+    )(normed, middle, cotangents, weights, gate_proj, up_proj, down_proj)
 
 
 def rep_bits(rep_count):
@@ -688,13 +731,26 @@
     bits,
     share_ref,
     normed_ref,
-    delta_ref,
     head_ref,
-    branch_ref,
-    gains_ref,
+    weights_ref,
+    small_ref,
+    tokens_ref,
+    cot_ref,
+    second_ref,
+    middle_ref,
+    query_ref,
+    pair_ref,
+    total_ref,
+    table_ref,
+    column_ref,
+    row_ref,
     experts_out,
     dense_out,
     gains_out,
+    tokens_out,
+    delta_ref,
+    branch_ref,
+    heads_ref,
     dense_ref,
     total,
     land_core,
@@ -813,10 +869,24 @@
             across(gain_bits[stage]),
         )
 
-    gains_send[0] = gains_ref[...]
-    gain_copy(0).start()
     for stream in streams:
         expert_copy(0, stream).start()
+
+    def whole(index):
+        return weights_ref[index].reshape(count * rows, -1)
+
+    def gain(index):
+        at = EXPERTS + index
+        return jnp.concatenate([small_ref[z, at : at + 1, :rows] for z in range(count)], axis=1)
+
+    scaled, inverse = normalize(middle_ref[...])
+    middle_extra, midnorm_part = normalize_back(second_ref[...], gain(1), scaled, inverse)
+    grad_middle = cot_ref[...].astype(jnp.float32) + middle_extra
+    tokens_out[...] = grad_middle
+    branch_ref[...] = grad_middle.astype(jnp.bfloat16)
+    heads_ref[...] = dot_nt(branch_ref[...], whole(2)).astype(jnp.bfloat16)
+    bias = allowed_pairs(column_ref[...], row_ref[...])
+    attend_backward(query_ref, pair_ref, bias, total_ref, heads_ref, table_ref, delta_ref)
 
     part = dense_ref.shape[3] // 3
     normed_turned = normed_ref[...].T
@@ -873,6 +943,16 @@
         first_copy(stream).start()
     for stream in streams:
         add_core(held[stream])
+    grad_first = dot_nt(delta_ref[:, : NHEADS * HEAD], whole(0)) + dot_nt(
+        delta_ref[:, NHEADS * HEAD :], whole(1)
+    )
+    scaled, inverse = normalize(tokens_ref[...].astype(jnp.float32))
+    input_extra, prenorm_part = normalize_back(grad_first, gain(0), scaled, inverse)
+    tokens_out[...] = tokens_out[...] + input_extra
+    gains_send[0] = jnp.concatenate(
+        [prenorm_part, midnorm_part, jnp.zeros((6, prenorm_part.shape[1]), jnp.float32)], axis=0
+    )
+    gain_copy(0).start()
     gain_step(0)
 
     starts = []
@@ -1077,11 +1157,16 @@
         gain_line(k).wait_send()
 
 
-def spread(share, normed, deltas, head_low, branch, gains, bits, count):
+def spread(
+    share, normed, head_low, weights, small, tokens, cotangent, second, middle, *rest, bits, count
+):
+    query, pair, log_total, tables, starts = rest
     experts, _, _, final, hidden = share.shape
-    rows = normed.shape[1] // count
-    width = 3 * normed.shape[1] // 8
+    token_count, features = normed.shape
+    rows = features // count
+    width = 3 * features // 8
     dense_shape = (8, count, rows, width)
+    gains_shape = (8, features)
     steps = len(bits)
     last = rows >> (steps - 1)
     low = jnp.bfloat16
@@ -1089,14 +1174,18 @@
     dma = pltpu.SemaphoreType.DMA
     return pl.pallas_call(
         functools.partial(spread_kernel, count, bits),
-        in_specs=[vmem] * 6,
-        out_specs=[vmem, vmem, vmem],
+        in_specs=[vmem] * 15,
+        out_specs=[vmem] * 4,
         out_shape=[
             jax.ShapeDtypeStruct((experts, 3, 4 * (final << steps), hidden), low),
             jax.ShapeDtypeStruct(dense_shape, low),
-            jax.ShapeDtypeStruct(gains.shape, jnp.float32),
+            jax.ShapeDtypeStruct(gains_shape, jnp.float32),
+            jax.ShapeDtypeStruct((token_count, features), jnp.float32),
         ],
         scratch_shapes=[
+            pltpu.VMEM((token_count, 2 * features), low),
+            pltpu.VMEM((token_count, features), low),
+            pltpu.VMEM((token_count, features), low),
             pltpu.VMEM(dense_shape, low),
             pltpu.VMEM((4, count, rows, width), low),
             pltpu.VMEM((4, count, rows, width), low),
@@ -1107,9 +1196,9 @@
             pltpu.VMEM((count, 2, last, width), low),
             pltpu.VMEM((count, 2, last, width), low),
             pltpu.VMEM((2, last, width), low),
-            pltpu.VMEM((steps + 2,) + gains.shape, jnp.float32),
-            pltpu.VMEM((steps + 1,) + gains.shape, jnp.float32),
-            pltpu.VMEM((count,) + gains.shape, jnp.float32),
+            pltpu.VMEM((steps + 2,) + gains_shape, jnp.float32),
+            pltpu.VMEM((steps + 1,) + gains_shape, jnp.float32),
+            pltpu.VMEM((count,) + gains_shape, jnp.float32),
             dma((4,)),
             dma((4,)),
             dma((4,)),
@@ -1131,19 +1220,50 @@
             dma((count,)),
         ],
         compiler_params=pltpu.CompilerParams(
-            collective_id=2, has_side_effects=True, vmem_limit_bytes=60 * 1024 * 1024
+            collective_id=2, has_side_effects=True, vmem_limit_bytes=63 * 1024 * 1024
         ),
         name="spread",
-    )(share, normed, deltas, head_low, branch, gains)
+    )(
+        share,
+        normed,
+        head_low,
+        weights,
+        small,
+        tokens,
+        cotangent,
+        second,
+        middle,
+        query,
+        pair,
+        log_total,
+        tables,
+        starts[:, None],
+        starts[None, :],
+    )
 
 
 def gather_kernel(
     count,
     bits,
-    own_ref,
+    weights_ref,
+    moments_ref,
     small_ref,
-    full_out,
+    tokens_ref,
+    cot_ref,
+    table_ref,
+    column_ref,
+    row_ref,
+    weights_out,
+    moments_out,
     small_out,
+    cot_out,
+    middle_out,
+    first_out,
+    second_out,
+    query_out,
+    pair_out,
+    head_out,
+    total_out,
     local_sem,
     line_send,
     line_recv,
@@ -1153,17 +1273,21 @@
     join_recv,
     small_send,
     small_recv,
+    right_sem,
+    left_sem,
+    arrive_sem,
 ):
     rep = lax.axis_index("rep")
     me = lax.axis_index("shard")
     core = rep % 2
     steps = len(bits)
     streams = range(2)
-    rows = own_ref.shape[1]
-    half = own_ref.shape[2] // 2
+    owns = (weights_ref, moments_ref)
+    fulls = (weights_out, moments_out)
+    rows, width = weights_ref.shape[1:]
+    half = width // 2
     fine = half // 4
     groups = 2
-    depth = own_ref.shape[0] // groups
     others = [lax.rem(me + k, count) for k in range(1, count)]
 
     def columns_of(start, size):
@@ -1175,10 +1299,14 @@
     def side(bit):
         return (rep // bit) % 2
 
-    own_copy = pltpu.make_async_copy(own_ref, full_out.at[:, me], local_sem.at[0])
-    own_copy.start()
-    own_small = pltpu.make_async_copy(small_ref, small_out.at[me], local_sem.at[1])
-    own_small.start()
+    own_copies = [
+        pltpu.make_async_copy(weights_ref, weights_out.at[:, me], local_sem.at[0]),
+        pltpu.make_async_copy(moments_ref, moments_out.at[:, me], local_sem.at[1]),
+    ]
+    for own_copy in own_copies:
+        own_copy.start()
+    small_out[me] = small_ref[...]
+    cot_out[me] = cot_ref[...]
     peers = [(rep, other) for other in others]
     peers += [(flip(rep, bit), me) for bit in (1,) + bits]
     greet(peers)
@@ -1205,14 +1333,11 @@
             device_id_type=MESH,
         )
 
-    def slab(group):
-        return pl.ds(group * depth, depth)
-
     def line_copy(group, stream, source, peer):
         place, columns = regions[stream][0][-1]
         return remote(
-            own_ref.at[slab(group), place, columns],
-            full_out.at[slab(group), source, place, columns],
+            owns[group].at[:, place, columns],
+            fulls[group].at[:, source, place, columns],
             line_send.at[group, stream, peer],
             line_recv.at[group, stream, source],
             (rep, peer),
@@ -1220,7 +1345,7 @@
 
     def grow_copy(step, group, stream, source):
         place, columns = regions[stream][0][step]
-        part = full_out.at[slab(group), source, place, columns]
+        part = fulls[group].at[:, source, place, columns]
         return remote(
             part,
             part,
@@ -1230,7 +1355,7 @@
         )
 
     def join_copy(group, stream, source):
-        part = full_out.at[slab(group), source, :, regions[stream][1]]
+        part = fulls[group].at[:, source, :, regions[stream][1]]
         return remote(
             part,
             part,
@@ -1248,9 +1373,46 @@
             (rep, peer),
         )
 
-    for other in others:
-        small_copy(me, other).start()
-    for group in range(groups):
+    def hand_on(block, to_right):
+        peer = jnp.minimum(me + 1, count - 1) if to_right else jnp.maximum(me - 1, 0)
+        return remote(
+            cot_out.at[block],
+            cot_out.at[block],
+            (right_sem if to_right else left_sem).at[block],
+            arrive_sem.at[block],
+            (rep, peer),
+        )
+
+    def line_start():
+        @pl.when(me < count - 1)
+        def _():
+            hand_on(me, True).start()
+
+        @pl.when(me > 0)
+        def _():
+            hand_on(me, False).start()
+
+    def line_step(step):
+        lower = me - step
+        upper = me + step
+
+        @pl.when(lower >= 0)
+        def _():
+            hand_on(jnp.maximum(lower, 0), True).wait_recv()
+
+            @pl.when(me < count - 1)
+            def _():
+                hand_on(jnp.maximum(lower, 0), True).start()
+
+        @pl.when(upper < count)
+        def _():
+            hand_on(jnp.minimum(upper, count - 1), False).wait_recv()
+
+            @pl.when(me > 0)
+            def _():
+                hand_on(jnp.minimum(upper, count - 1), False).start()
+
+    def line_send_group(group):
         for other in others:
             for stream in streams:
                 line_copy(group, stream, me, other).start()
@@ -1267,37 +1429,98 @@
                 else:
                     join_copy(group, stream, other).start()
 
-    for level in range(steps + 2):
-        if level <= steps:
-            advance(level, 0)
-        if level > 0:
-            advance(level - 1, 1)
+    for other in others:
+        small_copy(me, other).start()
+    line_send_group(0)
+    for other in others:
+        small_copy(other, other).wait_recv()
+
+    def gain(index):
+        at = EXPERTS + index
+        return jnp.concatenate([small_out[z, at : at + 1, :rows] for z in range(count)], axis=1)
+
+    inputs = tokens_ref[...].astype(jnp.float32)
+    first_out[...] = (normalize(inputs)[0] * gain(0)).astype(jnp.bfloat16)
+    advance(0, 0)
+    line_start()
+    line_send_group(1)
+    for level in range(1, steps + 1):
+        advance(level, 0)
+        if level == 1:
+            line_step(1)
+    for other in others:
+        for stream in streams:
+            join_copy(0, stream, other).wait_recv()
+    own_copies[0].wait()
+
+    def whole(index):
+        return weights_out[index].reshape(count * rows, width)
+
+    project_inputs(first_out[...], whole, query_out, pair_out, table_ref)
+    advance(0, 1)
+    if count > 2:
+        line_step(2)
+    bias = allowed_pairs(column_ref[...], row_ref[...])
+    quarter = KVHEADS // 4
+    attend_forward(range(quarter), query_out, pair_out, bias, head_out, total_out)
+    advance(1, 1)
+    for step in range(3, count):
+        line_step(step)
+    attend_forward(range(quarter, KVHEADS), query_out, pair_out, bias, head_out, total_out)
+    for level in range(2, steps + 1):
+        advance(level, 1)
+    middle = inputs + dot_nn(head_out[...], whole(2))
+    middle_out[...] = middle
+    second_out[...] = (normalize(middle)[0] * gain(1)).astype(jnp.bfloat16)
     for group in range(groups):
         for other in others:
             for stream in streams:
-                join_copy(group, stream, other).wait()
+                join_copy(group, stream, other).wait_send()
+                if group == 1:
+                    join_copy(group, stream, other).wait_recv()
                 line_copy(group, stream, me, other).wait_send()
                 for step in range(steps):
                     grow_copy(step, group, stream, other).wait_send()
     for other in others:
-        small_copy(other, other).wait_recv()
         small_copy(me, other).wait_send()
-    own_copy.wait()
-    own_small.wait()
-
-
-def gather(own, small, bits, count):
-    depth, rows, columns = own.shape
+    for block in range(count):
+
+        @pl.when((block <= me) & (me < count - 1))
+        def _():
+            hand_on(block, True).wait_send()
+
+        @pl.when((block >= me) & (me > 0))
+        def _():
+            hand_on(block, False).wait_send()
+
+    own_copies[1].wait()
+
+
+def gather(weights, moments, small, tokens, cotangent, tables, starts, bits, count):
+    depth, rows, width = weights.shape
+    token_count = tokens.shape[0]
     steps = len(bits)
+    low = jnp.bfloat16
     vmem = pl.BlockSpec(memory_space=pltpu.VMEM)
     dma = pltpu.SemaphoreType.DMA
+    whole = jax.ShapeDtypeStruct((depth, count, rows, width), low)
+    features = jax.ShapeDtypeStruct((token_count, width), low)
     return pl.pallas_call(
         functools.partial(gather_kernel, count, bits),
-        in_specs=[vmem, vmem],
-        out_specs=[vmem, vmem],
+        in_specs=[vmem] * 8,
+        out_specs=[vmem] * 11,
         out_shape=[
-            jax.ShapeDtypeStruct((depth, count, rows, columns), own.dtype),
+            whole,
+            whole,
             jax.ShapeDtypeStruct((count,) + small.shape, small.dtype),
+            jax.ShapeDtypeStruct((count, token_count, width), low),
+            jax.ShapeDtypeStruct((token_count, width), jnp.float32),
+            features,
+            features,
+            features,
+            features,
+            features,
+            jax.ShapeDtypeStruct((2 * token_count, KVHEADS), jnp.float32),
         ],
         scratch_shapes=[
             dma((2,)),
@@ -1309,12 +1532,15 @@
             dma((2, 2, count)),
             dma((count,)),
             dma((count,)),
+            dma((count,)),
+            dma((count,)),
+            dma((count,)),
         ],
         compiler_params=pltpu.CompilerParams(
-            collective_id=3, has_side_effects=True, vmem_limit_bytes=32 * 1024 * 1024
+            collective_id=3, has_side_effects=True, vmem_limit_bytes=56 * 1024 * 1024
         ),
         name="gather",
-    )(own, small)
+    )(weights, moments, small, tokens, cotangent, tables, starts[:, None], starts[None, :])
 
 
 def local(
@@ -1345,15 +1571,15 @@
     shard_index = lax.axis_index("shard")
     rep_count = lax.axis_size("rep")
     shard_count = lax.axis_size("shard")
-    row_block, width = query_proj.shape
+    row_block = query_proj.shape[0]
     bits = rep_bits(rep_count)
     experts_here = gate_proj.shape[0]
     low = jnp.bfloat16
-    own_rows = jnp.stack(
+    own_weights = jnp.stack(
+        [query_proj, jnp.concatenate([key_proj, value_proj], axis=1), out_proj]
+    )
+    own_moments = jnp.stack(
         [
-            query_proj,
-            jnp.concatenate([key_proj, value_proj], axis=1),
-            out_proj,
             query_moment.astype(low),
             jnp.concatenate([key_moment.astype(low), value_moment.astype(low)], axis=1),
             out_moment.astype(low),
@@ -1371,54 +1597,36 @@
         jnp.stack([prenorm, midnorm]).astype(jnp.float32),
         ((0, 6), (0, tokens.shape[0] - row_block)),
     )
-    cotangent_all = lax.all_gather(cotangent, "shard", axis=0)
-    gathered, small = gather(
-        own_rows, jnp.concatenate([dense_weights, gain_rows], axis=0), bits, shard_count
-    )
-    full_query = gathered[0].reshape(width, width)
-    full_pair = gathered[1].reshape(width, width)
-    full_out = gathered[2].reshape(width, width)
-    full_key = full_pair[:, : width // 2]
-    full_value = full_pair[:, width // 2 :]
-    gain_before = small[:, EXPERTS, :row_block].reshape(width)
-    gain_after = small[:, EXPERTS + 1, :row_block].reshape(width)
+    tables = rotary_tables(jnp.arange(tokens.shape[0], dtype=jnp.int32) - sequence_start)
+    (
+        weights,
+        moments,
+        small,
+        cotangent_all,
+        middle,
+        normed_first,
+        normed_second,
+        query,
+        pair,
+        head_low,
+        log_total,
+    ) = gather(
+        own_weights,
+        own_moments,
+        jnp.concatenate([dense_weights, gain_rows], axis=0),
+        tokens,
+        cotangent,
+        tables,
+        sequence_start,
+        bits,
+        shard_count,
+    )
     expert_weights = lax.dynamic_slice_in_dim(
         small, shard_index * experts_here, experts_here, 1
     ).transpose(0, 2, 1)
-    group_size = NHEADS // KVHEADS
-    token_count = tokens.shape[0]
-    inputs = tokens.astype(jnp.float32)
-    scaled_first, inverse_first = root_scale(inputs)
-    normed_first = (scaled_first * gain_before).astype(jnp.bfloat16)
-    query_linear = jnp.dot(normed_first, full_query, preferred_element_type=jnp.float32).reshape(
-        token_count, NHEADS, HEAD
-    )
-    key_linear = jnp.dot(normed_first, full_key, preferred_element_type=jnp.float32).reshape(
-        token_count, KVHEADS, HEAD
-    )
-    values = (
-        jnp.dot(normed_first, full_value, preferred_element_type=jnp.float32)
-        .astype(jnp.bfloat16)
-        .reshape(token_count, KVHEADS, HEAD)
-    )
-    cosine_table, sine_table = rotary_tables(
-        jnp.arange(token_count, dtype=jnp.int32) - sequence_start
-    )
-    queries = (
-        (query_linear * cosine_table + rotate_half(query_linear) * sine_table)
-        .astype(jnp.bfloat16)
-        .reshape(token_count, KVHEADS, group_size, HEAD)
-    )
-    rotated_keys = (key_linear * cosine_table + rotate_half(key_linear) * sine_table).astype(
-        jnp.bfloat16
-    )
-    head_out, log_total = attend_forward(queries, rotated_keys, values, sequence_start)
-    head_low = head_out.astype(jnp.bfloat16)
-    middle = inputs + jnp.dot(head_low, full_out, preferred_element_type=jnp.float32)
-    scaled_second, inverse_second = root_scale(middle)
-    normed_second = (scaled_second * gain_after).astype(jnp.bfloat16)
-    returned, grad_second, expert_share = moe(
+    mixed, grad_second, expert_share = moe(
         normed_second,
+        middle,
         cotangent_all,
         expert_weights,
         gate_proj,
@@ -1427,51 +1635,23 @@
         bits,
         shard_count,
     )
-    mixed = middle + returned
-    grad_mixed = cotangent.astype(jnp.float32)
-    middle_extra, midnorm_part = root_back(grad_second, gain_after, scaled_second, inverse_second)
-    grad_middle = grad_mixed + middle_extra
-    grad_branch = grad_middle.astype(jnp.bfloat16)
-    grad_heads = (
-        jnp.einsum("td,qd->tq", grad_branch, full_out, preferred_element_type=jnp.float32)
-        .astype(jnp.bfloat16)
-        .reshape(queries.shape)
-    )
-    grad_queries, grad_keys, grad_values = attend_backward(
-        queries, rotated_keys, values, sequence_start, log_total, grad_heads
-    )
-    grad_queries = grad_queries.reshape(token_count, NHEADS, HEAD)
-    query_delta = (
-        (grad_queries * cosine_table + rotate_back(grad_queries * sine_table))
-        .astype(jnp.bfloat16)
-        .reshape(token_count, -1)
-    )
-    key_delta = (
-        (grad_keys * cosine_table + rotate_back(grad_keys * sine_table))
-        .astype(jnp.bfloat16)
-        .reshape(token_count, -1)
-    )
-    value_delta = grad_values.astype(jnp.bfloat16).reshape(token_count, -1)
-    grad_first = (
-        jnp.einsum("tq,dq->td", query_delta, full_query, preferred_element_type=jnp.float32)
-        + jnp.einsum("tq,dq->td", key_delta, full_key, preferred_element_type=jnp.float32)
-        + jnp.einsum("tq,dq->td", value_delta, full_value, preferred_element_type=jnp.float32)
-    )
-    input_extra, prenorm_part = root_back(grad_first, gain_before, scaled_first, inverse_first)
-    grad_tokens = grad_middle + input_extra
-    deltas = jnp.concatenate([query_delta, key_delta, value_delta], axis=1)
-    gains_local = jnp.concatenate(
-        [jnp.stack([prenorm_part, midnorm_part]), jnp.zeros((6, prenorm_part.shape[0]))], axis=0
-    )
-    expert_grads, dense_grads, gains_grad = spread(
+    expert_grads, dense_grads, gains_grad, grad_tokens = spread(
         expert_share,
         normed_first,
-        deltas,
         head_low,
-        grad_branch,
-        gains_local,
-        bits,
-        shard_count,
+        weights,
+        small,
+        tokens,
+        cotangent,
+        grad_second,
+        middle,
+        query,
+        pair,
+        log_total,
+        tables,
+        sequence_start,
+        bits=bits,
+        count=shard_count,
     )
     gains_here = lax.dynamic_slice_in_dim(gains_grad, shard_index * row_block, row_block, 1)
     prenorm_grad = gains_here[0]
@@ -1495,7 +1675,7 @@
         out_update,
     ) = dense_update(
         dense_grads,
-        gathered,
+        moments,
         (query_moment, key_moment, value_moment, out_moment),
         LAYOUT,
         shard_index,
@@ -1505,7 +1685,7 @@
     )
     down_grad, down_next, down_update = expert_update(expert_grads, (2,), (down_moment,))
     return (
-        mixed.astype(jnp.bfloat16),
+        mixed,
         grad_tokens,
         query_grad,
         query_next,

time: 561 us -> 478 us (0.85)
  local copies, waits for them, and re-layouts: 36 us -> 7.68 us
  matrix products: 21.9 us -> 0 us
  other arithmetic: 24.9 us -> 10.1 us
  between operations: 15.4 us -> 1.14 us
    dot_general x14 -> x0, matrix products: 21.9 us -> none  [the longest x1 3.11 us: one_block(): jnp.einsum('kgqt,qkgd->tkd', softmax_full.astype(jnp.bfloat16), grad_bloc...]
    pallas_call x1, Pallas kernels: 127 us -> 116 us  [moe(): pl.pallas_call(functools.partial(moe_kernel, count, bits), in_specs=[vmem...]
    convert_element_type x8 -> x0, other arithmetic: 9.3 us -> none  [the longest x1 4.36 us: one_block(): (softmax_full * (grad_softmax - inner_sum)).astype(jnp.bfloat16)]
    unnamed x114 -> x26, local copies, waits for them, and re-layouts: 9.37 us -> 1.82 us
    pallas_call x1, Pallas kernels: 86.4 us -> 93 us  [gather(): pl.pallas_call(functools.partial(gather_kernel, count, bits), in_specs=[v...]
    slice x2 -> x0, local copies, waits for them, and re-layouts: 5.72 us -> none  [the longest x1 5.13 us: local(): full_out = gathered[2].reshape(width, width)]
  transfers between devices with their start and end apart: 1 -> 0, of which waited for: 0 -> 0; matrix products, arithmetic and copies ran while one was open for 7% -> 0% of each run, Pallas kernels for 16% -> 0%
where the time goes in v1:
time: 478 us; the launch traced here: 470 us
  Pallas kernels  451 us (94%)
  other arithmetic  10.1 us (2%)
  local copies, waits for them, and re-layouts  7.68 us (2%)
    pallas_call x1, Pallas kernels, spread(): pl.pallas_call(functools.partial(spread_kernel, count, bits), in_specs=[v...  141 us
    pallas_call x1, Pallas kernels, moe(): pl.pallas_call(functools.partial(moe_kernel, count, bits), in_specs=[vmem...  116 us
    pallas_call x1, Pallas kernels, gather(): pl.pallas_call(functools.partial(gather_kernel, count, bits), in_specs=[v...  93 us
    pallas_call x2, Pallas kernels, expert_update(): pl.pallas_call(functools.partial(expert_update_kernel, kinds, scale), gri...  54.8 us
    pallas_call x1, Pallas kernels, dense_update(): pl.pallas_call(functools.partial(dense_update_kernel, layout), grid=(1,),...  46.7 us

profile of v1, /device:TPU:0, one launch (start us, length us, event | category | flops | bytes accessed | tf_op | source)
XLA Modules:
  0.0 469.8 jit_solution(16085564386066775059)
XLA Ops:
  0.7 0.0 copy-start.4
  0.7 0.0 copy-start.6
  0.7 0.0 copy-start.7
  0.7 0.0 copy-start.5
  0.7 0.8 stack.53
  1.5 0.7 stack.54
  2.2 0.7 subtract_convert_fusion
  2.8 0.8 select_reduce_fusion
  3.6 0.6 pad_maximum_fusion.3.small_ref
  4.2 1.5 copy.56.column_ref
  5.7 1.1 convert_element_type.19
  6.8 0.0 copy-start
  6.8 0.0 copy-start.1
  6.8 1.2 convert_element_type.20
  8.0 0.1 maximum_bitcast_fusion.1
  8.1 0.5 multiply_cosine_fusion
  8.7 0.4 maximum_bitcast_fusion.3
  9.0 0.8 pad_maximum_fusion.2.table_ref
  9.8 0.0 copy-done.6
  9.8 0.0 copy-done.7
  9.8 0.1 maximum_bitcast_fusion
  9.9 0.0 copy-done.4
  9.9 0.0 copy-done.5
  9.9 1.3 pad_maximum_fusion.weights_ref
  11.2 0.0 copy-done
  11.2 0.0 copy-done.1
  11.2 0.2 convert_bitcast_fusion
  11.4 1.3 pad_maximum_fusion.1.moments_ref
  12.7 93.0 %gather.1 = (bf16[3,4,256,1024]{3,2,1,0:T(8,128)(2,1)}, bf16[3,4,256,1024]{3,2,1,0:T(8,128)(2,1)}, f32[4,24,256]{2,1,0:T(8,128)}, bf16[4,256,1024]{2,1,0:T(8,128...) custom-call(bf16[3,256,1024]{2,1,0:T(8,128)(2,1)} %pad_maximum_fusio, ...), custom_call_target="tpu_custom_call" | custom-call | tf_op jit(solution)/shard_map/gather/pallas_call | solution.py:1508
  105.6 1.1 copy.57
  106.7 1.0 dynamic-slice_bitcast_fusion.weight_ref
  107.7 115.6 %moe.1 = (bf16[256,1024]{1,0:T(8,128)(2,1)}, f32[256,1024]{1,0:T(8,128)}, bf16[4,3,2,64,512]{4,3,2,1,0:T(8,128)(2,1)}) custom-call(bf16[256,1024]{1,0:T(8,128)(2,1)} %get-tuple-element.68.own_ref, f32[256,1024]{1,0:T(8,128)} %get-tuple-element.69.middle_ref, bf16[4,256,1024]{2,1,0:T(8,128)(2,1)} %get-tuple-element.70.cot_ref, ...), custom_call_target="tpu_custom_call" | custom-call | flops 38999998464 | bytes 20000000 | tf_op jit(solution)/shard_map/moe/pallas_call | solution.py:676
  223.3 0.0 copy-start.10
  223.3 0.0 copy-start.11
  223.3 140.9 %spread.1 = (bf16[4,3,1024,512]{3,2,1,0:T(8,128)(2,1)}, bf16[8,4,256,384]{3,2,1,0:T(8,128)(2,1)}, f32[8,1024]{1,0:T(8,128)}, f32[256,1024]{1,0:T(8,128)}) custom-call(bf16[4,3,2,64,512]{4,3,2,1,0:T(8,128)(2,1)} %get-tuple-element.73.share_ref, bf16[256,1024]{1,0:T(8,128)(2,1)} %get-tuple-element.74.normed_ref, bf16[256,1024]{1,0:T(8,128)(2,1)} %get-tuple-element.75.head_ref, ...), custom_call_target="tpu_custom_call" | custom-call | tf_op jit(solution)/shard_map/spread/pallas_call | solution.py:1175
  364.2 0.9 fusion.5
  365.1 0.0 copy-done.10
  365.1 0.6 broadcast_multiply_fusion.1
  365.7 0.0 copy-done.11
  365.7 0.6 broadcast_multiply_fusion
  366.2 46.7 %dense_update.1 = (f32[256,1024]{1,0:T(8,128)}, f32[256,1024]{1,0:T(8,128)}, f32[256,1024]{1,0:T(8,128)}, f32[256,512]{1,0:T(8,128)}, f32[256,512]{1,0:T(8,128)}...) custom-call(s32[1]{0:T(128)} %bitcast.14.place_ref, ...), custom_call_target="tpu_custom_call" | custom-call | flops 28000000000 | bytes 25165824 | tf_op jit(solution)/shard_map/dense_update/pallas_call | solution.py:322
  412.9 0.0 copy-done.8
  412.9 0.0 copy-done.9
  413.0 19.0 %expert_update.3 = (f32[4,512,1024]{2,1,0:T(8,128)}, f32[4,512,1024]{2,1,0:T(8,128)}, f32[4,512,1024]{2,1,0:T(8,128)}) custom-call(bf16[4,3,1024,512]{3,2,1,0:T(8,128)(2,1)} %get-tuple-element.97.refs_0_, f32[4,512,1024]{2,1,0:T(8,128)} %refs_1_.5), custom_call_target="tpu_custom_call" | custom-call | flops 10000000000 | bytes 37748736 | tf_op jit(solution)/shard_map/expert_update/pallas_call | solution.py:248
  431.9 35.9 %expert_update.2 = (f32[4,1024,512]{2,1,0:T(8,128)}, f32[4,1024,512]{2,1,0:T(8,128)}, f32[4,1024,512]{2,1,0:T(8,128)}, f32[4,1024,512]{2,1,0:T(8,128)}, f32[4,10...) custom-call(bf16[4,3,1024,512]{3,2,1,0:T(8,128)(2,1)} %get-tuple-element.97.refs_0_, f32[4,1024,512]{2,1,0:T(8,128)} %refs_1_.4, ...), custom_call_target="tpu_custom_call" | custom-call | flops 20000000000 | bytes 75497472 | tf_op jit(solution)/shard_map/expert_update/pallas_call | solution.py:248
  467.8 0.0 copy-done.3
  467.8 0.8 copy.61
  468.6 1.0 copy.62
  (8 shorter events, 0.0 us)
Async XLA Ops:
  0.7 9.2 %copy-start.4 = (bf16[256,1024]{1,0:T(8,128)(2,1)S(1)}, bf16[256,1024]{1,0:T(8,128)(2,1)}, u32[]{:S(2)}) copy-start(bf16[256,1024]{1,0:T(8,128)(2,1)} %param.31) | copy-start | bytes 1572868
  0.7 9.1 %copy-start.6 = (bf16[256,512]{1,0:T(8,128)(2,1)S(1)}, bf16[256,512]{1,0:T(8,128)(2,1)}, u32[]{:S(2)}) copy-start(bf16[256,512]{1,0:T(8,128)(2,1)} %param.30) | copy-start | bytes 786436
  0.7 9.1 %copy-start.7 = (bf16[256,512]{1,0:T(8,128)(2,1)S(1)}, bf16[256,512]{1,0:T(8,128)(2,1)}, u32[]{:S(2)}) copy-start(bf16[256,512]{1,0:T(8,128)(2,1)} %param.29) | copy-start | bytes 786436
  0.7 9.2 %copy-start.5 = (bf16[256,1024]{1,0:T(8,128)(2,1)S(1)}, bf16[256,1024]{1,0:T(8,128)(2,1)}, u32[]{:S(2)}) copy-start(bf16[256,1024]{1,0:T(8,128)(2,1)} %param.28) | copy-start | bytes 1572868
  6.8 4.4 copy-start
  6.8 4.4 copy-start.1
  223.3 141.8 %copy-start.10 = (f32[256]{0:T(256)S(1)}, f32[256]{0:T(256)}, u32[]{:S(2)}) copy-start(f32[256]{0:T(256)} %param.41) | copy-start | bytes 3076
  223.3 142.3 %copy-start.11 = (f32[256]{0:T(256)S(1)}, f32[256]{0:T(256)}, u32[]{:S(2)}) copy-start(f32[256]{0:T(256)} %param.42) | copy-start | bytes 3076
  365.1 47.9 %copy-start.8 = (f32[1,256]{1,0:T(1,128)}, f32[1,256]{1,0:T(1,128)S(1)}, u32[]{:S(2)}) copy-start(f32[1,256]{1,0:T(1,128)S(1)} %get-tuple-element.113) | copy-start | bytes 3076
  365.1 47.9 %copy-start.9 = (f32[1,256]{1,0:T(1,128)}, f32[1,256]{1,0:T(1,128)S(1)}, u32[]{:S(2)}) copy-start(f32[1,256]{1,0:T(1,128)S(1)} %get-tuple-element.114) | copy-start | bytes 3076
  431.9 35.9 %copy-start.3 = (bf16[256,1024]{1,0:T(8,128)(2,1)S(1)}, bf16[256,1024]{1,0:T(8,128)(2,1)}, u32[]{:S(2)}) copy-start(bf16[256,1024]{1,0:T(8,128)(2,1)} %get-tuple-element.150) | copy-start | bytes 1572868
  431.9 36.7 %copy-start.2 = (f32[256,1024]{1,0:T(8,128)S(1)}, f32[256,1024]{1,0:T(8,128)}, u32[]{:S(2)}) copy-start(f32[256,1024]{1,0:T(8,128)} %get-tuple-element.151) | copy-start | bytes 3145732

commit v2 on v1

--- a/solution.py
+++ b/solution.py
@@ -201,35 +201,42 @@
     return list(zip(firsts, first_lows, seconds, second_lows))
 
 
+def scaled_gram(gram):
+    shape = gram.shape
+    rows = lax.broadcasted_iota(jnp.int32, shape, 0)
+    diagonal = rows == lax.broadcasted_iota(jnp.int32, shape, 1)
+    inverse = 1.0 / (jnp.sqrt(jnp.sum(jnp.where(diagonal, gram, 0.0))) + 1e-07)
+    return (gram * (inverse * inverse), inverse)
+
+
 def expert_update_kernel(kinds, scale, *refs):
     a = newton_first
     grads_ref = refs[0]
     moments = refs[1 : 1 + len(kinds)]
     outs = refs[1 + len(kinds) :]
     half = grads_ref.shape[3]
+    tall = kinds[0] < 2
     states = []
     for index in range(len(kinds)):
         for e in range(grads_ref.shape[0]):
             grad = grads_ref[e, index].astype(jnp.float32)
-            tall = kinds[index] < 2
             if not tall:
                 grad = jnp.concatenate([grad[:half], grad[half:]], axis=1)
             moment = momentum_keep * moments[index][e] + grad
             outs[3 * index][e] = grad
             outs[3 * index + 1][e] = moment
-            inverse = 1.0 / (jnp.sqrt(jnp.sum(moment * moment)) + 1e-07)
-            low = (moment * inverse).astype(jnp.bfloat16)
+            low = moment.astype(jnp.bfloat16)
             sides = (((0,), (0,)), ((), ())) if tall else (((1,), (1,)), ((), ()))
-            gram = lax.dot_general(low, low, sides, preferred_element_type=jnp.float32)
-            states.append((index, e, tall, inverse, low, gram))
+            gram, inverse = scaled_gram(
+                lax.dot_general(low, low, sides, preferred_element_type=jnp.float32)
+            )
+            states.append((index, e, inverse, low, gram))
     parts = newton_parts([state[-1] for state in states])
-    for (index, e, tall, inverse, low, _), (first, first_low, second, second_low) in zip(
-        states, parts
-    ):
+    for (index, e, inverse, low, _), (first, first_low, second, second_low) in zip(states, parts):
         rest = a * (first + second) + jnp.dot(
             first_low, second_low, preferred_element_type=jnp.float32
         )
-        rest = (-scale * rest).astype(jnp.bfloat16)
+        rest = ((-scale * inverse) * rest).astype(jnp.bfloat16)
         if tall:
             step = jnp.dot(low, rest, preferred_element_type=jnp.float32)
         else:
@@ -265,60 +272,81 @@
     a = newton_first
     amount = len(layout)
     own_moments = refs[:amount]
-    outs = refs[amount : 4 * amount]
-    whole, own_grads = refs[4 * amount :]
+    outs = refs[amount : 3 * amount]
+    updates = refs[3 * amount : 3 * amount + 2]
+    matrices = refs[3 * amount + 2 : 3 * amount + 4]
+    own_grads = refs[3 * amount + 4]
     blocks, count, block_rows, width = grads_ref.shape
     part = width // 3
     me = place_ref[0]
+    core = place_ref[1]
     start = pl.multiple_of(me * block_rows, block_rows)
+
+    def momentum(moments, grads):
+        return (
+            (momentum_keep * moments.astype(jnp.float32) + grads.astype(jnp.float32))
+            .astype(jnp.bfloat16)
+            .reshape(count * block_rows, part)
+        )
+
     for block in range(blocks):
+        outer = slice(block * part, (block + 1) * part)
+        lanes = pl.ds(pl.multiple_of(2 * core * part, part), part)
+        matrices[0][:, outer] = momentum(
+            moments_ref[2 * core, :, :, outer], grads_ref[block, :, :, lanes]
+        )
         for index in range(3):
             columns = slice(8 * part * index + block * part, 8 * part * index + (block + 1) * part)
             inner = slice(index * part, (index + 1) * part)
-            outer = slice(block * part, (block + 1) * part)
-            grads = grads_ref[block, :, :, inner].reshape(count * block_rows, part)
-            moments = moments_ref[index, :, :, outer].reshape(count * block_rows, part)
-            whole[:, columns] = (
-                momentum_keep * moments.astype(jnp.float32) + grads.astype(jnp.float32)
-            ).astype(jnp.bfloat16)
             own_grads[:, columns] = grads_ref[block, me, :, inner].astype(jnp.float32)
-    for group in ((0, 1), (2, 3)):
-        states = []
-        for index in group:
-            begin, size = layout[index]
-            grad_out, next_out, _ = outs[3 * index : 3 * index + 3]
-            columns = slice(begin, begin + size)
-            grad = own_grads[:, columns]
-            grad_out[...] = grad
-            next_out[...] = momentum_keep * own_moments[index][...] + grad
-            matrix = whole[:, columns].astype(jnp.float32)
-            inverse = 1.0 / (jnp.sqrt(jnp.sum(matrix * matrix)) + 1e-07)
-            low = (matrix * inverse).astype(jnp.bfloat16)
-            gram = lax.dot_general(
-                low, low, (((0,), (0,)), ((), ())), preferred_element_type=jnp.float32
-            )
-            own = whole[pl.ds(start, block_rows), columns].astype(jnp.float32) * inverse
-            states.append((index, size, own, gram))
-        parts = newton_parts([state[-1] for state in states])
-        for (index, size, own, _), (_, first_low, _, second_low) in zip(states, parts):
-            scale = rate_matrix * math.sqrt(max(1.0, size / (count * block_rows)))
-            once = a * own + jnp.dot(
-                own.astype(jnp.bfloat16), first_low, preferred_element_type=jnp.float32
-            )
-            outs[3 * index + 2][...] = (-scale) * (
-                a * once
-                + jnp.dot(
-                    once.astype(jnp.bfloat16), second_low, preferred_element_type=jnp.float32
+    for block in range(blocks // 2):
+        outer = slice(block * part, (block + 1) * part)
+        lanes = pl.ds(pl.multiple_of((core * (blocks // 2) + block) * part, part), part)
+        matrices[1][:, outer] = momentum(
+            moments_ref[1, :, :, lanes],
+            grads_ref[core * (blocks // 2) + block, :, :, part : 2 * part],
+        )
+    for index, (begin, size) in enumerate(layout):
+        grad = own_grads[:, begin : begin + size]
+        outs[2 * index][...] = grad
+        outs[2 * index + 1][...] = momentum_keep * own_moments[index][...] + grad
+    states = []
+    for matrix in matrices:
+        low = matrix[...]
+        states.append(
+            scaled_gram(
+                lax.dot_general(
+                    low, low, (((0,), (0,)), ((), ())), preferred_element_type=jnp.float32
                 )
             )
-
-
-def dense_update(grads, moments, own_moments, layout, shard_index):
+        )
+    parts = newton_parts([state[0] for state in states])
+    for matrix, update, (_, inverse), (_, first_low, _, second_low) in zip(
+        matrices, updates, states, parts
+    ):
+        rows, columns = matrix.shape
+        scale = rate_matrix * math.sqrt(max(1.0, columns / rows))
+        own = matrix[pl.ds(start, block_rows)]
+        once = a * own.astype(jnp.float32) + jnp.dot(
+            own, first_low, preferred_element_type=jnp.float32
+        )
+        update[...] = (-scale * inverse) * (
+            a * once
+            + jnp.dot(once.astype(jnp.bfloat16), second_low, preferred_element_type=jnp.float32)
+        )
+
+
+def dense_update(grads, moments, own_moments, layout, shard_index, rep_index):
     _, count, block_rows, width = moments.shape
     whole = lambda shape: pl.BlockSpec(shape, lambda i: (0,) * len(shape))
     shapes = []
     for _, size in layout:
-        shapes += [jax.ShapeDtypeStruct((block_rows, size), jnp.float32)] * 3
+        shapes += [jax.ShapeDtypeStruct((block_rows, size), jnp.float32)] * 2
+    shapes += [
+        jax.ShapeDtypeStruct((block_rows, width), jnp.float32),
+        jax.ShapeDtypeStruct((block_rows, width // 2), jnp.float32),
+    ]
+    place = jnp.stack([shard_index, rep_index % 2]).astype(jnp.int32)
     return pl.pallas_call(
         functools.partial(dense_update_kernel, layout),
         grid=(1,),
@@ -327,15 +355,16 @@
         out_specs=[whole(shape.shape) for shape in shapes],
         out_shape=shapes,
         scratch_shapes=[
-            pltpu.VMEM((count * block_rows, 3 * width), jnp.bfloat16),
+            pltpu.VMEM((count * block_rows, width), jnp.bfloat16),
+            pltpu.VMEM((count * block_rows, width // 2), jnp.bfloat16),
             pltpu.VMEM((block_rows, 3 * width), jnp.float32),
         ],
         compiler_params=pltpu.CompilerParams(vmem_limit_bytes=63 * 1024 * 1024),
         name="dense_update",
         cost_estimate=pl.CostEstimate(
-            flops=28000000000, bytes_accessed=24 * width * width, transcendentals=0
+            flops=14000000000, bytes_accessed=24 * width * width, transcendentals=0
         ),
-    )(shard_index.reshape(1).astype(jnp.int32), grads, moments, *own_moments)
+    )(place, grads, moments, *own_moments)
 
 
 LAYOUT = ((0, 1024), (1024, 512), (1536, 512), (2048, 1024))
@@ -744,10 +773,11 @@
     table_ref,
     column_ref,
     row_ref,
-    experts_out,
+    experts_hbm,
     dense_out,
     gains_out,
     tokens_out,
+    experts_out,
     delta_ref,
     branch_ref,
     heads_ref,
@@ -986,12 +1016,6 @@
             later_copy(1, stream).start()
     gain_step(1)
 
-    for stream in streams:
-        own_copy(stream).wait()
-        expert_copy(0, stream).wait_recv()
-        if steps > 1:
-            expert_copy(1, stream).start()
-
     for step in range(1, steps):
         for stream in streams:
             later_copy(step, stream).wait_recv()
@@ -1006,6 +1030,12 @@
                 later_copy(step + 1, stream).start()
         gain_step(step + 1)
 
+    for stream in streams:
+        own_copy(stream).wait()
+        expert_copy(0, stream).wait_recv()
+        if steps > 1:
+            expert_copy(1, stream).start()
+
     last = starts[0][1]
     places = [rows_of(starts[stream][0], last) for stream in streams]
     for stream in streams:
@@ -1124,6 +1154,10 @@
         for k in range(1, count):
             line_arrival(lax.rem(me + k, count), stream).wait_recv()
         grow_copy(steps - 1, stream).start()
+    for stream in streams:
+        expert_copy(steps, stream).wait()
+    leave = pltpu.make_async_copy(experts_out, experts_hbm, local_sem.at[0])
+    leave.start()
     for step in reversed(range(steps)):
         for stream in streams:
             grow_copy(step, stream).wait_recv()
@@ -1138,7 +1172,6 @@
         join_copy(stream).start()
     for stream in streams:
         join_copy(stream).wait()
-        expert_copy(steps, stream).wait()
         for level in range(steps):
             expert_copy(level, stream).wait_send()
         first_copy(stream).wait_send()
@@ -1155,6 +1188,7 @@
     for k in range(1, count):
         shard_copy(k).wait_send()
         gain_line(k).wait_send()
+    leave.wait()
 
 
 def spread(
@@ -1175,7 +1209,7 @@
     return pl.pallas_call(
         functools.partial(spread_kernel, count, bits),
         in_specs=[vmem] * 15,
-        out_specs=[vmem] * 4,
+        out_specs=[pl.BlockSpec(memory_space=pl.ANY)] + [vmem] * 3,
         out_shape=[
             jax.ShapeDtypeStruct((experts, 3, 4 * (final << steps), hidden), low),
             jax.ShapeDtypeStruct(dense_shape, low),
@@ -1183,6 +1217,7 @@
             jax.ShapeDtypeStruct((token_count, features), jnp.float32),
         ],
         scratch_shapes=[
+            pltpu.VMEM((experts, 3, 4 * (final << steps), hidden), low),
             pltpu.VMEM((token_count, 2 * features), low),
             pltpu.VMEM((token_count, features), low),
             pltpu.VMEM((token_count, features), low),
@@ -1253,7 +1288,7 @@
     table_ref,
     column_ref,
     row_ref,
-    weights_out,
+    weights_hbm,
     moments_out,
     small_out,
     cot_out,
@@ -1264,6 +1299,7 @@
     pair_out,
     head_out,
     total_out,
+    weights_out,
     local_sem,
     line_send,
     line_recv,
@@ -1442,36 +1478,36 @@
     inputs = tokens_ref[...].astype(jnp.float32)
     first_out[...] = (normalize(inputs)[0] * gain(0)).astype(jnp.bfloat16)
     advance(0, 0)
-    line_start()
     line_send_group(1)
     for level in range(1, steps + 1):
         advance(level, 0)
-        if level == 1:
-            line_step(1)
     for other in others:
         for stream in streams:
             join_copy(0, stream, other).wait_recv()
     own_copies[0].wait()
+    leave = pltpu.make_async_copy(weights_out, weights_hbm, local_sem.at[2])
+    leave.start()
 
     def whole(index):
         return weights_out[index].reshape(count * rows, width)
 
     project_inputs(first_out[...], whole, query_out, pair_out, table_ref)
     advance(0, 1)
-    if count > 2:
-        line_step(2)
+    line_start()
     bias = allowed_pairs(column_ref[...], row_ref[...])
     quarter = KVHEADS // 4
     attend_forward(range(quarter), query_out, pair_out, bias, head_out, total_out)
     advance(1, 1)
-    for step in range(3, count):
-        line_step(step)
-    attend_forward(range(quarter, KVHEADS), query_out, pair_out, bias, head_out, total_out)
+    attend_forward(range(quarter, 2 * quarter), query_out, pair_out, bias, head_out, total_out)
+    line_step(1)
+    attend_forward(range(2 * quarter, KVHEADS), query_out, pair_out, bias, head_out, total_out)
     for level in range(2, steps + 1):
         advance(level, 1)
     middle = inputs + dot_nn(head_out[...], whole(2))
     middle_out[...] = middle
     second_out[...] = (normalize(middle)[0] * gain(1)).astype(jnp.bfloat16)
+    for step in range(2, count):
+        line_step(step)
     for group in range(groups):
         for other in others:
             for stream in streams:
@@ -1494,6 +1530,7 @@
             hand_on(block, False).wait_send()
 
     own_copies[1].wait()
+    leave.wait()
 
 
 def gather(weights, moments, small, tokens, cotangent, tables, starts, bits, count):
@@ -1508,7 +1545,7 @@
     return pl.pallas_call(
         functools.partial(gather_kernel, count, bits),
         in_specs=[vmem] * 8,
-        out_specs=[vmem] * 11,
+        out_specs=[pl.BlockSpec(memory_space=pl.ANY)] + [vmem] * 10,
         out_shape=[
             whole,
             whole,
@@ -1523,7 +1560,8 @@
             jax.ShapeDtypeStruct((2 * token_count, KVHEADS), jnp.float32),
         ],
         scratch_shapes=[
-            dma((2,)),
+            pltpu.VMEM(whole.shape, low),
+            dma((3,)),
             dma((2, 2, count)),
             dma((2, 2, count)),
             dma((steps, 2, 2, count)),
@@ -1660,26 +1698,34 @@
     midnorm_next = momentum_keep * midnorm_moment + midnorm_grad
     prenorm_update = -rate_gain * prenorm_next
     midnorm_update = -rate_gain * midnorm_next
+    rep_index = lax.axis_index("rep")
     (
         query_grad,
         query_next,
-        query_update,
         key_grad,
         key_next,
-        key_update,
         value_grad,
         value_next,
-        value_update,
         out_grad,
         out_next,
-        out_update,
+        own_wide,
+        own_narrow,
     ) = dense_update(
         dense_grads,
         moments,
         (query_moment, key_moment, value_moment, out_moment),
         LAYOUT,
         shard_index,
+        rep_index,
     )
+    pairs = [(index, index + 1 - 2 * (index % 2)) for index in range(rep_count)]
+    other_wide = lax.ppermute(own_wide, "rep", pairs)
+    other_narrow = lax.ppermute(own_narrow, "rep", pairs)
+    first_core = rep_index % 2 == 0
+    query_update = jnp.where(first_core, own_wide, other_wide)
+    out_update = jnp.where(first_core, other_wide, own_wide)
+    key_update = jnp.where(first_core, own_narrow, other_narrow)
+    value_update = jnp.where(first_core, other_narrow, own_narrow)
     gate_grad, gate_next, gate_update, up_grad, up_next, up_update = expert_update(
         expert_grads, (0, 1), (gate_moment, up_moment)
     )

time: 478 us -> 453 us (0.948)
  Pallas kernels: 451 us -> 421 us
  other arithmetic: 10.1 us -> 15.4 us
    pallas_call x1, Pallas kernels: 46.7 us -> 24.1 us  [dense_update(): pl.pallas_call(functools.partial(dense_update_kernel, layout), grid=(1,),...]
    pallas_call x2, Pallas kernels: 54.8 us -> 49 us  [expert_update(): pl.pallas_call(functools.partial(expert_update_kernel, kinds, scale), gri...]
  transfers between devices with their start and end apart: 0 -> 2, of which waited for: 0 -> 0; matrix products, arithmetic and copies ran while one was open for 0% -> 1% of each run, Pallas kernels for 0% -> 11%
where the time goes in v2:
time: 453 us; the launch traced here: 446 us
  Pallas kernels  421 us (93%)
  other arithmetic  15.4 us (3%)
  local copies, waits for them, and re-layouts  7.75 us (2%)
    pallas_call x1, Pallas kernels, spread(): pl.pallas_call(functools.partial(spread_kernel, count, bits), in_specs=[v...  140 us
    pallas_call x1, Pallas kernels, moe(): pl.pallas_call(functools.partial(moe_kernel, count, bits), in_specs=[vmem...  118 us
    pallas_call x1, Pallas kernels, gather(): pl.pallas_call(functools.partial(gather_kernel, count, bits), in_specs=[v...  89.7 us
    pallas_call x2, Pallas kernels, expert_update(): pl.pallas_call(functools.partial(expert_update_kernel, kinds, scale), gri...  49 us
    pallas_call x1, Pallas kernels, dense_update(): pl.pallas_call(functools.partial(dense_update_kernel, layout), grid=(1,),...  24.1 us
  transfers between devices with their start and end apart: 2, of which 0 were waited for; matrix products, arithmetic and copies ran while one was open for 1% of the time, Pallas kernels for 11%

profile of v2, /device:TPU:0, one launch (start us, length us, event | category | flops | bytes accessed | tf_op | source)
XLA Modules:
  0.0 445.6 jit_solution(3667069797469093326)
XLA Ops:
  0.7 0.0 copy-start
  0.7 0.0 copy-start.1
  0.7 0.8 stack.62
  1.5 0.7 stack.63
  2.2 0.7 subtract_convert_fusion
  2.9 1.5 copy.56.column_ref
  4.3 1.1 convert_element_type.19
  5.4 0.0 copy-start.5
  5.4 0.0 copy-start.6
  5.4 1.2 convert_element_type.20
  6.6 0.8 select_reduce_fusion
  7.4 0.6 pad_maximum_fusion.3.small_ref
  8.0 0.5 multiply_cosine_fusion
  8.6 1.1 maximum_bitcast_fusion
  9.7 0.0 copy-done
  9.7 0.0 copy-done.1
  9.7 0.2 convert_bitcast_fusion
  9.9 0.4 maximum_bitcast_fusion.3
  10.2 0.8 pad_maximum_fusion.2.table_ref
  11.0 0.0 copy-done.5
  11.0 0.0 copy-done.6
  11.0 1.3 pad_maximum_fusion.weights_ref
  12.3 1.3 pad_maximum_fusion.1.moments_ref
  13.7 89.7 %gather.1 = (bf16[3,4,256,1024]{3,2,1,0:T(8,128)(2,1)}, bf16[3,4,256,1024]{3,2,1,0:T(8,128)(2,1)}, f32[4,24,256]{2,1,0:T(8,128)}, bf16[4,256,1024]{2,1,0:T(8,128...) custom-call(bf16[3,256,1024]{2,1,0:T(8,128)(2,1)} %pad_maximum_fusio, ...), custom_call_target="tpu_custom_call" | custom-call | tf_op jit(solution)/shard_map/gather/pallas_call | solution.py:1545
  103.3 1.1 copy.57
  104.4 0.6 pad_add_fusion.place_ref
  105.0 1.0 dynamic-slice_bitcast_fusion.weight_ref
  106.0 117.6 %moe.1 = (bf16[256,1024]{1,0:T(8,128)(2,1)}, f32[256,1024]{1,0:T(8,128)}, bf16[4,3,2,64,512]{4,3,2,1,0:T(8,128)(2,1)}) custom-call(bf16[256,1024]{1,0:T(8,128)(2,1)} %get-tuple-element.66.own_ref, f32[256,1024]{1,0:T(8,128)} %get-tuple-element.67.middle_ref, bf16[4,256,1024]{2,1,0:T(8,128)(2,1)} %get-tuple-element.68.cot_ref, ...), custom_call_target="tpu_custom_call" | custom-call | flops 38999998464 | bytes 20000000 | tf_op jit(solution)/shard_map/moe/pallas_call | solution.py:705
  223.6 140.2 %spread.1 = (bf16[4,3,1024,512]{3,2,1,0:T(8,128)(2,1)}, bf16[8,4,256,384]{3,2,1,0:T(8,128)(2,1)}, f32[8,1024]{1,0:T(8,128)}, f32[256,1024]{1,0:T(8,128)}) custom-call(bf16[4,3,2,64,512]{4,3,2,1,0:T(8,128)(2,1)} %get-tuple-element.71.share_ref, bf16[256,1024]{1,0:T(8,128)(2,1)} %get-tuple-element.72.normed_ref, bf16[256,1024]{1,0:T(8,128)(2,1)} %get-tuple-element.73.head_ref, ...), custom_call_target="tpu_custom_call" | custom-call | tf_op jit(solution)/shard_map/spread/pallas_call | solution.py:1209
  363.9 24.1 %dense_update.1 = (f32[256,1024]{1,0:T(8,128)}, f32[256,1024]{1,0:T(8,128)}, f32[256,512]{1,0:T(8,128)}, f32[256,512]{1,0:T(8,128)}, f32[256,512]{1,0:T(8,128)},...) custom-call(s32[2]{0:T(128)} %pad_add_fusion.place_ref, ...), custom_call_target="tpu_custom_call" | custom-call | flops 14000000000 | bytes 25165824 | tf_op jit(solution)/shard_map/dense_update/pallas_call | solution.py:350
  388.0 0.6 collective-permute-start.1
  388.6 0.1 collective-permute-start
  388.7 31.3 %expert_update.2 = (f32[4,1024,512]{2,1,0:T(8,128)}, f32[4,1024,512]{2,1,0:T(8,128)}, f32[4,1024,512]{2,1,0:T(8,128)}, f32[4,1024,512]{2,1,0:T(8,128)}, f32[4,10...) custom-call(bf16[4,3,1024,512]{3,2,1,0:T(8,128)(2,1)} %get-tuple-element.93.refs_0_, f32[4,1024,512]{2,1,0:T(8,128)} %refs_1_.4, ...), custom_call_target="tpu_custom_call" | custom-call | flops 20000000000 | bytes 75497472 | tf_op jit(solution)/shard_map/expert_update/pallas_call | solution.py:255
  420.0 0.0 copy-start.2
  420.0 17.7 %expert_update.3 = (f32[4,512,1024]{2,1,0:T(8,128)}, f32[4,512,1024]{2,1,0:T(8,128)}, f32[4,512,1024]{2,1,0:T(8,128)}) custom-call(bf16[4,3,1024,512]{3,2,1,0:T(8,128)(2,1)} %get-tuple-element.93.refs_0_, f32[4,512,1024]{2,1,0:T(8,128)} %refs_1_.5), custom_call_target="tpu_custom_call" | custom-call | flops 10000000000 | bytes 37748736 | tf_op jit(solution)/shard_map/expert_update/pallas_call | solution.py:255
  437.7 0.9 fusion.5
  438.7 0.0 copy-done.9
  438.7 0.6 broadcast_multiply_fusion.1
  439.2 0.0 copy-done.10
  439.2 0.6 broadcast_multiply_fusion
  439.8 0.0 collective-permute-done.1
  439.8 2.3 broadcast_select_fusion.2
  442.1 0.0 collective-permute-done
  442.1 0.0 copy-done.2
  442.1 1.5 broadcast_select_fusion
  443.6 0.8 copy.61
  444.4 1.0 copy.62
  445.4 0.0 copy-done.8
  (13 shorter events, 0.1 us)
Async XLA Ops:
  0.7 9.0 %copy-start = (f32[256,1024]{1,0:T(8,128)S(1)}, f32[256,1024]{1,0:T(8,128)}, u32[]{:S(2)}) copy-start(f32[256,1024]{1,0:T(8,128)} %refs_3_.1) | copy-start | bytes 3145732
  0.7 9.0 %copy-start.1 = (f32[256,1024]{1,0:T(8,128)S(1)}, f32[256,1024]{1,0:T(8,128)}, u32[]{:S(2)}) copy-start(f32[256,1024]{1,0:T(8,128)} %refs_0_.1) | copy-start | bytes 3145732
  5.4 5.6 %copy-start.5 = (bf16[256,1024]{1,0:T(8,128)(2,1)S(1)}, bf16[256,1024]{1,0:T(8,128)(2,1)}, u32[]{:S(2)}) copy-start(bf16[256,1024]{1,0:T(8,128)(2,1)} %param.31) | copy-start | bytes 1572868
  5.4 5.6 %copy-start.6 = (bf16[256,1024]{1,0:T(8,128)(2,1)S(1)}, bf16[256,1024]{1,0:T(8,128)(2,1)}, u32[]{:S(2)}) copy-start(bf16[256,1024]{1,0:T(8,128)(2,1)} %param.28) | copy-start | bytes 1572868
  388.0 51.8 %collective-permute-start.1 = (f32[256,512]{1,0:T(8,128)}, f32[256,512]{1,0:T(8,128)}, u32[]{:S(2)}, u32[]{:S(2)}) collective-permute-start(f32[256,512]{1,0:T(8,128)} %get-tuple-element.87), channel_id=1, source_target_pairs={{0,4},{4,0},{8,12},{12,8},{16,20},{20,16},{24,28},{28,24},{1,5},{5... | collective-permute-start | bytes 1572872 | tf_op jit(solution)/shard_map/ppermute | solution.py:1723
  388.6 53.5 %collective-permute-start = (f32[256,1024]{1,0:T(8,128)}, f32[256,1024]{1,0:T(8,128)S(1)}, u32[]{:S(2)}, u32[]{:S(2)}) collective-permute-start(f32[256,1024]{1,0:T(8,128)} %get-tuple-element.84), channel_id=1, source_target_pairs={{0,4},{4,0},{8,12},{12,8},{16,20},{20,16},{24,28},{28,24},{1,5},{5... | collective-permute-start | bytes 3145736 | tf_op jit(solution)/shard_map/ppermute | solution.py:1722
  420.0 18.7 %copy-start.9 = (f32[256]{0:T(256)S(1)}, f32[256]{0:T(256)}, u32[]{:S(2)}) copy-start(f32[256]{0:T(256)} %param.41) | copy-start | bytes 3076
  420.0 19.2 %copy-start.10 = (f32[256]{0:T(256)S(1)}, f32[256]{0:T(256)}, u32[]{:S(2)}) copy-start(f32[256]{0:T(256)} %param.42) | copy-start | bytes 3076
  420.0 22.1 %copy-start.2 = (f32[256,1024]{1,0:T(8,128)S(1)}, f32[256,1024]{1,0:T(8,128)}, u32[]{:S(2)}) copy-start(f32[256,1024]{1,0:T(8,128)} %get-tuple-element.84) | copy-start | bytes 3145732
  437.7 6.6 %copy-start.3 = (f32[256,1024]{1,0:T(8,128)S(1)}, f32[256,1024]{1,0:T(8,128)}, u32[]{:S(2)}) copy-start(f32[256,1024]{1,0:T(8,128)} %get-tuple-element.151) | copy-start | bytes 3145732
  437.7 5.8 %copy-start.4 = (bf16[256,1024]{1,0:T(8,128)(2,1)S(1)}, bf16[256,1024]{1,0:T(8,128)(2,1)}, u32[]{:S(2)}) copy-start(bf16[256,1024]{1,0:T(8,128)(2,1)} %get-tuple-element.150) | copy-start | bytes 1572868
  438.7 6.7 %copy-start.7 = (f32[1,256]{1,0:T(1,128)}, f32[1,256]{1,0:T(1,128)S(1)}, u32[]{:S(2)}) copy-start(f32[1,256]{1,0:T(1,128)S(1)} %get-tuple-element.113) | copy-start | bytes 3076
  438.7 6.7 %copy-start.8 = (f32[1,256]{1,0:T(1,128)}, f32[1,256]{1,0:T(1,128)S(1)}, u32[]{:S(2)}) copy-start(f32[1,256]{1,0:T(1,128)S(1)} %get-tuple-element.114) | copy-start | bytes 3076

commit v3 on v2

--- a/solution.py
+++ b/solution.py
@@ -409,13 +409,12 @@
     count,
     bits,
     own_ref,
-    middle_ref,
     cot_ref,
     weight_ref,
     gate_hbm,
     up_hbm,
     down_hbm,
-    out_ref,
+    stage_out,
     back_ref,
     share_ref,
     tok,
@@ -425,9 +424,7 @@
     gate_delta,
     up_delta,
     stage_back,
-    stage_out,
     got_back,
-    got_out,
     *rest,
 ):
     landing = rest[: 1 + 2 * len(bits)]
@@ -438,8 +435,6 @@
         arrive_sem,
         back_send,
         back_recv,
-        out_send,
-        out_recv,
         sum_send,
         sum_recv,
     ) = rest[1 + 2 * len(bits) :]
@@ -583,9 +578,6 @@
         def _():
             returning(stage_back, got_back, back_send, back_recv, block).start()
 
-    for k in range(1, count):
-        returning(stage_out, got_out, out_send, out_recv, lax.rem(me + k, count)).start()
-
     plan = stream_plan(rep, bits, core * half, half // 2)
 
     def sum_copy(stage, slot, e, start, size, bit):
@@ -655,24 +647,9 @@
         ).wait_recv()
         total = total + got_back[source].astype(jnp.float32)
     back_ref[...] = total
-    total = stage_out[me].astype(jnp.float32)
-    for k in range(1, count):
-        source = lax.rem(me + k, count)
-        pltpu.make_async_remote_copy(
-            src_ref=stage_out.at[source],
-            dst_ref=got_out.at[source],
-            send_sem=out_send.at[source],
-            recv_sem=out_recv.at[source],
-            device_id=(rep, source),
-            device_id_type=MESH,
-        ).wait_recv()
-        total = total + got_out[source].astype(jnp.float32)
-    out_ref[...] = (middle_ref[...] + total).astype(out_ref.dtype)
-
     for k in range(1, count):
         block = lax.rem(me + k, count)
         returning(stage_back, got_back, back_send, back_recv, block).wait_send()
-        returning(stage_out, got_out, out_send, out_recv, block).wait_send()
     for e in range(experts):
         for stage in range(stages):
             for copy, _, _, _ in copies(stage, e):
@@ -688,7 +665,7 @@
             hand_on(block, False).wait_send()
 
 
-def moe(normed, middle, cotangents, weights, gate_proj, up_proj, down_proj, bits, count):
+def moe(normed, cotangents, weights, gate_proj, up_proj, down_proj, bits, count):
     tokens, width = normed.shape
     experts, _, hidden = gate_proj.shape
     half = width // 2
@@ -704,10 +681,10 @@
     dma = pltpu.SemaphoreType.DMA
     return pl.pallas_call(
         functools.partial(moe_kernel, count, bits),
-        in_specs=[vmem, vmem, vmem, vmem, anywhere, anywhere, anywhere],
+        in_specs=[vmem, vmem, vmem, anywhere, anywhere, anywhere],
         out_specs=[vmem, vmem, vmem],
         out_shape=[
-            jax.ShapeDtypeStruct((tokens, width), low),
+            jax.ShapeDtypeStruct((count, tokens, width), low),
             jax.ShapeDtypeStruct((tokens, width), jnp.float32),
             jax.ShapeDtypeStruct((experts, 3, 2, final, hidden), low),
         ],
@@ -720,14 +697,10 @@
             pltpu.VMEM((experts, count * tokens, hidden), low),
             pltpu.VMEM((count, tokens, width), low),
             pltpu.VMEM((count, tokens, width), low),
-            pltpu.VMEM((count, tokens, width), low),
-            pltpu.VMEM((count, tokens, width), low),
         ]
         + landings
         + [
             dma((4,)),
-            dma((count,)),
-            dma((count,)),
             dma((count,)),
             dma((count,)),
             dma((count,)),
@@ -743,7 +716,7 @@
         cost_estimate=pl.CostEstimate(
             flops=39000000000, bytes_accessed=20000000, transcendentals=2000000
         ),
-    )(normed, middle, cotangents, weights, gate_proj, up_proj, down_proj)
+    )(normed, cotangents, weights, gate_proj, up_proj, down_proj)
 
 
 def rep_bits(rep_count):
@@ -759,6 +732,7 @@
     count,
     bits,
     share_ref,
+    returned_ref,
     normed_ref,
     head_ref,
     weights_ref,
@@ -777,7 +751,9 @@
     dense_out,
     gains_out,
     tokens_out,
+    mixed_out,
     experts_out,
+    got_ref,
     delta_ref,
     branch_ref,
     heads_ref,
@@ -815,6 +791,8 @@
         gain_recv,
         gain_line_send,
         gain_line_recv,
+        back_send,
+        back_recv,
     ) = rest[later:]
     rep = lax.axis_index("rep")
     me = lax.axis_index("shard")
@@ -879,6 +857,15 @@
     peers += [across(bit) for bit in (1,) + bits]
     greet(peers)
 
+    def returning(peer, source):
+        return remote(
+            returned_ref.at[peer],
+            got_ref.at[source],
+            back_send.at[peer],
+            back_recv.at[source],
+            (rep, peer),
+        )
+
     def core_copy(block):
         return remote(
             dense_ref.at[4 * (1 - core) + block],
@@ -901,6 +888,9 @@
 
     for stream in streams:
         expert_copy(0, stream).start()
+
+    for k in range(1, count):
+        returning(lax.rem(me + k, count), me).start()
 
     def whole(index):
         return weights_ref[index].reshape(count * rows, -1)
@@ -1154,6 +1144,12 @@
         for k in range(1, count):
             line_arrival(lax.rem(me + k, count), stream).wait_recv()
         grow_copy(steps - 1, stream).start()
+    mixed = middle_ref[...] + returned_ref[me].astype(jnp.float32)
+    for k in range(1, count):
+        source = lax.rem(me + k, count)
+        returning(source, source).wait_recv()
+        mixed = mixed + got_ref[source].astype(jnp.float32)
+    mixed_out[...] = mixed.astype(mixed_out.dtype)
     for stream in streams:
         expert_copy(steps, stream).wait()
     leave = pltpu.make_async_copy(experts_out, experts_hbm, local_sem.at[0])
@@ -1188,11 +1184,12 @@
     for k in range(1, count):
         shard_copy(k).wait_send()
         gain_line(k).wait_send()
+        returning(lax.rem(me + k, count), me).wait_send()
     leave.wait()
 
 
 def spread(
-    share, normed, head_low, weights, small, tokens, cotangent, second, middle, *rest, bits, count
+    share, returned, normed, head_low, weights, small, tokens, cotangent, second, middle, *rest, bits, count
 ):
     query, pair, log_total, tables, starts = rest
     experts, _, _, final, hidden = share.shape
@@ -1208,16 +1205,18 @@
     dma = pltpu.SemaphoreType.DMA
     return pl.pallas_call(
         functools.partial(spread_kernel, count, bits),
-        in_specs=[vmem] * 15,
-        out_specs=[pl.BlockSpec(memory_space=pl.ANY)] + [vmem] * 3,
+        in_specs=[vmem] * 16,
+        out_specs=[pl.BlockSpec(memory_space=pl.ANY)] + [vmem] * 4,
         out_shape=[
             jax.ShapeDtypeStruct((experts, 3, 4 * (final << steps), hidden), low),
             jax.ShapeDtypeStruct(dense_shape, low),
             jax.ShapeDtypeStruct(gains_shape, jnp.float32),
             jax.ShapeDtypeStruct((token_count, features), jnp.float32),
+            jax.ShapeDtypeStruct((token_count, features), low),
         ],
         scratch_shapes=[
             pltpu.VMEM((experts, 3, 4 * (final << steps), hidden), low),
+            pltpu.VMEM((count, token_count, features), low),
             pltpu.VMEM((token_count, 2 * features), low),
             pltpu.VMEM((token_count, features), low),
             pltpu.VMEM((token_count, features), low),
@@ -1253,6 +1252,8 @@
             dma((steps + 1,)),
             dma((count,)),
             dma((count,)),
+            dma((count,)),
+            dma((count,)),
         ],
         compiler_params=pltpu.CompilerParams(
             collective_id=2, has_side_effects=True, vmem_limit_bytes=63 * 1024 * 1024
@@ -1260,6 +1261,7 @@
         name="spread",
     )(
         share,
+        returned,
         normed,
         head_low,
         weights,
@@ -1280,8 +1282,14 @@
 def gather_kernel(
     count,
     bits,
-    weights_ref,
-    moments_ref,
+    query_weight,
+    key_weight,
+    value_weight,
+    out_weight,
+    query_moment,
+    key_moment,
+    value_moment,
+    out_moment,
     small_ref,
     tokens_ref,
     cot_ref,
@@ -1289,7 +1297,7 @@
     column_ref,
     row_ref,
     weights_hbm,
-    moments_out,
+    moments_hbm,
     small_out,
     cot_out,
     middle_out,
@@ -1300,6 +1308,9 @@
     head_out,
     total_out,
     weights_out,
+    moments_out,
+    weights_ref,
+    moments_ref,
     local_sem,
     line_send,
     line_recv,
@@ -1335,6 +1346,15 @@
     def side(bit):
         return (rep // bit) % 2
 
+    narrow = width // 2
+    for target, sources in (
+        (weights_ref, (query_weight, key_weight, value_weight, out_weight)),
+        (moments_ref, (query_moment, key_moment, value_moment, out_moment)),
+    ):
+        target[0] = sources[0][...].astype(target.dtype)
+        target[1, :, :narrow] = sources[1][...].astype(target.dtype)
+        target[1, :, narrow:] = sources[2][...].astype(target.dtype)
+        target[2] = sources[3][...].astype(target.dtype)
     own_copies = [
         pltpu.make_async_copy(weights_ref, weights_out.at[:, me], local_sem.at[0]),
         pltpu.make_async_copy(moments_ref, moments_out.at[:, me], local_sem.at[1]),
@@ -1481,6 +1501,8 @@
     line_send_group(1)
     for level in range(1, steps + 1):
         advance(level, 0)
+    advance(0, 1)
+    line_start()
     for other in others:
         for stream in streams:
             join_copy(0, stream, other).wait_recv()
@@ -1492,28 +1514,36 @@
         return weights_out[index].reshape(count * rows, width)
 
     project_inputs(first_out[...], whole, query_out, pair_out, table_ref)
-    advance(0, 1)
-    line_start()
     bias = allowed_pairs(column_ref[...], row_ref[...])
     quarter = KVHEADS // 4
-    attend_forward(range(quarter), query_out, pair_out, bias, head_out, total_out)
     advance(1, 1)
-    attend_forward(range(quarter, 2 * quarter), query_out, pair_out, bias, head_out, total_out)
+    attend_forward(range(2 * quarter), query_out, pair_out, bias, head_out, total_out)
     line_step(1)
     attend_forward(range(2 * quarter, KVHEADS), query_out, pair_out, bias, head_out, total_out)
     for level in range(2, steps + 1):
         advance(level, 1)
+    leaving = pltpu.make_async_copy(moments_out, moments_hbm, local_sem.at[3])
+
+    def moments_leave():
+        for other in others:
+            for stream in streams:
+                join_copy(1, stream, other).wait_recv()
+        own_copies[1].wait()
+        leaving.start()
+
     middle = inputs + dot_nn(head_out[...], whole(2))
     middle_out[...] = middle
     second_out[...] = (normalize(middle)[0] * gain(1)).astype(jnp.bfloat16)
     for step in range(2, count):
         line_step(step)
+        if step == 2:
+            moments_leave()
+    if count < 3:
+        moments_leave()
     for group in range(groups):
         for other in others:
             for stream in streams:
                 join_copy(group, stream, other).wait_send()
-                if group == 1:
-                    join_copy(group, stream, other).wait_recv()
                 line_copy(group, stream, me, other).wait_send()
                 for step in range(steps):
                     grow_copy(step, group, stream, other).wait_send()
@@ -1529,12 +1559,13 @@
         def _():
             hand_on(block, False).wait_send()
 
-    own_copies[1].wait()
     leave.wait()
+    leaving.wait()
 
 
 def gather(weights, moments, small, tokens, cotangent, tables, starts, bits, count):
-    depth, rows, width = weights.shape
+    rows, width = weights[0].shape
+    depth = 3
     token_count = tokens.shape[0]
     steps = len(bits)
     low = jnp.bfloat16
@@ -1544,8 +1575,8 @@
     features = jax.ShapeDtypeStruct((token_count, width), low)
     return pl.pallas_call(
         functools.partial(gather_kernel, count, bits),
-        in_specs=[vmem] * 8,
-        out_specs=[pl.BlockSpec(memory_space=pl.ANY)] + [vmem] * 10,
+        in_specs=[vmem] * 14,
+        out_specs=[pl.BlockSpec(memory_space=pl.ANY)] * 2 + [vmem] * 9,
         out_shape=[
             whole,
             whole,
@@ -1561,7 +1592,10 @@
         ],
         scratch_shapes=[
             pltpu.VMEM(whole.shape, low),
-            dma((3,)),
+            pltpu.VMEM(whole.shape, low),
+            pltpu.VMEM((depth, rows, width), low),
+            pltpu.VMEM((depth, rows, width), low),
+            dma((4,)),
             dma((2, 2, count)),
             dma((2, 2, count)),
             dma((steps, 2, 2, count)),
@@ -1578,7 +1612,16 @@
             collective_id=3, has_side_effects=True, vmem_limit_bytes=56 * 1024 * 1024
         ),
         name="gather",
-    )(weights, moments, small, tokens, cotangent, tables, starts[:, None], starts[None, :])
+    )(
+        *weights,
+        *moments,
+        small,
+        tokens,
+        cotangent,
+        tables,
+        starts[:, None],
+        starts[None, :],
+    )
 
 
 def local(
@@ -1612,17 +1655,6 @@
     row_block = query_proj.shape[0]
     bits = rep_bits(rep_count)
     experts_here = gate_proj.shape[0]
-    low = jnp.bfloat16
-    own_weights = jnp.stack(
-        [query_proj, jnp.concatenate([key_proj, value_proj], axis=1), out_proj]
-    )
-    own_moments = jnp.stack(
-        [
-            query_moment.astype(low),
-            jnp.concatenate([key_moment.astype(low), value_moment.astype(low)], axis=1),
-            out_moment.astype(low),
-        ]
-    )
     dense_weights = jnp.sum(
         jnp.where(
             routes.T[None, :, :] == jnp.arange(EXPERTS, dtype=jnp.int32)[:, None, None],
@@ -1649,8 +1681,8 @@
         head_low,
         log_total,
     ) = gather(
-        own_weights,
-        own_moments,
+        (query_proj, key_proj, value_proj, out_proj),
+        (query_moment, key_moment, value_moment, out_moment),
         jnp.concatenate([dense_weights, gain_rows], axis=0),
         tokens,
         cotangent,
@@ -1662,9 +1694,8 @@
     expert_weights = lax.dynamic_slice_in_dim(
         small, shard_index * experts_here, experts_here, 1
     ).transpose(0, 2, 1)
-    mixed, grad_second, expert_share = moe(
+    returned, grad_second, expert_share = moe(
         normed_second,
-        middle,
         cotangent_all,
         expert_weights,
         gate_proj,
@@ -1673,8 +1704,9 @@
         bits,
         shard_count,
     )
-    expert_grads, dense_grads, gains_grad, grad_tokens = spread(
+    expert_grads, dense_grads, gains_grad, grad_tokens, mixed = spread(
         expert_share,
+        returned,
         normed_first,
         head_low,
         weights,

time: 453 us -> 421 us (0.929)
  Pallas kernels: 421 us -> 395 us
  other arithmetic: 15.4 us -> 9.24 us
    pallas_call x1, Pallas kernels: 140 us -> 126 us  [spread(): pl.pallas_call(functools.partial(spread_kernel, count, bits), in_specs=[v...]
    pallas_call x1, Pallas kernels: 118 us -> 109 us  [moe(): pl.pallas_call(functools.partial(moe_kernel, count, bits), in_specs=[vmem...]
  transfers between devices with their start and end apart: 2 -> 2, of which waited for: 0 -> 0; matrix products, arithmetic and copies ran while one was open for 1% -> 1% of each run, Pallas kernels for 11% -> 12%
where the time goes in v3:
time: 421 us; the launch traced here: 414 us
  Pallas kernels  395 us (94%)
  other arithmetic  9.24 us (2%)
  local copies, waits for them, and re-layouts  8.59 us (2%)
    pallas_call x1, Pallas kernels, spread(): pl.pallas_call(functools.partial(spread_kernel, count, bits), in_specs=[v...  126 us
    pallas_call x1, Pallas kernels, moe(): pl.pallas_call(functools.partial(moe_kernel, count, bits), in_specs=[vmem...  109 us
    pallas_call x1, Pallas kernels, gather(): pl.pallas_call(functools.partial(gather_kernel, count, bits), in_specs=[v...  87 us
    pallas_call x2, Pallas kernels, expert_update(): pl.pallas_call(functools.partial(expert_update_kernel, kinds, scale), gri...  49.1 us
    pallas_call x1, Pallas kernels, dense_update(): pl.pallas_call(functools.partial(dense_update_kernel, layout), grid=(1,),...  24.3 us
  transfers between devices with their start and end apart: 2, of which 0 were waited for; matrix products, arithmetic and copies ran while one was open for 1% of the time, Pallas kernels for 12%

profile of v3, /device:TPU:0, one launch (start us, length us, event | category | flops | bytes accessed | tf_op | source)
XLA Modules:
  0.0 414.5 jit_solution(12618558129507082353)
XLA Ops:
  0.7 0.7 stack.30
  1.4 0.7 stack.31
  2.0 0.7 subtract_convert_fusion
  2.7 1.5 copy.56.column_ref
  4.2 0.8 select_reduce_fusion
  4.9 0.6 pad_maximum_fusion.1.small_ref
  5.6 0.5 multiply_cosine_fusion
  6.1 0.4 maximum_bitcast_fusion.1
  6.5 0.8 pad_maximum_fusion.table_ref
  7.3 87.0 %gather.1 = (bf16[3,4,256,1024]{3,2,1,0:T(8,128)(2,1)}, bf16[3,4,256,1024]{3,2,1,0:T(8,128)(2,1)}, f32[4,24,256]{2,1,0:T(8,128)}, bf16[4,256,1024]{2,1,0:T(8,128...) custom-call(bf16[256,1024]{1,0:T(8,128)(2,1)} %query_weight.1, ...), custom_call_target="tpu_custom_call" | custom-call | tf_op jit(solution)/shard_map/gather/pallas_call | solution.py:1576
  94.3 1.1 copy.57
  95.4 0.6 pad_add_fusion.place_ref
  96.0 1.0 dynamic-slice_bitcast_fusion.weight_ref
  97.0 108.6 %moe.1 = (bf16[4,256,1024]{2,1,0:T(8,128)(2,1)}, f32[256,1024]{1,0:T(8,128)}, bf16[4,3,2,64,512]{4,3,2,1,0:T(8,128)(2,1)}) custom-call(bf16[256,1024]{1,0:T(8,128)(2,1)} %get-tuple-element.67.own_ref, bf16[4,256,1024]{2,1,0:T(8,128)(2,1)} %get-tuple-element.68.cot_ref, f32[4,256,4]{2,1,0:T(8,128)} %dynamic-slice_bitcast_fusion.weight_ref, ...), custom_call_target="tpu_custom_call" | custom-call | flops 38999998464 | bytes 20000000 | tf_op jit(solution)/shard_map/moe/pallas_call | solution.py:682
  205.6 126.1 %spread.1 = (bf16[4,3,1024,512]{3,2,1,0:T(8,128)(2,1)}, bf16[8,4,256,384]{3,2,1,0:T(8,128)(2,1)}, f32[8,1024]{1,0:T(8,128)}, f32[256,1024]{1,0:T(8,128)}, bf16[256,1024]{1,0:T(8,128)(2,1)}) custom-call(bf16[4,3,2,64,512]{4,3,2,1,0:T(8,128)(2,1)} %get-tuple-element.70.share_ref, bf16[4,256,1024]{2,1,0:T(8,128)(2,1)} %get-tuple-element.71.returned_ref, ...), custom_call_target="tpu_custom_call" | custom-call | tf_op jit(solution)/shard_map/spread/pallas_call | solution.py:1206
  331.7 24.3 %dense_update.1 = (f32[256,1024]{1,0:T(8,128)}, f32[256,1024]{1,0:T(8,128)}, f32[256,512]{1,0:T(8,128)}, f32[256,512]{1,0:T(8,128)}, f32[256,512]{1,0:T(8,128)},...) custom-call(s32[2]{0:T(128)} %pad_add_fusion.place_ref, ...), custom_call_target="tpu_custom_call" | custom-call | flops 14000000000 | bytes 25165824 | tf_op jit(solution)/shard_map/dense_update/pallas_call | solution.py:350
  356.0 0.4 collective-permute-start.1
  356.4 0.1 collective-permute-start
  356.5 31.3 %expert_update.2 = (f32[4,1024,512]{2,1,0:T(8,128)}, f32[4,1024,512]{2,1,0:T(8,128)}, f32[4,1024,512]{2,1,0:T(8,128)}, f32[4,1024,512]{2,1,0:T(8,128)}, f32[4,10...) custom-call(bf16[4,3,1024,512]{3,2,1,0:T(8,128)(2,1)} %get-tuple-element.95.refs_0_, f32[4,1024,512]{2,1,0:T(8,128)} %refs_1_.4, ...), custom_call_target="tpu_custom_call" | custom-call | flops 20000000000 | bytes 75497472 | tf_op jit(solution)/shard_map/expert_update/pallas_call | solution.py:255
  387.8 0.0 copy-start.4
  387.8 0.0 copy-start.5
  387.8 0.0 copy-start
  387.8 0.0 copy-start.1
  387.8 17.8 %expert_update.3 = (f32[4,512,1024]{2,1,0:T(8,128)}, f32[4,512,1024]{2,1,0:T(8,128)}, f32[4,512,1024]{2,1,0:T(8,128)}) custom-call(bf16[4,3,1024,512]{3,2,1,0:T(8,128)(2,1)} %get-tuple-element.95.refs_0_, f32[4,512,1024]{2,1,0:T(8,128)} %refs_1_.5), custom_call_target="tpu_custom_call" | custom-call | flops 10000000000 | bytes 37748736 | tf_op jit(solution)/shard_map/expert_update/pallas_call | solution.py:255
  405.6 0.8 fusion.5
  406.5 0.0 copy-start.2
  406.5 0.0 copy-start.3
  406.5 0.0 copy-done.4
  406.5 0.6 broadcast_multiply_fusion.1
  407.0 0.0 copy-done.5
  407.0 0.6 broadcast_multiply_fusion
  407.6 0.0 collective-permute-done.1
  407.6 2.3 broadcast_select_fusion.2
  409.9 0.0 collective-permute-done
  409.9 0.0 copy-done
  409.9 1.5 broadcast_select_fusion
  411.4 1.9 copy.61
  413.3 0.0 copy-done.1
  413.3 1.0 copy.62
  414.2 0.0 copy-done.2
  414.2 0.0 copy-done.3
  (3 shorter events, 0.0 us)
Async XLA Ops:
  356.0 51.6 %collective-permute-start.1 = (f32[256,512]{1,0:T(8,128)}, f32[256,512]{1,0:T(8,128)}, u32[]{:S(2)}, u32[]{:S(2)}) collective-permute-start(f32[256,512]{1,0:T(8,128)} %get-tuple-element.89), channel_id=1, source_target_pairs={{0,4},{4,0},{8,12},{12,8},{16,20},{20,16},{24,28},{28,24},{1,5},{5... | collective-permute-start | bytes 1572872 | tf_op jit(solution)/shard_map/ppermute | solution.py:1755
  356.4 53.5 %collective-permute-start = (f32[256,1024]{1,0:T(8,128)}, f32[256,1024]{1,0:T(8,128)S(1)}, u32[]{:S(2)}, u32[]{:S(2)}) collective-permute-start(f32[256,1024]{1,0:T(8,128)} %get-tuple-element.86), channel_id=1, source_target_pairs={{0,4},{4,0},{8,12},{12,8},{16,20},{20,16},{24,28},{28,24},{1,5},{5... | collective-permute-start | bytes 3145736 | tf_op jit(solution)/shard_map/ppermute | solution.py:1754
  387.8 18.7 %copy-start.4 = (f32[256]{0:T(256)S(1)}, f32[256]{0:T(256)}, u32[]{:S(2)}) copy-start(f32[256]{0:T(256)} %param.41) | copy-start | bytes 3076
  387.8 19.2 %copy-start.5 = (f32[256]{0:T(256)S(1)}, f32[256]{0:T(256)}, u32[]{:S(2)}) copy-start(f32[256]{0:T(256)} %param.42) | copy-start | bytes 3076
  387.8 22.1 %copy-start = (f32[256,1024]{1,0:T(8,128)S(1)}, f32[256,1024]{1,0:T(8,128)}, u32[]{:S(2)}) copy-start(f32[256,1024]{1,0:T(8,128)} %get-tuple-element.86) | copy-start | bytes 3145732
  387.8 25.4 %copy-start.1 = (f32[256,1024]{1,0:T(8,128)S(1)}, f32[256,1024]{1,0:T(8,128)}, u32[]{:S(2)}) copy-start(f32[256,1024]{1,0:T(8,128)} %get-tuple-element.151) | copy-start | bytes 3145732
  406.5 7.8 %copy-start.2 = (f32[1,256]{1,0:T(1,128)}, f32[1,256]{1,0:T(1,128)S(1)}, u32[]{:S(2)}) copy-start(f32[1,256]{1,0:T(1,128)S(1)} %get-tuple-element.115) | copy-start | bytes 3076
  406.5 7.8 %copy-start.3 = (f32[1,256]{1,0:T(1,128)}, f32[1,256]{1,0:T(1,128)S(1)}, u32[]{:S(2)}) copy-start(f32[1,256]{1,0:T(1,128)S(1)} %get-tuple-element.116) | copy-start | bytes 3076

commit v4 on v3

--- a/solution.py
+++ b/solution.py
@@ -268,7 +268,7 @@
     )(grads, *moments)
 
 
-def dense_update_kernel(layout, place_ref, grads_ref, moments_ref, *refs):
+def dense_update_kernel(layout, place_ref, next_ref, grads_ref, *refs):
     a = newton_first
     amount = len(layout)
     own_moments = refs[:amount]
@@ -276,36 +276,25 @@
     updates = refs[3 * amount : 3 * amount + 2]
     matrices = refs[3 * amount + 2 : 3 * amount + 4]
     own_grads = refs[3 * amount + 4]
-    blocks, count, block_rows, width = grads_ref.shape
+    blocks, count, block_rows, width = next_ref.shape
     part = width // 3
     me = place_ref[0]
     core = place_ref[1]
     start = pl.multiple_of(me * block_rows, block_rows)
 
-    def momentum(moments, grads):
-        return (
-            (momentum_keep * moments.astype(jnp.float32) + grads.astype(jnp.float32))
-            .astype(jnp.bfloat16)
-            .reshape(count * block_rows, part)
-        )
-
     for block in range(blocks):
         outer = slice(block * part, (block + 1) * part)
         lanes = pl.ds(pl.multiple_of(2 * core * part, part), part)
-        matrices[0][:, outer] = momentum(
-            moments_ref[2 * core, :, :, outer], grads_ref[block, :, :, lanes]
-        )
+        matrices[0][:, outer] = next_ref[block, :, :, lanes].reshape(count * block_rows, part)
         for index in range(3):
             columns = slice(8 * part * index + block * part, 8 * part * index + (block + 1) * part)
             inner = slice(index * part, (index + 1) * part)
-            own_grads[:, columns] = grads_ref[block, me, :, inner].astype(jnp.float32)
+            own_grads[:, columns] = grads_ref[block, :, inner].astype(jnp.float32)
     for block in range(blocks // 2):
         outer = slice(block * part, (block + 1) * part)
-        lanes = pl.ds(pl.multiple_of((core * (blocks // 2) + block) * part, part), part)
-        matrices[1][:, outer] = momentum(
-            moments_ref[1, :, :, lanes],
-            grads_ref[core * (blocks // 2) + block, :, :, part : 2 * part],
-        )
+        matrices[1][:, outer] = next_ref[
+            core * (blocks // 2) + block, :, :, part : 2 * part
+        ].reshape(count * block_rows, part)
     for index, (begin, size) in enumerate(layout):
         grad = own_grads[:, begin : begin + size]
         outs[2 * index][...] = grad
@@ -336,8 +325,9 @@
         )
 
 
-def dense_update(grads, moments, own_moments, layout, shard_index, rep_index):
-    _, count, block_rows, width = moments.shape
+def dense_update(nexts, grads, own_moments, layout, shard_index, rep_index):
+    _, count, block_rows, _ = nexts.shape
+    width = own_moments[0].shape[1]
     whole = lambda shape: pl.BlockSpec(shape, lambda i: (0,) * len(shape))
     shapes = []
     for _, size in layout:
@@ -350,7 +340,7 @@
     return pl.pallas_call(
         functools.partial(dense_update_kernel, layout),
         grid=(1,),
-        in_specs=[pl.BlockSpec(memory_space=pltpu.SMEM), whole(grads.shape), whole(moments.shape)]
+        in_specs=[pl.BlockSpec(memory_space=pltpu.SMEM), whole(nexts.shape), whole(grads.shape)]
         + [whole(moment.shape) for moment in own_moments],
         out_specs=[whole(shape.shape) for shape in shapes],
         out_shape=shapes,
@@ -364,7 +354,7 @@
         cost_estimate=pl.CostEstimate(
             flops=14000000000, bytes_accessed=24 * width * width, transcendentals=0
         ),
-    )(place, grads, moments, *own_moments)
+    )(place, nexts, grads, *own_moments)
 
 
 LAYOUT = ((0, 1024), (1024, 512), (1536, 512), (2048, 1024))
@@ -425,6 +415,8 @@
     up_delta,
     stage_back,
     got_back,
+    sum_back,
+    sum_out,
     *rest,
 ):
     landing = rest[: 1 + 2 * len(bits)]
@@ -508,7 +500,7 @@
     def dot_nt(left, right):
         return lax.dot_general(left, right, nt, preferred_element_type=jnp.float32)
 
-    def visit(j, carry):
+    def arrivals(j):
         lower = me - j
         upper = me + j
 
@@ -528,29 +520,53 @@
             def _():
                 hand_on(jnp.minimum(upper, count - 1), False).start()
 
+    def block_at(j):
         near = (j + 1) // 2
         alternating = me + near - 2 * near * (j % 2)
-        block = jnp.where(j <= 2 * margin, alternating, me + longer * (j - margin))
-        places = pl.ds(pl.multiple_of(block * tokens, tokens), tokens)
+        return jnp.where(j <= 2 * margin, alternating, me + longer * (j - margin))
+
+    def places_of(block):
+        return pl.ds(pl.multiple_of(block * tokens, tokens), tokens)
+
+    def factors(e, block):
+        places = places_of(block)
         rows = tok[block]
         grads = cot_ref[block]
-        turned[:, places] = rows.T
-        hiddens = []
-        for e in range(experts):
-            weight = weight_ref[block, :, e : e + 1]
-            u = dot(rows, mats[e, 0])
-            w = dot(rows, mats[e, 1])
-            gate = 1.0 / (1.0 + jnp.exp(-u))
-            act = u * gate
-            hidden = (weight * (act * w)).astype(jnp.bfloat16)
-            hid[e, :, places] = hidden.T
-            hiddens.append(hidden)
-            pulled = weight * (
-                dot_nt(grads[:, :half], mats[e, 2, :half])
-                + dot_nt(grads[:, half:], mats[e, 2, half:])
+        weight = weight_ref[block, :, e : e + 1]
+        u = dot(rows, mats[e, 0])
+        w = dot(rows, mats[e, 1])
+        gate = 1.0 / (1.0 + jnp.exp(-u))
+        act = u * gate
+        hidden = (weight * (act * w)).astype(jnp.bfloat16)
+        hid[e, :, places] = hidden.T
+        pulled = weight * (
+            dot_nt(grads[:, :half], mats[e, 2, :half])
+            + dot_nt(grads[:, half:], mats[e, 2, half:])
+        )
+        gate_delta[e, places] = (pulled * w * (gate + act * (1.0 - gate))).astype(jnp.bfloat16)
+        up_delta[e, places] = (pulled * act).astype(jnp.bfloat16)
+        return hidden
+
+    def sums(block, e, hidden, place):
+        places = places_of(block)
+        for side in range(2):
+            part = slice(side * half, (side + 1) * half)
+            back = dot_nt(gate_delta[e, places], mats[e, 0, part]) + dot_nt(
+                up_delta[e, places], mats[e, 1, part]
             )
-            gate_delta[e, places] = (pulled * w * (gate + act * (1.0 - gate))).astype(jnp.bfloat16)
-            up_delta[e, places] = (pulled * act).astype(jnp.bfloat16)
+            out = dot(hidden, mats[e, 2, part])
+            if e > 0:
+                back = place[0][:, part] + back
+                out = place[1][:, part] + out
+            place[0][:, part] = back
+            place[1][:, part] = out
+
+    def visit(j, carry):
+        arrivals(j)
+        block = block_at(j)
+        places = places_of(block)
+        turned[:, places] = tok[block].T
+        hiddens = [factors(e, block) for e in range(experts)]
         for side in range(2):
             part = slice(side * half, (side + 1) * half)
             total_back = None
@@ -571,13 +587,17 @@
 
         return carry
 
-    lax.fori_loop(0, count, visit, 0)
-    for block in range(count):
+    lax.fori_loop(0, count - 1, visit, 0)
+    arrivals(count - 1)
+    last = block_at(count - 1)
+    for k in range(1, count):
+        block = block_at(k - 1)
 
         @pl.when((block - me) * inward < 0)
         def _():
             returning(stage_back, got_back, back_send, back_recv, block).start()
 
+    turned[:, places_of(last)] = tok[last].T
     plan = stream_plan(rep, bits, core * half, half // 2)
 
     def sum_copy(stage, slot, e, start, size, bit):
@@ -617,12 +637,17 @@
     for turn in range(experts + stages):
         if turn < experts:
             e = turn
+            sums(last, e, factors(e, last), (sum_back, sum_out))
             for side in range(2):
                 part = slice(side * half, (side + 1) * half)
                 mats[e, 0, part] = dot(turned[part], gate_delta[e]).astype(jnp.bfloat16)
                 mats[e, 1, part] = dot(turned[part], up_delta[e]).astype(jnp.bfloat16)
                 mats[e, 2, part] = dot(hid[e], cot_ref[:, :, part].reshape(count * tokens, half)).astype(jnp.bfloat16)
             copies(0, e)[0][0].start()
+            if e == experts - 1:
+                stage_back[last] = sum_back[...].astype(jnp.bfloat16)
+                stage_out[last] = sum_out[...].astype(jnp.bfloat16)
+                returning(stage_back, got_back, back_send, back_recv, last).start()
         for stage in range(stages):
             e = turn - 1 - stage
             if 0 <= e < experts:
@@ -697,6 +722,8 @@
             pltpu.VMEM((experts, count * tokens, hidden), low),
             pltpu.VMEM((count, tokens, width), low),
             pltpu.VMEM((count, tokens, width), low),
+            pltpu.VMEM((tokens, width), jnp.float32),
+            pltpu.VMEM((tokens, width), jnp.float32),
         ]
         + landings
         + [
@@ -747,13 +774,19 @@
     table_ref,
     column_ref,
     row_ref,
+    query_moment,
+    key_moment,
+    value_moment,
+    out_moment,
     experts_hbm,
     dense_out,
+    grads_out,
     gains_out,
     tokens_out,
     mixed_out,
     experts_out,
     got_ref,
+    moment_piece,
     delta_ref,
     branch_ref,
     heads_ref,
@@ -793,6 +826,11 @@
         gain_line_recv,
         back_send,
         back_recv,
+        moment_sem,
+        own_send,
+        own_recv,
+        own_join_send,
+        own_join_recv,
     ) = rest[later:]
     rep = lax.axis_index("rep")
     me = lax.axis_index("shard")
@@ -985,6 +1023,40 @@
             start = start + near * size
         starts.append((start, size, line))
 
+    last = starts[0][1]
+    places = [rows_of(starts[stream][0], last) for stream in streams]
+    inner = [slice(index * part, (index + 1) * part) for index in range(3)]
+
+    def moment_copy(stream, index):
+        block = 4 * core + held[stream]
+        lanes = pl.ds(pl.multiple_of((held[stream] if index == 1 else block) * part, part), part)
+        source = (query_moment, key_moment, out_moment)[index]
+        return pltpu.make_async_copy(
+            source.at[places[stream], lanes],
+            moment_piece.at[stream, :, inner[index]],
+            moment_sem.at[stream, index],
+        )
+
+    def moment_other(stream):
+        lanes = pl.ds(pl.multiple_of(held[stream] * part, part), part)
+        return pltpu.make_async_copy(
+            value_moment.at[places[stream], lanes],
+            moment_piece.at[stream, :, inner[1]],
+            moment_sem.at[stream, 1],
+        )
+
+    for stream in streams:
+        moment_copy(stream, 0).start()
+        moment_copy(stream, 2).start()
+
+        @pl.when(core == 0)
+        def _():
+            moment_copy(stream, 1).start()
+
+        @pl.when(core == 1)
+        def _():
+            moment_other(stream).start()
+
     def later_copy(step, stream):
         keep, send, size = starts[stream][2][step - 1]
         return remote(
@@ -1026,8 +1098,6 @@
         if steps > 1:
             expert_copy(1, stream).start()
 
-    last = starts[0][1]
-    places = [rows_of(starts[stream][0], last) for stream in streams]
     for stream in streams:
         for line in range(count):
             piece_send[line, stream] = total[held[stream], line, places[stream]]
@@ -1070,6 +1140,27 @@
             (rep, source),
         )
 
+    def own_grow(step, stream):
+        block = 4 * core + held[stream]
+        if step == 0:
+            part_ref = grads_out.at[block]
+        else:
+            keep, _, size = starts[stream][2][step - 1]
+            part_ref = grads_out.at[block, rows_of(keep, size)]
+        return remote(
+            part_ref,
+            part_ref,
+            own_send.at[step, stream],
+            own_recv.at[step, stream],
+            across(order(stream)[step]),
+        )
+
+    def own_join(stream):
+        part_ref = grads_out.at[pl.ds(4 * core + 2 * stream, 2)]
+        return remote(
+            part_ref, part_ref, own_join_send.at[stream], own_join_recv.at[stream], across(1)
+        )
+
     for k in range(1, count):
         shard_copy(k).start()
         gain_line(k).start()
@@ -1078,7 +1169,12 @@
         source = lax.rem(me + k, count)
         shard_arrival(source).wait_recv()
         summed = summed + piece_land[source].astype(jnp.float32)
-    piece[...] = summed.astype(jnp.bfloat16)
+    for stream in streams:
+        for index in range(3):
+            moment_copy(stream, index).wait()
+        grads_out[4 * core + held[stream], places[stream]] = summed[stream].astype(jnp.bfloat16)
+        own_grow(steps - 1, stream).start()
+    piece[...] = (momentum_keep * moment_piece[...] + summed).astype(jnp.bfloat16)
 
     def line_copy(k, stream):
         target = lax.rem(me + k, count)
@@ -1144,6 +1240,13 @@
         for k in range(1, count):
             line_arrival(lax.rem(me + k, count), stream).wait_recv()
         grow_copy(steps - 1, stream).start()
+    for step in reversed(range(steps)):
+        for stream in streams:
+            own_grow(step, stream).wait_recv()
+            if step > 0:
+                own_grow(step - 1, stream).start()
+            else:
+                own_join(stream).start()
     mixed = middle_ref[...] + returned_ref[me].astype(jnp.float32)
     for k in range(1, count):
         source = lax.rem(me + k, count)
@@ -1168,6 +1271,9 @@
         join_copy(stream).start()
     for stream in streams:
         join_copy(stream).wait()
+        own_join(stream).wait()
+        for step in range(steps):
+            own_grow(step, stream).wait_send()
         for level in range(steps):
             expert_copy(level, stream).wait_send()
         first_copy(stream).wait_send()
@@ -1191,7 +1297,7 @@
 def spread(
     share, returned, normed, head_low, weights, small, tokens, cotangent, second, middle, *rest, bits, count
 ):
-    query, pair, log_total, tables, starts = rest
+    query, pair, log_total, tables, starts, moments = rest
     experts, _, _, final, hidden = share.shape
     token_count, features = normed.shape
     rows = features // count
@@ -1205,11 +1311,12 @@
     dma = pltpu.SemaphoreType.DMA
     return pl.pallas_call(
         functools.partial(spread_kernel, count, bits),
-        in_specs=[vmem] * 16,
-        out_specs=[pl.BlockSpec(memory_space=pl.ANY)] + [vmem] * 4,
+        in_specs=[vmem] * 16 + [pl.BlockSpec(memory_space=pl.ANY)] * 4,
+        out_specs=[pl.BlockSpec(memory_space=pl.ANY)] + [vmem] * 5,
         out_shape=[
             jax.ShapeDtypeStruct((experts, 3, 4 * (final << steps), hidden), low),
             jax.ShapeDtypeStruct(dense_shape, low),
+            jax.ShapeDtypeStruct((8, rows, width), low),
             jax.ShapeDtypeStruct(gains_shape, jnp.float32),
             jax.ShapeDtypeStruct((token_count, features), jnp.float32),
             jax.ShapeDtypeStruct((token_count, features), low),
@@ -1217,6 +1324,7 @@
         scratch_shapes=[
             pltpu.VMEM((experts, 3, 4 * (final << steps), hidden), low),
             pltpu.VMEM((count, token_count, features), low),
+            pltpu.VMEM((2, last, width), jnp.float32),
             pltpu.VMEM((token_count, 2 * features), low),
             pltpu.VMEM((token_count, features), low),
             pltpu.VMEM((token_count, features), low),
@@ -1254,6 +1362,11 @@
             dma((count,)),
             dma((count,)),
             dma((count,)),
+            dma((2, 3)),
+            dma((steps, 2)),
+            dma((steps, 2)),
+            dma((2,)),
+            dma((2,)),
         ],
         compiler_params=pltpu.CompilerParams(
             collective_id=2, has_side_effects=True, vmem_limit_bytes=63 * 1024 * 1024
@@ -1276,6 +1389,7 @@
         tables,
         starts[:, None],
         starts[None, :],
+        *moments,
     )
 
 
@@ -1286,10 +1400,6 @@
     key_weight,
     value_weight,
     out_weight,
-    query_moment,
-    key_moment,
-    value_moment,
-    out_moment,
     small_ref,
     tokens_ref,
     cot_ref,
@@ -1297,7 +1407,6 @@
     column_ref,
     row_ref,
     weights_hbm,
-    moments_hbm,
     small_out,
     cot_out,
     middle_out,
@@ -1308,9 +1417,7 @@
     head_out,
     total_out,
     weights_out,
-    moments_out,
     weights_ref,
-    moments_ref,
     local_sem,
     line_send,
     line_recv,
@@ -1329,12 +1436,9 @@
     core = rep % 2
     steps = len(bits)
     streams = range(2)
-    owns = (weights_ref, moments_ref)
-    fulls = (weights_out, moments_out)
     rows, width = weights_ref.shape[1:]
     half = width // 2
     fine = half // 4
-    groups = 2
     others = [lax.rem(me + k, count) for k in range(1, count)]
 
     def columns_of(start, size):
@@ -1347,20 +1451,12 @@
         return (rep // bit) % 2
 
     narrow = width // 2
-    for target, sources in (
-        (weights_ref, (query_weight, key_weight, value_weight, out_weight)),
-        (moments_ref, (query_moment, key_moment, value_moment, out_moment)),
-    ):
-        target[0] = sources[0][...].astype(target.dtype)
-        target[1, :, :narrow] = sources[1][...].astype(target.dtype)
-        target[1, :, narrow:] = sources[2][...].astype(target.dtype)
-        target[2] = sources[3][...].astype(target.dtype)
-    own_copies = [
-        pltpu.make_async_copy(weights_ref, weights_out.at[:, me], local_sem.at[0]),
-        pltpu.make_async_copy(moments_ref, moments_out.at[:, me], local_sem.at[1]),
-    ]
-    for own_copy in own_copies:
-        own_copy.start()
+    weights_ref[0] = query_weight[...]
+    weights_ref[1, :, :narrow] = key_weight[...]
+    weights_ref[1, :, narrow:] = value_weight[...]
+    weights_ref[2] = out_weight[...]
+    own_copy = pltpu.make_async_copy(weights_ref, weights_out.at[:, me], local_sem.at[0])
+    own_copy.start()
     small_out[me] = small_ref[...]
     cot_out[me] = cot_ref[...]
     peers = [(rep, other) for other in others]
@@ -1389,34 +1485,34 @@
             device_id_type=MESH,
         )
 
-    def line_copy(group, stream, source, peer):
+    def line_copy(stream, source, peer):
         place, columns = regions[stream][0][-1]
         return remote(
-            owns[group].at[:, place, columns],
-            fulls[group].at[:, source, place, columns],
-            line_send.at[group, stream, peer],
-            line_recv.at[group, stream, source],
+            weights_ref.at[:, place, columns],
+            weights_out.at[:, source, place, columns],
+            line_send.at[stream, peer],
+            line_recv.at[stream, source],
             (rep, peer),
         )
 
-    def grow_copy(step, group, stream, source):
+    def grow_copy(step, stream, source):
         place, columns = regions[stream][0][step]
-        part = fulls[group].at[:, source, place, columns]
+        part = weights_out.at[:, source, place, columns]
         return remote(
             part,
             part,
-            grow_send.at[step, group, stream, source],
-            grow_recv.at[step, group, stream, source],
+            grow_send.at[step, stream, source],
+            grow_recv.at[step, stream, source],
             (flip(rep, order(stream)[step]), me),
         )
 
-    def join_copy(group, stream, source):
-        part = fulls[group].at[:, source, :, regions[stream][1]]
+    def join_copy(stream, source):
+        part = weights_out.at[:, source, :, regions[stream][1]]
         return remote(
             part,
             part,
-            join_send.at[group, stream, source],
-            join_recv.at[group, stream, source],
+            join_send.at[stream, source],
+            join_recv.at[stream, source],
             (flip(rep, 1), me),
         )
 
@@ -1468,26 +1564,26 @@
             def _():
                 hand_on(jnp.minimum(upper, count - 1), False).start()
 
-    def line_send_group(group):
+    def line_send_all():
         for other in others:
             for stream in streams:
-                line_copy(group, stream, me, other).start()
-
-    def advance(level, group):
+                line_copy(stream, me, other).start()
+
+    def advance(level):
         for other in others:
             for stream in streams:
                 if level == 0:
-                    line_copy(group, stream, other, other).wait_recv()
+                    line_copy(stream, other, other).wait_recv()
                 else:
-                    grow_copy(steps - level, group, stream, other).wait_recv()
+                    grow_copy(steps - level, stream, other).wait_recv()
                 if level < steps:
-                    grow_copy(steps - 1 - level, group, stream, other).start()
+                    grow_copy(steps - 1 - level, stream, other).start()
                 else:
-                    join_copy(group, stream, other).start()
+                    join_copy(stream, other).start()
 
     for other in others:
         small_copy(me, other).start()
-    line_send_group(0)
+    line_send_all()
     for other in others:
         small_copy(other, other).wait_recv()
 
@@ -1497,16 +1593,16 @@
 
     inputs = tokens_ref[...].astype(jnp.float32)
     first_out[...] = (normalize(inputs)[0] * gain(0)).astype(jnp.bfloat16)
-    advance(0, 0)
-    line_send_group(1)
+    advance(0)
+    line_start()
     for level in range(1, steps + 1):
-        advance(level, 0)
-    advance(0, 1)
-    line_start()
+        advance(level)
+        if level == 1:
+            line_step(1)
     for other in others:
         for stream in streams:
-            join_copy(0, stream, other).wait_recv()
-    own_copies[0].wait()
+            join_copy(stream, other).wait_recv()
+    own_copy.wait()
     leave = pltpu.make_async_copy(weights_out, weights_hbm, local_sem.at[2])
     leave.start()
 
@@ -1515,38 +1611,23 @@
 
     project_inputs(first_out[...], whole, query_out, pair_out, table_ref)
     bias = allowed_pairs(column_ref[...], row_ref[...])
-    quarter = KVHEADS // 4
-    advance(1, 1)
-    attend_forward(range(2 * quarter), query_out, pair_out, bias, head_out, total_out)
-    line_step(1)
-    attend_forward(range(2 * quarter, KVHEADS), query_out, pair_out, bias, head_out, total_out)
-    for level in range(2, steps + 1):
-        advance(level, 1)
-    leaving = pltpu.make_async_copy(moments_out, moments_hbm, local_sem.at[3])
-
-    def moments_leave():
-        for other in others:
-            for stream in streams:
-                join_copy(1, stream, other).wait_recv()
-        own_copies[1].wait()
-        leaving.start()
-
+    if count > 2:
+        line_step(2)
+    attend_forward(range(KVHEADS // 2), query_out, pair_out, bias, head_out, total_out)
+    for step in range(3, count - 1):
+        line_step(step)
+    attend_forward(range(KVHEADS // 2, KVHEADS), query_out, pair_out, bias, head_out, total_out)
     middle = inputs + dot_nn(head_out[...], whole(2))
     middle_out[...] = middle
     second_out[...] = (normalize(middle)[0] * gain(1)).astype(jnp.bfloat16)
-    for step in range(2, count):
-        line_step(step)
-        if step == 2:
-            moments_leave()
-    if count < 3:
-        moments_leave()
-    for group in range(groups):
-        for other in others:
-            for stream in streams:
-                join_copy(group, stream, other).wait_send()
-                line_copy(group, stream, me, other).wait_send()
-                for step in range(steps):
-                    grow_copy(step, group, stream, other).wait_send()
+    if count > 3:
+        line_step(count - 1)
+    for other in others:
+        for stream in streams:
+            join_copy(stream, other).wait_send()
+            line_copy(stream, me, other).wait_send()
+            for step in range(steps):
+                grow_copy(step, stream, other).wait_send()
     for other in others:
         small_copy(me, other).wait_send()
     for block in range(count):
@@ -1560,10 +1641,9 @@
             hand_on(block, False).wait_send()
 
     leave.wait()
-    leaving.wait()
-
-
-def gather(weights, moments, small, tokens, cotangent, tables, starts, bits, count):
+
+
+def gather(weights, small, tokens, cotangent, tables, starts, bits, count):
     rows, width = weights[0].shape
     depth = 3
     token_count = tokens.shape[0]
@@ -1575,10 +1655,9 @@
     features = jax.ShapeDtypeStruct((token_count, width), low)
     return pl.pallas_call(
         functools.partial(gather_kernel, count, bits),
-        in_specs=[vmem] * 14,
-        out_specs=[pl.BlockSpec(memory_space=pl.ANY)] * 2 + [vmem] * 9,
+        in_specs=[vmem] * 10,
+        out_specs=[pl.BlockSpec(memory_space=pl.ANY)] + [vmem] * 9,
         out_shape=[
-            whole,
             whole,
             jax.ShapeDtypeStruct((count,) + small.shape, small.dtype),
             jax.ShapeDtypeStruct((count, token_count, width), low),
@@ -1592,16 +1671,14 @@
         ],
         scratch_shapes=[
             pltpu.VMEM(whole.shape, low),
-            pltpu.VMEM(whole.shape, low),
             pltpu.VMEM((depth, rows, width), low),
-            pltpu.VMEM((depth, rows, width), low),
-            dma((4,)),
-            dma((2, 2, count)),
-            dma((2, 2, count)),
-            dma((steps, 2, 2, count)),
-            dma((steps, 2, 2, count)),
-            dma((2, 2, count)),
-            dma((2, 2, count)),
+            dma((3,)),
+            dma((2, count)),
+            dma((2, count)),
+            dma((steps, 2, count)),
+            dma((steps, 2, count)),
+            dma((2, count)),
+            dma((2, count)),
             dma((count,)),
             dma((count,)),
             dma((count,)),
@@ -1614,7 +1691,6 @@
         name="gather",
     )(
         *weights,
-        *moments,
         small,
         tokens,
         cotangent,
@@ -1670,7 +1746,6 @@
     tables = rotary_tables(jnp.arange(tokens.shape[0], dtype=jnp.int32) - sequence_start)
     (
         weights,
-        moments,
         small,
         cotangent_all,
         middle,
@@ -1682,7 +1757,6 @@
         log_total,
     ) = gather(
         (query_proj, key_proj, value_proj, out_proj),
-        (query_moment, key_moment, value_moment, out_moment),
         jnp.concatenate([dense_weights, gain_rows], axis=0),
         tokens,
         cotangent,
@@ -1704,7 +1778,8 @@
         bits,
         shard_count,
     )
-    expert_grads, dense_grads, gains_grad, grad_tokens, mixed = spread(
+    own_moments = (query_moment, key_moment, value_moment, out_moment)
+    expert_grads, dense_next, dense_grads, gains_grad, grad_tokens, mixed = spread(
         expert_share,
         returned,
         normed_first,
@@ -1720,6 +1795,7 @@
         log_total,
         tables,
         sequence_start,
+        own_moments,
         bits=bits,
         count=shard_count,
     )
@@ -1743,9 +1819,9 @@
         own_wide,
         own_narrow,
     ) = dense_update(
+        dense_next,
         dense_grads,
-        moments,
-        (query_moment, key_moment, value_moment, out_moment),
+        own_moments,
         LAYOUT,
         shard_index,
         rep_index,

time: 421 us -> 404 us (0.960)
  Pallas kernels: 395 us -> 378 us
    pallas_call x1, Pallas kernels: 87 us -> 67.1 us  [gather(): pl.pallas_call(functools.partial(gather_kernel, count, bits), in_specs=[v...]
where the time goes in v4:
time: 404 us; the launch traced here: 398 us
  Pallas kernels  378 us (94%)
  other arithmetic  9.24 us (2%)
  local copies, waits for them, and re-layouts  8.59 us (2%)
    pallas_call x1, Pallas kernels, spread(): pl.pallas_call(functools.partial(spread_kernel, count, bits), in_specs=[v...  130 us
    pallas_call x1, Pallas kernels, moe(): pl.pallas_call(functools.partial(moe_kernel, count, bits), in_specs=[vmem...  110 us
    pallas_call x1, Pallas kernels, gather(): pl.pallas_call(functools.partial(gather_kernel, count, bits), in_specs=[v...  67.1 us
    pallas_call x2, Pallas kernels, expert_update(): pl.pallas_call(functools.partial(expert_update_kernel, kinds, scale), gri...  49.1 us
    pallas_call x1, Pallas kernels, dense_update(): pl.pallas_call(functools.partial(dense_update_kernel, layout), grid=(1,),...  22.8 us
  transfers between devices with their start and end apart: 2, of which 0 were waited for; matrix products, arithmetic and copies ran while one was open for 1% of the time, Pallas kernels for 12%

profile of v4, /device:TPU:0, one launch (start us, length us, event | category | flops | bytes accessed | tf_op | source)
XLA Modules:
  0.0 397.8 jit_solution(1063948772347716835)
XLA Ops:
  0.7 0.7 subtract_convert_fusion
  1.4 1.5 copy.56.column_ref
  2.9 0.7 stack.30
  3.5 0.7 stack.31
  4.2 0.5 multiply_cosine_fusion
  4.7 0.8 select_reduce_fusion
  5.5 0.6 pad_maximum_fusion.1.small_ref
  6.1 0.4 maximum_bitcast_fusion.1
  6.5 0.8 pad_maximum_fusion.table_ref
  7.3 67.1 %gather.1 = (bf16[3,4,256,1024]{3,2,1,0:T(8,128)(2,1)}, f32[4,24,256]{2,1,0:T(8,128)}, bf16[4,256,1024]{2,1,0:T(8,128)(2,1)}, f32[256,1024]{1,0:T(8,128)}, bf16[...) custom-call(bf16[256,1024]{1,0:T(8,128)(2,1)} %query_weight.1, ...), custom_call_target="tpu_custom_call" | custom-call | tf_op jit(solution)/shard_map/gather/pallas_call | solution.py:1656
  74.4 1.1 copy.57
  75.5 1.0 dynamic-slice_bitcast_fusion.weight_ref
  76.5 0.6 pad_add_fusion.place_ref
  77.0 110.0 %moe.1 = (bf16[4,256,1024]{2,1,0:T(8,128)(2,1)}, f32[256,1024]{1,0:T(8,128)}, bf16[4,3,2,64,512]{4,3,2,1,0:T(8,128)(2,1)}) custom-call(bf16[256,1024]{1,0:T(8,128)(2,1)} %get-tuple-element.67.own_ref, bf16[4,256,1024]{2,1,0:T(8,128)(2,1)} %get-tuple-element.68.cot_ref, f32[4,256,4]{2,1,0:T(8,128)} %dynamic-slice_bitcast_fusion.weight_ref, ...), custom_call_target="tpu_custom_call" | custom-call | flops 38999998464 | bytes 20000000 | tf_op jit(solution)/shard_map/moe/pallas_call | solution.py:707
  187.0 129.5 %spread.1 = (bf16[4,3,1024,512]{3,2,1,0:T(8,128)(2,1)}, bf16[8,4,256,384]{3,2,1,0:T(8,128)(2,1)}, bf16[8,256,384]{2,1,0:T(8,128)(2,1)}, f32[8,1024]{1,0:T(8,128)...) custom-call(bf16[4,3,2,64,512]{4,3,2,1,0:T(8,128)(2,1)} %get-tuple-element.70.share_ref, ...), custom_call_target="tpu_custom_call" | custom-call | tf_op jit(solution)/shard_map/spread/pallas_call | solution.py:1312
  316.5 22.8 %dense_update.1 = (f32[256,1024]{1,0:T(8,128)}, f32[256,1024]{1,0:T(8,128)}, f32[256,512]{1,0:T(8,128)}, f32[256,512]{1,0:T(8,128)}, f32[256,512]{1,0:T(8,128)},...) custom-call(s32[2]{0:T(128)} %pad_add_fusion.place_ref, ...), custom_call_target="tpu_custom_call" | custom-call | flops 14000000000 | bytes 25165824 | tf_op jit(solution)/shard_map/dense_update/pallas_call | solution.py:340
  339.3 0.4 collective-permute-start.1
  339.7 0.1 collective-permute-start
  339.8 31.3 %expert_update.2 = (f32[4,1024,512]{2,1,0:T(8,128)}, f32[4,1024,512]{2,1,0:T(8,128)}, f32[4,1024,512]{2,1,0:T(8,128)}, f32[4,1024,512]{2,1,0:T(8,128)}, f32[4,10...) custom-call(bf16[4,3,1024,512]{3,2,1,0:T(8,128)(2,1)} %get-tuple-element.95.refs_0_, f32[4,1024,512]{2,1,0:T(8,128)} %refs_1_.4, ...), custom_call_target="tpu_custom_call" | custom-call | flops 20000000000 | bytes 75497472 | tf_op jit(solution)/shard_map/expert_update/pallas_call | solution.py:255
  371.2 0.0 copy-start.4
  371.2 0.0 copy-start.5
  371.2 0.0 copy-start
  371.2 0.0 copy-start.1
  371.2 17.8 %expert_update.3 = (f32[4,512,1024]{2,1,0:T(8,128)}, f32[4,512,1024]{2,1,0:T(8,128)}, f32[4,512,1024]{2,1,0:T(8,128)}) custom-call(bf16[4,3,1024,512]{3,2,1,0:T(8,128)(2,1)} %get-tuple-element.95.refs_0_, f32[4,512,1024]{2,1,0:T(8,128)} %refs_1_.5), custom_call_target="tpu_custom_call" | custom-call | flops 10000000000 | bytes 37748736 | tf_op jit(solution)/shard_map/expert_update/pallas_call | solution.py:255
  389.0 0.8 fusion.5
  389.8 0.0 copy-start.2
  389.8 0.0 copy-start.3
  389.8 0.0 copy-done.4
  389.8 0.6 broadcast_multiply_fusion.1
  390.4 0.0 copy-done.5
  390.4 0.6 broadcast_multiply_fusion
  391.0 0.0 collective-permute-done.1
  391.0 2.3 broadcast_select_fusion.2
  393.2 0.0 collective-permute-done
  393.3 0.0 copy-done
  393.3 1.5 broadcast_select_fusion
  394.7 1.9 copy.61
  396.6 0.0 copy-done.1
  396.6 1.0 copy.62
  397.6 0.0 copy-done.2
  397.6 0.0 copy-done.3
  (3 shorter events, 0.0 us)
Async XLA Ops:
  339.3 51.6 %collective-permute-start.1 = (f32[256,512]{1,0:T(8,128)}, f32[256,512]{1,0:T(8,128)}, u32[]{:S(2)}, u32[]{:S(2)}) collective-permute-start(f32[256,512]{1,0:T(8,128)} %get-tuple-element.89), channel_id=1, source_target_pairs={{0,4},{4,0},{8,12},{12,8},{16,20},{20,16},{24,28},{28,24},{1,5},{5... | collective-permute-start | bytes 1572872 | tf_op jit(solution)/shard_map/ppermute | solution.py:1831
  339.7 53.5 %collective-permute-start = (f32[256,1024]{1,0:T(8,128)}, f32[256,1024]{1,0:T(8,128)S(1)}, u32[]{:S(2)}, u32[]{:S(2)}) collective-permute-start(f32[256,1024]{1,0:T(8,128)} %get-tuple-element.86), channel_id=1, source_target_pairs={{0,4},{4,0},{8,12},{12,8},{16,20},{20,16},{24,28},{28,24},{1,5},{5... | collective-permute-start | bytes 3145736 | tf_op jit(solution)/shard_map/ppermute | solution.py:1830
  371.2 18.7 %copy-start.4 = (f32[256]{0:T(256)S(1)}, f32[256]{0:T(256)}, u32[]{:S(2)}) copy-start(f32[256]{0:T(256)} %param.41) | copy-start | bytes 3076
  371.2 19.2 %copy-start.5 = (f32[256]{0:T(256)S(1)}, f32[256]{0:T(256)}, u32[]{:S(2)}) copy-start(f32[256]{0:T(256)} %param.42) | copy-start | bytes 3076
  371.2 22.1 %copy-start = (f32[256,1024]{1,0:T(8,128)S(1)}, f32[256,1024]{1,0:T(8,128)}, u32[]{:S(2)}) copy-start(f32[256,1024]{1,0:T(8,128)} %get-tuple-element.86) | copy-start | bytes 3145732
  371.2 25.4 %copy-start.1 = (f32[256,1024]{1,0:T(8,128)S(1)}, f32[256,1024]{1,0:T(8,128)}, u32[]{:S(2)}) copy-start(f32[256,1024]{1,0:T(8,128)} %get-tuple-element.151) | copy-start | bytes 3145732
  389.8 7.8 %copy-start.2 = (f32[1,256]{1,0:T(1,128)}, f32[1,256]{1,0:T(1,128)S(1)}, u32[]{:S(2)}) copy-start(f32[1,256]{1,0:T(1,128)S(1)} %get-tuple-element.115) | copy-start | bytes 3076
  389.8 7.8 %copy-start.3 = (f32[1,256]{1,0:T(1,128)}, f32[1,256]{1,0:T(1,128)S(1)}, u32[]{:S(2)}) copy-start(f32[1,256]{1,0:T(1,128)S(1)} %get-tuple-element.116) | copy-start | bytes 3076

commit v5 on v4

--- a/solution.py
+++ b/solution.py
@@ -133,9 +133,11 @@
         total_ref[:, block : block + 1] = row_max + jnp.log(totals)
 
 
-def attend_backward(query_ref, pair_ref, bias, total_ref, grad_ref, table_ref, delta_ref):
+def attend_backward(
+    blocks, query_ref, pair_ref, bias, total_ref, grad_ref, table_ref, delta_ref
+):
     folded = []
-    for block in range(KVHEADS):
+    for block in blocks:
         queries, key, value, scores = attend_pair(block, query_ref, pair_ref, bias)
         grads = stacked(block_lanes(grad_ref, block))
         softmax_full = jnp.exp(scores - total_ref[:, block : block + 1])
@@ -904,15 +906,6 @@
             (rep, peer),
         )
 
-    def core_copy(block):
-        return remote(
-            dense_ref.at[4 * (1 - core) + block],
-            land_core.at[block],
-            core_send.at[block],
-            core_recv.at[block],
-            across(1),
-        )
-
     gain_bits = (1,) + bits
 
     def gain_copy(stage):
@@ -924,11 +917,11 @@
             across(gain_bits[stage]),
         )
 
-    for stream in streams:
-        expert_copy(0, stream).start()
-
-    for k in range(1, count):
-        returning(lax.rem(me + k, count), me).start()
+    def gain_step(stage):
+        gain_copy(stage).wait_recv()
+        gains_send[stage + 1] = gains_send[stage] + gains_land[stage]
+        if stage + 1 < len(gain_bits):
+            gain_copy(stage + 1).start()
 
     def whole(index):
         return weights_ref[index].reshape(count * rows, -1)
@@ -936,71 +929,326 @@
     def gain(index):
         at = EXPERTS + index
         return jnp.concatenate([small_ref[z, at : at + 1, :rows] for z in range(count)], axis=1)
+
+    part = dense_ref.shape[3] // 3
+    chunks = (pl.ds(2 * part, part), pl.ds(0, 2 * part))
+    chunk_parts = ((2,), (0, 1))
+    inner = [slice(index * part, (index + 1) * part) for index in range(3)]
+    first = [side(order(stream)[0]) for stream in streams]
+    held = [2 * stream + first[stream] for stream in streams]
+    given = [2 * stream + 1 - first[stream] for stream in streams]
+
+    starts = []
+    for stream in streams:
+        start, size, line = 0, rows, []
+        for step in range(1, steps):
+            size = size // 2
+            near = side(order(stream)[step])
+            line.append((start + near * size, start + (1 - near) * size, size))
+            start = start + near * size
+        starts.append((start, size, line))
+    last = starts[0][1]
+    places = [rows_of(starts[stream][0], last) for stream in streams]
+    others = [lax.rem(me + k, count) for k in range(1, count)]
+
+    def moment_copy(stream, index):
+        block = 4 * core + held[stream]
+        lanes = pl.ds(pl.multiple_of((held[stream] if index == 1 else block) * part, part), part)
+        source = (query_moment, key_moment, out_moment)[index]
+        return pltpu.make_async_copy(
+            source.at[places[stream], lanes],
+            moment_piece.at[stream, :, inner[index]],
+            moment_sem.at[stream, index],
+        )
+
+    def moment_other(stream):
+        lanes = pl.ds(pl.multiple_of(held[stream] * part, part), part)
+        return pltpu.make_async_copy(
+            value_moment.at[places[stream], lanes],
+            moment_piece.at[stream, :, inner[1]],
+            moment_sem.at[stream, 1],
+        )
+
+    def columns(ref, offset, block):
+        return ref[:, pl.ds(pl.multiple_of(offset + block * part, part), part)]
+
+    def make_block(chunk, block, turned):
+        if chunk == 0:
+            values = dot_nn(turned, columns(branch_ref, 0, block))
+        else:
+            values = dot_nn(
+                turned,
+                jnp.concatenate(
+                    [columns(delta_ref, 0, block), columns(delta_ref, 8 * part, block)], axis=1
+                ),
+            )
+        for line in range(count):
+            dense_ref[block, line, :, chunks[chunk]] = values[
+                line * rows : (line + 1) * rows
+            ].astype(jnp.bfloat16)
+
+    def core_copy(chunk, block):
+        return remote(
+            dense_ref.at[4 * (1 - core) + block, :, :, chunks[chunk]],
+            land_core.at[block, :, :, chunks[chunk]],
+            core_send.at[chunk, block],
+            core_recv.at[chunk, block],
+            across(1),
+        )
+
+    def first_copy(chunk, stream):
+        return remote(
+            total.at[given[stream], :, :, chunks[chunk]],
+            land_first.at[stream, :, :, chunks[chunk]],
+            half_send.at[chunk, 0, stream],
+            half_recv.at[chunk, 0, stream],
+            across(order(stream)[0]),
+        )
+
+    def later_copy(chunk, step, stream):
+        _, send, size = starts[stream][2][step - 1]
+        return remote(
+            total.at[held[stream], :, rows_of(send, size), chunks[chunk]],
+            land_later[step - 1].at[stream, :, :, chunks[chunk]],
+            half_send.at[chunk, step, stream],
+            half_recv.at[chunk, step, stream],
+            across(order(stream)[step]),
+        )
+
+    def shard_copy(chunk, source, peer):
+        return remote(
+            piece_send.at[peer, :, :, chunks[chunk]],
+            piece_land.at[source, :, :, chunks[chunk]],
+            shard_send.at[chunk, peer],
+            shard_recv.at[chunk, source],
+            (rep, peer),
+        )
+
+    def line_copy(chunk, stream, source, peer):
+        return remote(
+            piece.at[stream, :, chunks[chunk]],
+            dense_out.at[4 * core + held[stream], source, places[stream], chunks[chunk]],
+            line_send.at[chunk, stream, peer],
+            line_recv.at[chunk, stream, source],
+            (rep, peer),
+        )
+
+    def own_piece(chunk, stream):
+        return pltpu.make_async_copy(
+            piece.at[stream, :, chunks[chunk]],
+            dense_out.at[4 * core + held[stream], me, places[stream], chunks[chunk]],
+            local_sem.at[2 + 2 * chunk + stream],
+        )
+
+    def region(step, stream):
+        if step == 0:
+            return pl.ds(0, rows)
+        keep, _, size = starts[stream][2][step - 1]
+        return rows_of(keep, size)
+
+    def grow_copy(chunk, step, stream):
+        place = dense_out.at[
+            4 * core + held[stream], :, region(step, stream), chunks[chunk]
+        ]
+        return remote(
+            place,
+            place,
+            grow_send.at[chunk, step, stream],
+            grow_recv.at[chunk, step, stream],
+            across(order(stream)[step]),
+        )
+
+    def own_grow(chunk, step, stream):
+        place = grads_out.at[4 * core + held[stream], region(step, stream), chunks[chunk]]
+        return remote(
+            place,
+            place,
+            own_send.at[chunk, step, stream],
+            own_recv.at[chunk, step, stream],
+            across(order(stream)[step]),
+        )
+
+    def join_copy(chunk, stream):
+        place = dense_out.at[pl.ds(4 * core + 2 * stream, 2), :, :, chunks[chunk]]
+        return remote(
+            place, place, join_send.at[chunk, stream], join_recv.at[chunk, stream], across(1)
+        )
+
+    def own_join(chunk, stream):
+        place = grads_out.at[pl.ds(4 * core + 2 * stream, 2), :, chunks[chunk]]
+        return remote(
+            place,
+            place,
+            own_join_send.at[chunk, stream],
+            own_join_recv.at[chunk, stream],
+            across(1),
+        )
+
+    def add_into(block, line, place, lanes, one, two):
+        total[block, line, place, lanes] = (
+            one.astype(jnp.float32) + two.astype(jnp.float32)
+        ).astype(jnp.bfloat16)
+
+    def chain(chunk):
+        lanes = chunks[chunk]
+        turned = (head_ref if chunk == 0 else normed_ref)[...].T
+        every = pl.ds(0, rows)
+        for block in range(4):
+            make_block(chunk, 4 * (1 - core) + block, turned)
+            core_copy(chunk, block).start()
+        for block in range(4):
+            make_block(chunk, 4 * core + block, turned)
+        yield
+
+        def add_core(block):
+            for line in range(count):
+                add_into(
+                    block,
+                    line,
+                    every,
+                    lanes,
+                    dense_ref[4 * core + block, line, :, lanes],
+                    land_core[block, line, :, lanes],
+                )
+
+        for block in range(4):
+            core_copy(chunk, block).wait_recv()
+        for stream in streams:
+            add_core(given[stream])
+            first_copy(chunk, stream).start()
+        for stream in streams:
+            add_core(held[stream])
+        yield
+        for stream in streams:
+            first_copy(chunk, stream).wait_recv()
+            for line in range(count):
+                add_into(
+                    held[stream],
+                    line,
+                    every,
+                    lanes,
+                    total[held[stream], line, :, lanes],
+                    land_first[stream, line, :, lanes],
+                )
+            if steps > 1:
+                later_copy(chunk, 1, stream).start()
+        yield
+        for step in range(1, steps):
+            for stream in streams:
+                later_copy(chunk, step, stream).wait_recv()
+                place = region(step, stream)
+                for line in range(count):
+                    add_into(
+                        held[stream],
+                        line,
+                        place,
+                        lanes,
+                        total[held[stream], line, place, lanes],
+                        land_later[step - 1][stream, line, :, lanes],
+                    )
+                if step + 1 < steps:
+                    later_copy(chunk, step + 1, stream).start()
+            if step + 1 < steps:
+                yield
+        for stream in streams:
+            for line in range(count):
+                piece_send[line, stream, :, lanes] = total[
+                    held[stream], line, places[stream], lanes
+                ]
+        for other in others:
+            shard_copy(chunk, me, other).start()
+        yield
+        summed = piece_send[me, :, :, lanes].astype(jnp.float32)
+        for other in others:
+            shard_copy(chunk, other, other).wait_recv()
+            summed = summed + piece_land[other, :, :, lanes].astype(jnp.float32)
+        for stream in streams:
+            for index in chunk_parts[chunk]:
+                moment_copy(stream, index).wait()
+            grads_out[4 * core + held[stream], places[stream], lanes] = summed[stream].astype(
+                jnp.bfloat16
+            )
+            own_grow(chunk, steps - 1, stream).start()
+        piece[:, :, lanes] = (momentum_keep * moment_piece[:, :, lanes] + summed).astype(
+            jnp.bfloat16
+        )
+        for stream in streams:
+            own_piece(chunk, stream).start()
+            for other in others:
+                line_copy(chunk, stream, me, other).start()
+        yield
+        for stream in streams:
+            own_piece(chunk, stream).wait()
+            for other in others:
+                line_copy(chunk, stream, other, other).wait_recv()
+            grow_copy(chunk, steps - 1, stream).start()
+        yield
+        for step in reversed(range(steps)):
+            for stream in streams:
+                grow_copy(chunk, step, stream).wait_recv()
+                own_grow(chunk, step, stream).wait_recv()
+                if step > 0:
+                    grow_copy(chunk, step - 1, stream).start()
+                    own_grow(chunk, step - 1, stream).start()
+                else:
+                    join_copy(chunk, stream).start()
+                    own_join(chunk, stream).start()
+            yield
+        for stream in streams:
+            join_copy(chunk, stream).wait()
+            own_join(chunk, stream).wait()
+
+    early, late = chain(0), chain(1)
+
+    def go(steps_of):
+        next(steps_of, None)
+
+    for stream in streams:
+        moment_copy(stream, 0).start()
+        moment_copy(stream, 2).start()
+
+        @pl.when(core == 0)
+        def _():
+            moment_copy(stream, 1).start()
+
+        @pl.when(core == 1)
+        def _():
+            moment_other(stream).start()
 
     scaled, inverse = normalize(middle_ref[...])
     middle_extra, midnorm_part = normalize_back(second_ref[...], gain(1), scaled, inverse)
     grad_middle = cot_ref[...].astype(jnp.float32) + middle_extra
     tokens_out[...] = grad_middle
     branch_ref[...] = grad_middle.astype(jnp.bfloat16)
+    go(early)
+    for stream in streams:
+        expert_copy(0, stream).start()
+    for other in others:
+        returning(other, me).start()
     heads_ref[...] = dot_nt(branch_ref[...], whole(2)).astype(jnp.bfloat16)
     bias = allowed_pairs(column_ref[...], row_ref[...])
-    attend_backward(query_ref, pair_ref, bias, total_ref, heads_ref, table_ref, delta_ref)
-
-    part = dense_ref.shape[3] // 3
-    normed_turned = normed_ref[...].T
-    head_turned = head_ref[...].T
-
-    def make_block(block):
-        def columns(ref, offset):
-            return ref[:, pl.ds(pl.multiple_of(offset + block * part, part), part)]
-
-        pair = jnp.concatenate([columns(delta_ref, 0), columns(delta_ref, 8 * part)], axis=1)
-        left = jnp.dot(normed_turned, pair, preferred_element_type=jnp.float32)
-        right = jnp.dot(head_turned, columns(branch_ref, 0), preferred_element_type=jnp.float32)
-        for line in range(count):
-            place = slice(line * rows, (line + 1) * rows)
-            dense_ref[block, line, :, : 2 * part] = left[place].astype(jnp.bfloat16)
-            dense_ref[block, line, :, 2 * part :] = right[place].astype(jnp.bfloat16)
-
-    for block in range(4):
-        make_block(4 * (1 - core) + block)
-        core_copy(block).start()
-    for block in range(4):
-        make_block(4 * core + block)
-
-    def gain_step(stage):
-        gain_copy(stage).wait_recv()
-        gains_send[stage + 1] = gains_send[stage] + gains_land[stage]
-        if stage + 1 < len(gain_bits):
-            gain_copy(stage + 1).start()
-
-    first = [side(order(stream)[0]) for stream in streams]
-    held = [2 * stream + first[stream] for stream in streams]
-    given = [2 * stream + 1 - first[stream] for stream in streams]
-
-    def first_copy(stream):
-        return remote(
-            total.at[given[stream]],
-            land_first.at[stream],
-            half_send.at[0, stream],
-            half_recv.at[0, stream],
-            across(order(stream)[0]),
-        )
-
-    def add_core(block):
-        for line in range(count):
-            total[block, line] = (
-                dense_ref[4 * core + block, line].astype(jnp.float32)
-                + land_core[block, line].astype(jnp.float32)
-            ).astype(jnp.bfloat16)
-
-    for block in range(4):
-        core_copy(block).wait_recv()
-    for stream in streams:
-        add_core(given[stream])
-        first_copy(stream).start()
-    for stream in streams:
-        add_core(held[stream])
+
+    def backward(begin, end):
+        attend_backward(
+            range(begin, end),
+            query_ref,
+            pair_ref,
+            bias,
+            total_ref,
+            heads_ref,
+            table_ref,
+            delta_ref,
+        )
+
+    quarter = KVHEADS // 4
+    backward(0, quarter)
+    go(early)
+    backward(quarter, 3 * quarter)
+    go(early)
+    backward(3 * quarter, KVHEADS)
+    go(late)
+    go(early)
+    go(late)
     grad_first = dot_nt(delta_ref[:, : NHEADS * HEAD], whole(0)) + dot_nt(
         delta_ref[:, NHEADS * HEAD :], whole(1)
     )
@@ -1011,286 +1259,80 @@
         [prenorm_part, midnorm_part, jnp.zeros((6, prenorm_part.shape[1]), jnp.float32)], axis=0
     )
     gain_copy(0).start()
+    go(early)
     gain_step(0)
-
-    starts = []
-    for stream in streams:
-        start, size, line = 0, rows, []
-        for step in range(1, steps):
-            size = size // 2
-            near = side(order(stream)[step])
-            line.append((start + near * size, start + (1 - near) * size, size))
-            start = start + near * size
-        starts.append((start, size, line))
-
-    last = starts[0][1]
-    places = [rows_of(starts[stream][0], last) for stream in streams]
-    inner = [slice(index * part, (index + 1) * part) for index in range(3)]
-
-    def moment_copy(stream, index):
-        block = 4 * core + held[stream]
-        lanes = pl.ds(pl.multiple_of((held[stream] if index == 1 else block) * part, part), part)
-        source = (query_moment, key_moment, out_moment)[index]
-        return pltpu.make_async_copy(
-            source.at[places[stream], lanes],
-            moment_piece.at[stream, :, inner[index]],
-            moment_sem.at[stream, index],
-        )
-
-    def moment_other(stream):
-        lanes = pl.ds(pl.multiple_of(held[stream] * part, part), part)
-        return pltpu.make_async_copy(
-            value_moment.at[places[stream], lanes],
-            moment_piece.at[stream, :, inner[1]],
-            moment_sem.at[stream, 1],
-        )
-
-    for stream in streams:
-        moment_copy(stream, 0).start()
-        moment_copy(stream, 2).start()
-
-        @pl.when(core == 0)
-        def _():
-            moment_copy(stream, 1).start()
-
-        @pl.when(core == 1)
-        def _():
-            moment_other(stream).start()
-
-    def later_copy(step, stream):
-        keep, send, size = starts[stream][2][step - 1]
-        return remote(
-            total.at[held[stream], :, rows_of(send, size)],
-            land_later[step - 1].at[stream],
-            half_send.at[step, stream],
-            half_recv.at[step, stream],
-            across(order(stream)[step]),
-        )
-
-    for stream in streams:
-        first_copy(stream).wait_recv()
-        for line in range(count):
-            total[held[stream], line] = (
-                total[held[stream], line].astype(jnp.float32)
-                + land_first[stream, line].astype(jnp.float32)
-            ).astype(jnp.bfloat16)
-        if steps > 1:
-            later_copy(1, stream).start()
-    gain_step(1)
-
-    for step in range(1, steps):
-        for stream in streams:
-            later_copy(step, stream).wait_recv()
-            keep, _, size = starts[stream][2][step - 1]
-            for line in range(count):
-                place = rows_of(keep, size)
-                total[held[stream], line, place] = (
-                    total[held[stream], line, place].astype(jnp.float32)
-                    + land_later[step - 1][stream, line].astype(jnp.float32)
-                ).astype(jnp.bfloat16)
-            if step + 1 < steps:
-                later_copy(step + 1, stream).start()
-        gain_step(step + 1)
-
+    go(late)
+    go(early)
     for stream in streams:
         own_copy(stream).wait()
         expert_copy(0, stream).wait_recv()
-        if steps > 1:
-            expert_copy(1, stream).start()
-
-    for stream in streams:
-        for line in range(count):
-            piece_send[line, stream] = total[held[stream], line, places[stream]]
-
-    def shard_copy(k):
-        target = lax.rem(me + k, count)
-        return remote(
-            piece_send.at[target],
-            piece_land.at[me],
-            shard_send.at[target],
-            shard_recv.at[me],
-            (rep, target),
-        )
-
-    def shard_arrival(source):
-        return remote(
-            piece_send.at[source],
-            piece_land.at[source],
-            shard_send.at[source],
-            shard_recv.at[source],
-            (rep, source),
-        )
-
-    def gain_line(k):
-        target = lax.rem(me + k, count)
-        return remote(
-            gains_send.at[len(gain_bits)],
-            gains_all.at[me],
-            gain_line_send.at[target],
-            gain_line_recv.at[me],
-            (rep, target),
-        )
-
-    def gain_arrival(source):
+        expert_copy(1, stream).start()
+    gain_step(1)
+    go(late)
+    for stage in range(2, len(gain_bits)):
+        gain_step(stage)
+
+    def gain_line(source, peer):
         return remote(
             gains_send.at[len(gain_bits)],
             gains_all.at[source],
-            gain_line_send.at[source],
+            gain_line_send.at[peer],
             gain_line_recv.at[source],
-            (rep, source),
-        )
-
-    def own_grow(step, stream):
-        block = 4 * core + held[stream]
-        if step == 0:
-            part_ref = grads_out.at[block]
-        else:
-            keep, _, size = starts[stream][2][step - 1]
-            part_ref = grads_out.at[block, rows_of(keep, size)]
-        return remote(
-            part_ref,
-            part_ref,
-            own_send.at[step, stream],
-            own_recv.at[step, stream],
-            across(order(stream)[step]),
-        )
-
-    def own_join(stream):
-        part_ref = grads_out.at[pl.ds(4 * core + 2 * stream, 2)]
-        return remote(
-            part_ref, part_ref, own_join_send.at[stream], own_join_recv.at[stream], across(1)
-        )
-
-    for k in range(1, count):
-        shard_copy(k).start()
-        gain_line(k).start()
-    summed = piece_send[me].astype(jnp.float32)
-    for k in range(1, count):
-        source = lax.rem(me + k, count)
-        shard_arrival(source).wait_recv()
-        summed = summed + piece_land[source].astype(jnp.float32)
-    for stream in streams:
-        for index in range(3):
-            moment_copy(stream, index).wait()
-        grads_out[4 * core + held[stream], places[stream]] = summed[stream].astype(jnp.bfloat16)
-        own_grow(steps - 1, stream).start()
-    piece[...] = (momentum_keep * moment_piece[...] + summed).astype(jnp.bfloat16)
-
-    def line_copy(k, stream):
-        target = lax.rem(me + k, count)
-        return remote(
-            piece.at[stream],
-            dense_out.at[4 * core + held[stream], me, places[stream]],
-            line_send.at[stream, target],
-            line_recv.at[stream, me],
-            (rep, target),
-        )
-
-    def line_arrival(source, stream):
-        return remote(
-            piece.at[stream],
-            dense_out.at[4 * core + held[stream], source, places[stream]],
-            line_send.at[stream, source],
-            line_recv.at[stream, source],
-            (rep, source),
-        )
-
-    def own_piece(stream):
-        return pltpu.make_async_copy(
-            piece.at[stream],
-            dense_out.at[4 * core + held[stream], me, places[stream]],
-            local_sem.at[2 + stream],
-        )
-
-    for stream in streams:
-        own_piece(stream).start()
-        for k in range(1, count):
-            line_copy(k, stream).start()
+            (rep, peer),
+        )
+
+    for other in others:
+        gain_line(me, other).start()
+    go(early)
+    go(late)
+    go(early)
     gained = gains_send[len(gain_bits)]
-    for k in range(1, count):
-        source = lax.rem(me + k, count)
-        gain_arrival(source).wait_recv()
-        gained = gained + gains_all[source]
+    for other in others:
+        gain_line(other, other).wait_recv()
+        gained = gained + gains_all[other]
     gains_out[...] = gained
-
+    mixed = middle_ref[...] + returned_ref[me].astype(jnp.float32)
+    for other in others:
+        returning(other, other).wait_recv()
+        mixed = mixed + got_ref[other].astype(jnp.float32)
+    mixed_out[...] = mixed.astype(mixed_out.dtype)
+    go(late)
     for level in range(1, steps):
         for stream in streams:
             expert_copy(level, stream).wait_recv()
             expert_copy(level + 1, stream).start()
-    if steps == 1:
-        for stream in streams:
-            expert_copy(1, stream).start()
-
-    def grow_copy(step, stream):
-        if step == 0:
-            place = dense_out.at[4 * core + held[stream]]
-        else:
-            keep, _, size = starts[stream][2][step - 1]
-            place = dense_out.at[4 * core + held[stream], :, rows_of(keep, size)]
-        return remote(
-            place,
-            place,
-            grow_send.at[step, stream],
-            grow_recv.at[step, stream],
-            across(order(stream)[step]),
-        )
-
-    for stream in streams:
-        own_piece(stream).wait()
-        for k in range(1, count):
-            line_arrival(lax.rem(me + k, count), stream).wait_recv()
-        grow_copy(steps - 1, stream).start()
-    for step in reversed(range(steps)):
-        for stream in streams:
-            own_grow(step, stream).wait_recv()
-            if step > 0:
-                own_grow(step - 1, stream).start()
-            else:
-                own_join(stream).start()
-    mixed = middle_ref[...] + returned_ref[me].astype(jnp.float32)
-    for k in range(1, count):
-        source = lax.rem(me + k, count)
-        returning(source, source).wait_recv()
-        mixed = mixed + got_ref[source].astype(jnp.float32)
-    mixed_out[...] = mixed.astype(mixed_out.dtype)
+    go(late)
     for stream in streams:
         expert_copy(steps, stream).wait()
     leave = pltpu.make_async_copy(experts_out, experts_hbm, local_sem.at[0])
     leave.start()
-    for step in reversed(range(steps)):
-        for stream in streams:
-            grow_copy(step, stream).wait_recv()
-            if step > 0:
-                grow_copy(step - 1, stream).start()
-
-    def join_copy(stream):
-        place = dense_out.at[pl.ds(4 * core + 2 * stream, 2)]
-        return remote(place, place, join_send.at[stream], join_recv.at[stream], across(1))
+    for _ in late:
+        pass
+    for _ in early:
+        pass
 
     for stream in streams:
-        join_copy(stream).start()
-    for stream in streams:
-        join_copy(stream).wait()
-        own_join(stream).wait()
-        for step in range(steps):
-            own_grow(step, stream).wait_send()
         for level in range(steps):
             expert_copy(level, stream).wait_send()
-        first_copy(stream).wait_send()
-        for step in range(1, steps):
-            later_copy(step, stream).wait_send()
-        for k in range(1, count):
-            line_copy(k, stream).wait_send()
-        for step in range(steps):
-            grow_copy(step, stream).wait_send()
-    for block in range(4):
-        core_copy(block).wait_send()
+        for chunk in range(2):
+            first_copy(chunk, stream).wait_send()
+            for step in range(1, steps):
+                later_copy(chunk, step, stream).wait_send()
+            for other in others:
+                line_copy(chunk, stream, me, other).wait_send()
+            for step in range(steps):
+                grow_copy(chunk, step, stream).wait_send()
+                own_grow(chunk, step, stream).wait_send()
+    for chunk in range(2):
+        for block in range(4):
+            core_copy(chunk, block).wait_send()
+        for other in others:
+            shard_copy(chunk, me, other).wait_send()
     for stage in range(len(gain_bits)):
         gain_copy(stage).wait_send()
-    for k in range(1, count):
-        shard_copy(k).wait_send()
-        gain_line(k).wait_send()
-        returning(lax.rem(me + k, count), me).wait_send()
+    for other in others:
+        gain_line(me, other).wait_send()
+        returning(other, me).wait_send()
     leave.wait()
 
 
@@ -1341,19 +1383,19 @@
             pltpu.VMEM((steps + 2,) + gains_shape, jnp.float32),
             pltpu.VMEM((steps + 1,) + gains_shape, jnp.float32),
             pltpu.VMEM((count,) + gains_shape, jnp.float32),
-            dma((4,)),
-            dma((4,)),
-            dma((4,)),
-            dma((steps, 2)),
-            dma((steps, 2)),
-            dma((count,)),
-            dma((count,)),
-            dma((steps, 2)),
-            dma((steps, 2)),
+            dma((6,)),
+            dma((2, 4)),
+            dma((2, 4)),
+            dma((2, steps, 2)),
+            dma((2, steps, 2)),
             dma((2, count)),
             dma((2, count)),
-            dma((2,)),
-            dma((2,)),
+            dma((2, steps, 2)),
+            dma((2, steps, 2)),
+            dma((2, 2, count)),
+            dma((2, 2, count)),
+            dma((2, 2)),
+            dma((2, 2)),
             dma((steps + 1, 2)),
             dma((steps + 1, 2)),
             dma((steps + 1,)),
@@ -1363,10 +1405,10 @@
             dma((count,)),
             dma((count,)),
             dma((2, 3)),
-            dma((steps, 2)),
-            dma((steps, 2)),
-            dma((2,)),
-            dma((2,)),
+            dma((2, steps, 2)),
+            dma((2, steps, 2)),
+            dma((2, 2)),
+            dma((2, 2)),
         ],
         compiler_params=pltpu.CompilerParams(
             collective_id=2, has_side_effects=True, vmem_limit_bytes=63 * 1024 * 1024

time: 404 us -> 419 us (1.037)
  Pallas kernels: 378 us -> 393 us
    pallas_call x1, Pallas kernels: 130 us -> 144 us  [spread(): pl.pallas_call(functools.partial(spread_kernel, count, bits), in_specs=[v...]
where the time goes in v5:
time: 419 us; the launch traced here: 412 us
  Pallas kernels  393 us (94%)
  other arithmetic  9.24 us (2%)
  local copies, waits for them, and re-layouts  8.59 us (2%)
    pallas_call x1, Pallas kernels, spread(): pl.pallas_call(functools.partial(spread_kernel, count, bits), in_specs=[v...  144 us
    pallas_call x1, Pallas kernels, moe(): pl.pallas_call(functools.partial(moe_kernel, count, bits), in_specs=[vmem...  110 us
    pallas_call x1, Pallas kernels, gather(): pl.pallas_call(functools.partial(gather_kernel, count, bits), in_specs=[v...  67.1 us
    pallas_call x2, Pallas kernels, expert_update(): pl.pallas_call(functools.partial(expert_update_kernel, kinds, scale), gri...  49.1 us
    pallas_call x1, Pallas kernels, dense_update(): pl.pallas_call(functools.partial(dense_update_kernel, layout), grid=(1,),...  22.8 us
  transfers between devices with their start and end apart: 2, of which 0 were waited for; matrix products, arithmetic and copies ran while one was open for 1% of the time, Pallas kernels for 12%

profile of v5, /device:TPU:0, one launch (start us, length us, event | category | flops | bytes accessed | tf_op | source)
XLA Modules:
  0.0 412.1 jit_solution(16869319984067491181)
XLA Ops:
  0.7 0.7 subtract_convert_fusion
  1.4 1.5 copy.56.column_ref
  2.9 0.7 stack.30
  3.5 0.7 stack.31
  4.2 0.5 multiply_cosine_fusion
  4.7 0.8 select_reduce_fusion
  5.5 0.6 pad_maximum_fusion.1.small_ref
  6.1 0.4 maximum_bitcast_fusion.1
  6.5 0.8 pad_maximum_fusion.table_ref
  7.3 67.1 %gather.1 = (bf16[3,4,256,1024]{3,2,1,0:T(8,128)(2,1)}, f32[4,24,256]{2,1,0:T(8,128)}, bf16[4,256,1024]{2,1,0:T(8,128)(2,1)}, f32[256,1024]{1,0:T(8,128)}, bf16[...) custom-call(bf16[256,1024]{1,0:T(8,128)(2,1)} %query_weight.1, ...), custom_call_target="tpu_custom_call" | custom-call | tf_op jit(solution)/shard_map/gather/pallas_call | solution.py:1698
  74.4 1.1 copy.57
  75.5 1.0 dynamic-slice_bitcast_fusion.weight_ref
  76.5 0.6 pad_add_fusion.place_ref
  77.0 110.0 %moe.1 = (bf16[4,256,1024]{2,1,0:T(8,128)(2,1)}, f32[256,1024]{1,0:T(8,128)}, bf16[4,3,2,64,512]{4,3,2,1,0:T(8,128)(2,1)}) custom-call(bf16[256,1024]{1,0:T(8,128)(2,1)} %get-tuple-element.67.own_ref, bf16[4,256,1024]{2,1,0:T(8,128)(2,1)} %get-tuple-element.68.cot_ref, f32[4,256,4]{2,1,0:T(8,128)} %dynamic-slice_bitcast_fusion.weight_ref, ...), custom_call_target="tpu_custom_call" | custom-call | flops 38999998464 | bytes 20000000 | tf_op jit(solution)/shard_map/moe/pallas_call | solution.py:709
  187.0 143.9 %spread.1 = (bf16[4,3,1024,512]{3,2,1,0:T(8,128)(2,1)}, bf16[8,4,256,384]{3,2,1,0:T(8,128)(2,1)}, bf16[8,256,384]{2,1,0:T(8,128)(2,1)}, f32[8,1024]{1,0:T(8,128)...) custom-call(bf16[4,3,2,64,512]{4,3,2,1,0:T(8,128)(2,1)} %get-tuple-element.70.share_ref, ...), custom_call_target="tpu_custom_call" | custom-call | tf_op jit(solution)/shard_map/spread/pallas_call | solution.py:1354
  330.9 22.8 %dense_update.1 = (f32[256,1024]{1,0:T(8,128)}, f32[256,1024]{1,0:T(8,128)}, f32[256,512]{1,0:T(8,128)}, f32[256,512]{1,0:T(8,128)}, f32[256,512]{1,0:T(8,128)},...) custom-call(s32[2]{0:T(128)} %pad_add_fusion.place_ref, ...), custom_call_target="tpu_custom_call" | custom-call | flops 14000000000 | bytes 25165824 | tf_op jit(solution)/shard_map/dense_update/pallas_call | solution.py:342
  353.7 0.4 collective-permute-start.1
  354.1 0.1 collective-permute-start
  354.2 31.3 %expert_update.2 = (f32[4,1024,512]{2,1,0:T(8,128)}, f32[4,1024,512]{2,1,0:T(8,128)}, f32[4,1024,512]{2,1,0:T(8,128)}, f32[4,1024,512]{2,1,0:T(8,128)}, f32[4,10...) custom-call(bf16[4,3,1024,512]{3,2,1,0:T(8,128)(2,1)} %get-tuple-element.95.refs_0_, f32[4,1024,512]{2,1,0:T(8,128)} %refs_1_.4, ...), custom_call_target="tpu_custom_call" | custom-call | flops 20000000000 | bytes 75497472 | tf_op jit(solution)/shard_map/expert_update/pallas_call | solution.py:257
  385.5 0.0 copy-start.4
  385.5 0.0 copy-start.5
  385.5 0.0 copy-start
  385.5 0.0 copy-start.1
  385.5 17.8 %expert_update.3 = (f32[4,512,1024]{2,1,0:T(8,128)}, f32[4,512,1024]{2,1,0:T(8,128)}, f32[4,512,1024]{2,1,0:T(8,128)}) custom-call(bf16[4,3,1024,512]{3,2,1,0:T(8,128)(2,1)} %get-tuple-element.95.refs_0_, f32[4,512,1024]{2,1,0:T(8,128)} %refs_1_.5), custom_call_target="tpu_custom_call" | custom-call | flops 10000000000 | bytes 37748736 | tf_op jit(solution)/shard_map/expert_update/pallas_call | solution.py:257
  403.3 0.8 fusion.5
  404.2 0.0 copy-start.2
  404.2 0.0 copy-start.3
  404.2 0.0 copy-done.4
  404.2 0.6 broadcast_multiply_fusion.1
  404.7 0.0 copy-done.5
  404.7 0.6 broadcast_multiply_fusion
  405.3 0.0 collective-permute-done.1
  405.3 2.3 broadcast_select_fusion.2
  407.6 0.0 collective-permute-done
  407.6 0.0 copy-done
  407.6 1.5 broadcast_select_fusion
  409.1 1.9 copy.61
  411.0 0.0 copy-done.1
  411.0 1.0 copy.62
  411.9 0.0 copy-done.2
  411.9 0.0 copy-done.3
  (3 shorter events, 0.0 us)
Async XLA Ops:
  353.7 51.6 %collective-permute-start.1 = (f32[256,512]{1,0:T(8,128)}, f32[256,512]{1,0:T(8,128)}, u32[]{:S(2)}, u32[]{:S(2)}) collective-permute-start(f32[256,512]{1,0:T(8,128)} %get-tuple-element.89), channel_id=1, source_target_pairs={{0,4},{4,0},{8,12},{12,8},{16,20},{20,16},{24,28},{28,24},{1,5},{5... | collective-permute-start | bytes 1572872 | tf_op jit(solution)/shard_map/ppermute | solution.py:1873
  354.1 53.5 %collective-permute-start = (f32[256,1024]{1,0:T(8,128)}, f32[256,1024]{1,0:T(8,128)S(1)}, u32[]{:S(2)}, u32[]{:S(2)}) collective-permute-start(f32[256,1024]{1,0:T(8,128)} %get-tuple-element.86), channel_id=1, source_target_pairs={{0,4},{4,0},{8,12},{12,8},{16,20},{20,16},{24,28},{28,24},{1,5},{5... | collective-permute-start | bytes 3145736 | tf_op jit(solution)/shard_map/ppermute | solution.py:1872
  385.5 18.7 %copy-start.4 = (f32[256]{0:T(256)S(1)}, f32[256]{0:T(256)}, u32[]{:S(2)}) copy-start(f32[256]{0:T(256)} %param.41) | copy-start | bytes 3076
  385.5 19.2 %copy-start.5 = (f32[256]{0:T(256)S(1)}, f32[256]{0:T(256)}, u32[]{:S(2)}) copy-start(f32[256]{0:T(256)} %param.42) | copy-start | bytes 3076
  385.5 22.1 %copy-start = (f32[256,1024]{1,0:T(8,128)S(1)}, f32[256,1024]{1,0:T(8,128)}, u32[]{:S(2)}) copy-start(f32[256,1024]{1,0:T(8,128)} %get-tuple-element.86) | copy-start | bytes 3145732
  385.5 25.4 %copy-start.1 = (f32[256,1024]{1,0:T(8,128)S(1)}, f32[256,1024]{1,0:T(8,128)}, u32[]{:S(2)}) copy-start(f32[256,1024]{1,0:T(8,128)} %get-tuple-element.151) | copy-start | bytes 3145732
  404.2 7.8 %copy-start.2 = (f32[1,256]{1,0:T(1,128)}, f32[1,256]{1,0:T(1,128)S(1)}, u32[]{:S(2)}) copy-start(f32[1,256]{1,0:T(1,128)S(1)} %get-tuple-element.115) | copy-start | bytes 3076
  404.2 7.8 %copy-start.3 = (f32[1,256]{1,0:T(1,128)}, f32[1,256]{1,0:T(1,128)S(1)}, u32[]{:S(2)}) copy-start(f32[1,256]{1,0:T(1,128)S(1)} %get-tuple-element.116) | copy-start | bytes 3076

commit v6 on v4

--- a/solution.py
+++ b/solution.py
@@ -209,11 +209,37 @@
     return (gram * (inverse * inverse), inverse)
 
 
-def expert_update_kernel(kinds, scale, *refs):
+def expert_update_kernel(kinds, scale, carried, *refs):
     a = newton_first
     grads_ref = refs[0]
     moments = refs[1 : 1 + len(kinds)]
-    outs = refs[1 + len(kinds) :]
+    given = refs[1 + len(kinds) : 1 + len(kinds) + carried]
+    outs = refs[1 + len(kinds) + carried :]
+    if carried:
+        taken = outs[3 * len(kinds) : 3 * len(kinds) + carried]
+        sem = outs[-1]
+        core = lax.axis_index("rep") % 2
+
+        def move(source, target):
+            return pltpu.make_async_copy(given[source], taken[target], sem.at[target])
+
+        @pl.when(pl.program_id(0) == 0)
+        def _():
+            for pair in (0, 2):
+
+                @pl.when(core == 0)
+                def _():
+                    move(pair, pair).start()
+                    move(pair + 1, pair + 1).start()
+
+                @pl.when(core == 1)
+                def _():
+                    move(pair + 1, pair).start()
+                    move(pair, pair + 1).start()
+
+            for index in range(4, carried):
+                move(index, index).start()
+
     half = grads_ref.shape[3]
     tall = kinds[0] < 2
     states = []
@@ -242,9 +268,15 @@
         else:
             step = jnp.dot(rest, low, preferred_element_type=jnp.float32)
         outs[3 * index + 2][e] = (-scale * a * a * inverse) * outs[3 * index + 1][e] + step
-
-
-def expert_update(grads, kinds, moments):
+    if carried:
+
+        @pl.when(pl.program_id(0) == pl.num_programs(0) - 1)
+        def _():
+            for index in range(carried):
+                move(index, index).wait()
+
+
+def expert_update(grads, kinds, moments, carried=()):
     count, rows, columns = moments[0].shape
     group = 2 // len(kinds)
     scale = rate_matrix * math.sqrt(max(1.0, columns / rows))
@@ -252,12 +284,15 @@
     place = kinds[0] // len(kinds)
     taken = pl.BlockSpec((group, len(kinds)) + grads.shape[2:], lambda i: (i, place, 0, 0))
     shape = jax.ShapeDtypeStruct(moments[0].shape, jnp.float32)
+    hand_on = [pl.BlockSpec(memory_space=pl.ANY)] * len(carried)
     return pl.pallas_call(
-        functools.partial(expert_update_kernel, kinds, scale),
+        functools.partial(expert_update_kernel, kinds, scale, len(carried)),
         grid=(count // group,),
-        in_specs=[taken] + [block] * len(kinds),
-        out_specs=[block] * (3 * len(kinds)),
-        out_shape=[shape] * (3 * len(kinds)),
+        in_specs=[taken] + [block] * len(kinds) + hand_on,
+        out_specs=[block] * (3 * len(kinds)) + hand_on,
+        out_shape=[shape] * (3 * len(kinds))
+        + [jax.ShapeDtypeStruct(array.shape, array.dtype) for array in carried],
+        scratch_shapes=[pltpu.SemaphoreType.DMA((len(carried),))] if carried else [],
         compiler_params=pltpu.CompilerParams(vmem_limit_bytes=60 * 1024 * 1024),
         name="expert_update",
         cost_estimate=pl.CostEstimate(
@@ -265,7 +300,7 @@
             bytes_accessed=moments[0].size * len(kinds) * 18,
             transcendentals=0,
         ),
-    )(grads, *moments)
+    )(grads, *moments, *carried)
 
 
 def dense_update_kernel(layout, place_ref, next_ref, grads_ref, *refs):
@@ -275,12 +310,20 @@
     outs = refs[amount : 3 * amount]
     updates = refs[3 * amount : 3 * amount + 2]
     matrices = refs[3 * amount + 2 : 3 * amount + 4]
-    own_grads = refs[3 * amount + 4]
+    own_grads, own_next, sem = refs[3 * amount + 4 :]
     blocks, count, block_rows, width = next_ref.shape
     part = width // 3
     me = place_ref[0]
     core = place_ref[1]
     start = pl.multiple_of(me * block_rows, block_rows)
+    loads = [
+        pltpu.make_async_copy(
+            own_moments[index], own_next.at[:, begin : begin + size], sem.at[2 * index]
+        )
+        for index, (begin, size) in enumerate(layout)
+    ]
+    for load in loads:
+        load.start()
 
     for block in range(blocks):
         outer = slice(block * part, (block + 1) * part)
@@ -295,10 +338,17 @@
         matrices[1][:, outer] = next_ref[
             core * (blocks // 2) + block, :, :, part : 2 * part
         ].reshape(count * block_rows, part)
+    leaving = []
     for index, (begin, size) in enumerate(layout):
-        grad = own_grads[:, begin : begin + size]
-        outs[2 * index][...] = grad
-        outs[2 * index + 1][...] = momentum_keep * own_moments[index][...] + grad
+        loads[index].wait()
+        lanes = slice(begin, begin + size)
+        own_next[:, lanes] = momentum_keep * own_next[:, lanes] + own_grads[:, lanes]
+        leaving += [
+            pltpu.make_async_copy(own_grads.at[:, lanes], outs[2 * index], sem.at[2 * index]),
+            pltpu.make_async_copy(own_next.at[:, lanes], outs[2 * index + 1], sem.at[2 * index + 1]),
+        ]
+        leaving[-2].start()
+        leaving[-1].start()
     states = []
     for matrix in matrices:
         low = matrix[...]
@@ -323,12 +373,15 @@
             a * once
             + jnp.dot(once.astype(jnp.bfloat16), second_low, preferred_element_type=jnp.float32)
         )
+    for copy in leaving:
+        copy.wait()
 
 
 def dense_update(nexts, grads, own_moments, layout, shard_index, rep_index):
     _, count, block_rows, _ = nexts.shape
     width = own_moments[0].shape[1]
     whole = lambda shape: pl.BlockSpec(shape, lambda i: (0,) * len(shape))
+    anywhere = pl.BlockSpec(memory_space=pl.ANY)
     shapes = []
     for _, size in layout:
         shapes += [jax.ShapeDtypeStruct((block_rows, size), jnp.float32)] * 2
@@ -341,13 +394,15 @@
         functools.partial(dense_update_kernel, layout),
         grid=(1,),
         in_specs=[pl.BlockSpec(memory_space=pltpu.SMEM), whole(nexts.shape), whole(grads.shape)]
-        + [whole(moment.shape) for moment in own_moments],
-        out_specs=[whole(shape.shape) for shape in shapes],
+        + [anywhere] * len(own_moments),
+        out_specs=[anywhere] * (2 * len(layout)) + [whole(shape.shape) for shape in shapes[-2:]],
         out_shape=shapes,
         scratch_shapes=[
             pltpu.VMEM((count * block_rows, width), jnp.bfloat16),
             pltpu.VMEM((count * block_rows, width // 2), jnp.bfloat16),
             pltpu.VMEM((block_rows, 3 * width), jnp.float32),
+            pltpu.VMEM((block_rows, 3 * width), jnp.float32),
+            pltpu.SemaphoreType.DMA((2 * len(layout),)),
         ],
         compiler_params=pltpu.CompilerParams(vmem_limit_bytes=63 * 1024 * 1024),
         name="dense_update",
@@ -1829,15 +1884,25 @@
     pairs = [(index, index + 1 - 2 * (index % 2)) for index in range(rep_count)]
     other_wide = lax.ppermute(own_wide, "rep", pairs)
     other_narrow = lax.ppermute(own_narrow, "rep", pairs)
-    first_core = rep_index % 2 == 0
-    query_update = jnp.where(first_core, own_wide, other_wide)
-    out_update = jnp.where(first_core, other_wide, own_wide)
-    key_update = jnp.where(first_core, own_narrow, other_narrow)
-    value_update = jnp.where(first_core, other_narrow, own_narrow)
     gate_grad, gate_next, gate_update, up_grad, up_next, up_update = expert_update(
         expert_grads, (0, 1), (gate_moment, up_moment)
     )
-    down_grad, down_next, down_update = expert_update(expert_grads, (2,), (down_moment,))
+    (
+        down_grad,
+        down_next,
+        down_update,
+        query_update,
+        out_update,
+        key_update,
+        value_update,
+        grad_tokens,
+        mixed,
+    ) = expert_update(
+        expert_grads,
+        (2,),
+        (down_moment,),
+        (own_wide, other_wide, own_narrow, other_narrow, grad_tokens, mixed),
+    )
     return (
         mixed,
         grad_tokens,

time: 404 us -> 533 us (1.32)
  Pallas kernels: 378 us -> 512 us
    pallas_call x2, Pallas kernels: 49.1 us -> 183 us  [expert_update(): pl.pallas_call(functools.partial(expert_update_kernel, kinds, scale, len(...]
  transfers between devices with their start and end apart: 2 -> 2, of which waited for: 0 -> 0; matrix products, arithmetic and copies ran while one was open for 1% -> 0% of each run, Pallas kernels for 12% -> 6%
where the time goes in v6:
time: 533 us; the launch traced here: 526 us
  Pallas kernels  512 us (96%)
  local copies, waits for them, and re-layouts  6.9 us (1%)
  other arithmetic  5.48 us (1%)
    pallas_call x2, Pallas kernels, expert_update(): pl.pallas_call(functools.partial(expert_update_kernel, kinds, scale, len(...  183 us
    pallas_call x1, Pallas kernels, spread(): pl.pallas_call(functools.partial(spread_kernel, count, bits), in_specs=[v...  130 us
    pallas_call x1, Pallas kernels, moe(): pl.pallas_call(functools.partial(moe_kernel, count, bits), in_specs=[vmem...  110 us
    pallas_call x1, Pallas kernels, gather(): pl.pallas_call(functools.partial(gather_kernel, count, bits), in_specs=[v...  67.1 us
    pallas_call x1, Pallas kernels, dense_update(): pl.pallas_call(functools.partial(dense_update_kernel, layout), grid=(1,),...  22.6 us
  transfers between devices with their start and end apart: 2, of which 0 were waited for; matrix products, arithmetic and copies ran while one was open for 0% of the time, Pallas kernels for 6%

profile of v6, /device:TPU:0, one launch (start us, length us, event | category | flops | bytes accessed | tf_op | source)
XLA Modules:
  0.0 526.0 jit_solution(11420317652899184857)
XLA Ops:
  0.7 0.7 stack.30
  1.4 0.7 stack.31
  2.0 0.7 subtract_convert_fusion
  2.7 1.5 copy.56.column_ref
  4.2 0.8 select_reduce_fusion
  4.9 0.6 pad_maximum_fusion.1.small_ref
  5.6 0.5 multiply_cosine_fusion
  6.1 0.4 maximum_bitcast_fusion.1
  6.5 0.8 pad_maximum_fusion.table_ref
  7.3 67.1 %gather.1 = (bf16[3,4,256,1024]{3,2,1,0:T(8,128)(2,1)}, f32[4,24,256]{2,1,0:T(8,128)}, bf16[4,256,1024]{2,1,0:T(8,128)(2,1)}, f32[256,1024]{1,0:T(8,128)}, bf16[...) custom-call(bf16[256,1024]{1,0:T(8,128)(2,1)} %query_weight.1, ...), custom_call_target="tpu_custom_call" | custom-call | tf_op jit(solution)/shard_map/gather/pallas_call | solution.py:1711
  74.3 1.1 copy.57
  75.4 0.6 pad_add_fusion.place_ref
  76.0 1.0 dynamic-slice_bitcast_fusion.weight_ref
  77.0 110.0 %moe.1 = (bf16[4,256,1024]{2,1,0:T(8,128)(2,1)}, f32[256,1024]{1,0:T(8,128)}, bf16[4,3,2,64,512]{4,3,2,1,0:T(8,128)(2,1)}) custom-call(bf16[256,1024]{1,0:T(8,128)(2,1)} %get-tuple-element.73.own_ref, bf16[4,256,1024]{2,1,0:T(8,128)(2,1)} %get-tuple-element.74.cot_ref, f32[4,256,4]{2,1,0:T(8,128)} %dynamic-slice_bitcast_fusion.weight_ref, ...), custom_call_target="tpu_custom_call" | custom-call | flops 38999998464 | bytes 20000000 | tf_op jit(solution)/shard_map/moe/pallas_call | solution.py:762
  187.0 129.5 %spread.1 = (bf16[4,3,1024,512]{3,2,1,0:T(8,128)(2,1)}, bf16[8,4,256,384]{3,2,1,0:T(8,128)(2,1)}, bf16[8,256,384]{2,1,0:T(8,128)(2,1)}, f32[8,1024]{1,0:T(8,128)...) custom-call(bf16[4,3,2,64,512]{4,3,2,1,0:T(8,128)(2,1)} %get-tuple-element.76.share_ref, ...), custom_call_target="tpu_custom_call" | custom-call | tf_op jit(solution)/shard_map/spread/pallas_call | solution.py:1367
  316.5 22.6 %dense_update.1 = (f32[256,1024]{1,0:T(8,128)}, f32[256,1024]{1,0:T(8,128)}, f32[256,512]{1,0:T(8,128)}, f32[256,512]{1,0:T(8,128)}, f32[256,512]{1,0:T(8,128)},...) custom-call(s32[2]{0:T(128)} %pad_add_fusion.place_ref, ...), custom_call_target="tpu_custom_call" | custom-call | flops 14000000000 | bytes 25165824 | tf_op jit(solution)/shard_map/dense_update/pallas_call | solution.py:393
  339.1 0.4 collective-permute-start.1
  339.5 0.1 collective-permute-start
  339.7 0.0 copy-start.2
  339.7 0.0 copy-start.3
  339.7 31.3 %expert_update.3 = (f32[4,1024,512]{2,1,0:T(8,128)}, f32[4,1024,512]{2,1,0:T(8,128)}, f32[4,1024,512]{2,1,0:T(8,128)}, f32[4,1024,512]{2,1,0:T(8,128)}, f32[4,10...) custom-call(bf16[4,3,1024,512]{3,2,1,0:T(8,128)(2,1)} %get-tuple-element.86.refs_0_, f32[4,1024,512]{2,1,0:T(8,128)} %refs_1_.5, ...), custom_call_target="tpu_custom_call" | custom-call | flops 20000000000 | bytes 75497472 | tf_op jit(solution)/shard_map/expert_update/pallas_call | solution.py:288
  371.0 0.8 fusion.5
  371.9 0.0 copy-start
  371.9 0.0 copy-start.1
  371.9 0.0 copy-done.2
  371.9 0.6 broadcast_multiply_fusion.1
  372.4 0.0 copy-done.3
  372.4 0.6 broadcast_multiply_fusion
  373.0 0.0 collective-permute-done.1.refs_5_
  373.0 0.0 copy-start.5
  373.0 0.0 collective-permute-done.refs_3_
  373.0 0.0 copy-start.4
  373.0 0.8 copy-done.5
  373.8 0.4 copy-done.4
  374.2 151.6 %expert_update.2 = (f32[4,512,1024]{2,1,0:T(8,128)}, f32[4,512,1024]{2,1,0:T(8,128)}, f32[4,512,1024]{2,1,0:T(8,128)}, f32[256,1024]{1,0:T(8,128)}, f32[256,1024...) custom-call(bf16[4,3,1024,512]{3,2,1,0:T(8,128)(2,1)} %get-tuple-elem, ...), custom_call_target="tpu_custom_call" | custom-call | flops 10000000000 | bytes 37748736 | tf_op jit(solution)/shard_map/expert_update/pallas_call | solution.py:288
  525.8 0.0 copy-done
  525.8 0.0 copy-done.1
  (3 shorter events, 0.0 us)
Async XLA Ops:
  339.1 33.9 %collective-permute-start.1 = (f32[256,512]{1,0:T(8,128)}, f32[256,512]{1,0:T(8,128)S(1)}, u32[]{:S(2)}, u32[]{:S(2)}) collective-permute-start(f32[256,512]{1,0:T(8,128)} %get-tuple-element.90.refs_4_), channel_id=1, source_target_pairs={{0,4},{4,0},{8,12},{12,8},{16,20},{20,16},{24,28},{28,24},{1,5},{5... | collective-permute-start | bytes 1572872 | tf_op jit(solution)/shard_map/ppermute | solution.py:1886
  339.5 33.5 %collective-permute-start = (f32[256,1024]{1,0:T(8,128)}, f32[256,1024]{1,0:T(8,128)S(1)}, u32[]{:S(2)}, u32[]{:S(2)}) collective-permute-start(f32[256,1024]{1,0:T(8,128)} %get-tuple-element.89.refs_2_), channel_id=1, source_target_pairs={{0,4},{4,0},{8,12},{12,8},{16,20},{20,16},{24,28},{28,24},{1,5},{5... | collective-permute-start | bytes 3145736 | tf_op jit(solution)/shard_map/ppermute | solution.py:1885
  339.7 32.2 %copy-start.2 = (f32[256]{0:T(256)S(1)}, f32[256]{0:T(256)}, u32[]{:S(2)}) copy-start(f32[256]{0:T(256)} %param.41) | copy-start | bytes 3076
  339.7 32.8 %copy-start.3 = (f32[256]{0:T(256)S(1)}, f32[256]{0:T(256)}, u32[]{:S(2)}) copy-start(f32[256]{0:T(256)} %param.42) | copy-start | bytes 3076
  371.9 153.9 %copy-start = (f32[1,256]{1,0:T(1,128)}, f32[1,256]{1,0:T(1,128)S(1)}, u32[]{:S(2)}) copy-start(f32[1,256]{1,0:T(1,128)S(1)} %get-tuple-element.123) | copy-start | bytes 3076
  371.9 153.9 %copy-start.1 = (f32[1,256]{1,0:T(1,128)}, f32[1,256]{1,0:T(1,128)S(1)}, u32[]{:S(2)}) copy-start(f32[1,256]{1,0:T(1,128)S(1)} %get-tuple-element.124) | copy-start | bytes 3076
  373.0 0.8 copy-start.5
  373.0 1.2 copy-start.4

commit v7 on v6

--- a/solution.py
+++ b/solution.py
@@ -217,28 +217,20 @@
     outs = refs[1 + len(kinds) + carried :]
     if carried:
         taken = outs[3 * len(kinds) : 3 * len(kinds) + carried]
-        sem = outs[-1]
+        held = outs[3 * len(kinds) + carried : -2]
+        load_sem, store_sem = outs[-2:]
         core = lax.axis_index("rep") % 2
 
-        def move(source, target):
-            return pltpu.make_async_copy(given[source], taken[target], sem.at[target])
+        def load(index):
+            return pltpu.make_async_copy(given[index], held[index], load_sem.at[index])
+
+        def store(source, target):
+            return pltpu.make_async_copy(held[source], taken[target], store_sem.at[target])
 
         @pl.when(pl.program_id(0) == 0)
         def _():
-            for pair in (0, 2):
-
-                @pl.when(core == 0)
-                def _():
-                    move(pair, pair).start()
-                    move(pair + 1, pair + 1).start()
-
-                @pl.when(core == 1)
-                def _():
-                    move(pair + 1, pair).start()
-                    move(pair, pair + 1).start()
-
-            for index in range(4, carried):
-                move(index, index).start()
+            for index in range(carried):
+                load(index).start()
 
     half = grads_ref.shape[3]
     tall = kinds[0] < 2
@@ -270,10 +262,29 @@
         outs[3 * index + 2][e] = (-scale * a * a * inverse) * outs[3 * index + 1][e] + step
     if carried:
 
+        @pl.when(pl.program_id(0) == 0)
+        def _():
+            for index in range(carried):
+                load(index).wait()
+            for pair in (0, 2):
+
+                @pl.when(core == 0)
+                def _():
+                    store(pair, pair).start()
+                    store(pair + 1, pair + 1).start()
+
+                @pl.when(core == 1)
+                def _():
+                    store(pair + 1, pair).start()
+                    store(pair, pair + 1).start()
+
+            for index in range(4, carried):
+                store(index, index).start()
+
         @pl.when(pl.program_id(0) == pl.num_programs(0) - 1)
         def _():
             for index in range(carried):
-                move(index, index).wait()
+                store(index, index).wait()
 
 
 def expert_update(grads, kinds, moments, carried=()):
@@ -292,7 +303,8 @@
         out_specs=[block] * (3 * len(kinds)) + hand_on,
         out_shape=[shape] * (3 * len(kinds))
         + [jax.ShapeDtypeStruct(array.shape, array.dtype) for array in carried],
-        scratch_shapes=[pltpu.SemaphoreType.DMA((len(carried),))] if carried else [],
+        scratch_shapes=[pltpu.VMEM(array.shape, array.dtype) for array in carried]
+        + [pltpu.SemaphoreType.DMA((len(carried),))] * (2 if carried else 0),
         compiler_params=pltpu.CompilerParams(vmem_limit_bytes=60 * 1024 * 1024),
         name="expert_update",
         cost_estimate=pl.CostEstimate(

time: 533 us -> 402 us (0.75)
  Pallas kernels: 512 us -> 381 us
    pallas_call x2, Pallas kernels: 183 us -> 51.9 us  [expert_update(): pl.pallas_call(functools.partial(expert_update_kernel, kinds, scale, len(...]
  transfers between devices with their start and end apart: 2 -> 2, of which waited for: 0 -> 0; matrix products, arithmetic and copies ran while one was open for 0% -> 1% of each run, Pallas kernels for 6% -> 8%
where the time goes in v7:
time: 402 us; the launch traced here: 395 us
  Pallas kernels  381 us (95%)
  local copies, waits for them, and re-layouts  6.9 us (2%)
  other arithmetic  5.48 us (1%)
    pallas_call x1, Pallas kernels, spread(): pl.pallas_call(functools.partial(spread_kernel, count, bits), in_specs=[v...  130 us
    pallas_call x1, Pallas kernels, moe(): pl.pallas_call(functools.partial(moe_kernel, count, bits), in_specs=[vmem...  110 us
    pallas_call x1, Pallas kernels, gather(): pl.pallas_call(functools.partial(gather_kernel, count, bits), in_specs=[v...  67.1 us
    pallas_call x2, Pallas kernels, expert_update(): pl.pallas_call(functools.partial(expert_update_kernel, kinds, scale, len(...  51.9 us
    pallas_call x1, Pallas kernels, dense_update(): pl.pallas_call(functools.partial(dense_update_kernel, layout), grid=(1,),...  22.6 us
  transfers between devices with their start and end apart: 2, of which 0 were waited for; matrix products, arithmetic and copies ran while one was open for 1% of the time, Pallas kernels for 8%

profile of v7, /device:TPU:0, one launch (start us, length us, event | category | flops | bytes accessed | tf_op | source)
XLA Modules:
  0.0 395.0 jit_solution(14367667987885237500)
XLA Ops:
  0.7 0.7 stack.30
  1.4 0.7 stack.31
  2.0 0.7 subtract_convert_fusion
  2.7 1.5 copy.56.column_ref
  4.2 0.8 select_reduce_fusion
  4.9 0.6 pad_maximum_fusion.1.small_ref
  5.6 0.5 multiply_cosine_fusion
  6.1 0.4 maximum_bitcast_fusion.1
  6.5 0.8 pad_maximum_fusion.table_ref
  7.3 67.1 %gather.1 = (bf16[3,4,256,1024]{3,2,1,0:T(8,128)(2,1)}, f32[4,24,256]{2,1,0:T(8,128)}, bf16[4,256,1024]{2,1,0:T(8,128)(2,1)}, f32[256,1024]{1,0:T(8,128)}, bf16[...) custom-call(bf16[256,1024]{1,0:T(8,128)(2,1)} %query_weight.1, ...), custom_call_target="tpu_custom_call" | custom-call | tf_op jit(solution)/shard_map/gather/pallas_call | solution.py:1723
  74.3 1.1 copy.57
  75.4 0.6 pad_add_fusion.place_ref
  76.0 1.0 dynamic-slice_bitcast_fusion.weight_ref
  77.0 110.0 %moe.1 = (bf16[4,256,1024]{2,1,0:T(8,128)(2,1)}, f32[256,1024]{1,0:T(8,128)}, bf16[4,3,2,64,512]{4,3,2,1,0:T(8,128)(2,1)}) custom-call(bf16[256,1024]{1,0:T(8,128)(2,1)} %get-tuple-element.73.own_ref, bf16[4,256,1024]{2,1,0:T(8,128)(2,1)} %get-tuple-element.74.cot_ref, f32[4,256,4]{2,1,0:T(8,128)} %dynamic-slice_bitcast_fusion.weight_ref, ...), custom_call_target="tpu_custom_call" | custom-call | flops 38999998464 | bytes 20000000 | tf_op jit(solution)/shard_map/moe/pallas_call | solution.py:774
  187.0 129.5 %spread.1 = (bf16[4,3,1024,512]{3,2,1,0:T(8,128)(2,1)}, bf16[8,4,256,384]{3,2,1,0:T(8,128)(2,1)}, bf16[8,256,384]{2,1,0:T(8,128)(2,1)}, f32[8,1024]{1,0:T(8,128)...) custom-call(bf16[4,3,2,64,512]{4,3,2,1,0:T(8,128)(2,1)} %get-tuple-element.76.share_ref, ...), custom_call_target="tpu_custom_call" | custom-call | tf_op jit(solution)/shard_map/spread/pallas_call | solution.py:1379
  316.5 22.6 %dense_update.1 = (f32[256,1024]{1,0:T(8,128)}, f32[256,1024]{1,0:T(8,128)}, f32[256,512]{1,0:T(8,128)}, f32[256,512]{1,0:T(8,128)}, f32[256,512]{1,0:T(8,128)},...) custom-call(s32[2]{0:T(128)} %pad_add_fusion.place_ref, ...), custom_call_target="tpu_custom_call" | custom-call | flops 14000000000 | bytes 25165824 | tf_op jit(solution)/shard_map/dense_update/pallas_call | solution.py:405
  339.1 0.4 collective-permute-start.1
  339.5 0.1 collective-permute-start
  339.7 0.0 copy-start.2
  339.7 0.0 copy-start.3
  339.7 31.3 %expert_update.3 = (f32[4,1024,512]{2,1,0:T(8,128)}, f32[4,1024,512]{2,1,0:T(8,128)}, f32[4,1024,512]{2,1,0:T(8,128)}, f32[4,1024,512]{2,1,0:T(8,128)}, f32[4,10...) custom-call(bf16[4,3,1024,512]{3,2,1,0:T(8,128)(2,1)} %get-tuple-element.86.refs_0_, f32[4,1024,512]{2,1,0:T(8,128)} %refs_1_.5, ...), custom_call_target="tpu_custom_call" | custom-call | flops 20000000000 | bytes 75497472 | tf_op jit(solution)/shard_map/expert_update/pallas_call | solution.py:299
  371.0 0.8 fusion.5
  371.9 0.0 copy-start
  371.9 0.0 copy-start.1
  371.9 0.0 copy-done.2
  371.9 0.6 broadcast_multiply_fusion.1
  372.4 0.0 copy-done.3
  372.4 0.6 broadcast_multiply_fusion
  373.0 0.0 collective-permute-done.1.refs_5_
  373.0 0.0 copy-start.5
  373.0 0.0 collective-permute-done.refs_3_
  373.0 0.0 copy-start.4
  373.0 0.8 copy-done.5
  373.8 0.4 copy-done.4
  374.2 20.5 %expert_update.2 = (f32[4,512,1024]{2,1,0:T(8,128)}, f32[4,512,1024]{2,1,0:T(8,128)}, f32[4,512,1024]{2,1,0:T(8,128)}, f32[256,1024]{1,0:T(8,128)}, f32[256,1024...) custom-call(bf16[4,3,1024,512]{3,2,1,0:T(8,128)(2,1)} %get-tuple-elem, ...), custom_call_target="tpu_custom_call" | custom-call | flops 10000000000 | bytes 37748736 | tf_op jit(solution)/shard_map/expert_update/pallas_call | solution.py:299
  394.7 0.0 copy-done
  394.7 0.0 copy-done.1
  (3 shorter events, 0.0 us)
Async XLA Ops:
  339.1 33.9 %collective-permute-start.1 = (f32[256,512]{1,0:T(8,128)}, f32[256,512]{1,0:T(8,128)S(1)}, u32[]{:S(2)}, u32[]{:S(2)}) collective-permute-start(f32[256,512]{1,0:T(8,128)} %get-tuple-element.90.refs_4_), channel_id=1, source_target_pairs={{0,4},{4,0},{8,12},{12,8},{16,20},{20,16},{24,28},{28,24},{1,5},{5... | collective-permute-start | bytes 1572872 | tf_op jit(solution)/shard_map/ppermute | solution.py:1898
  339.5 33.5 %collective-permute-start = (f32[256,1024]{1,0:T(8,128)}, f32[256,1024]{1,0:T(8,128)S(1)}, u32[]{:S(2)}, u32[]{:S(2)}) collective-permute-start(f32[256,1024]{1,0:T(8,128)} %get-tuple-element.89.refs_2_), channel_id=1, source_target_pairs={{0,4},{4,0},{8,12},{12,8},{16,20},{20,16},{24,28},{28,24},{1,5},{5... | collective-permute-start | bytes 3145736 | tf_op jit(solution)/shard_map/ppermute | solution.py:1897
  339.7 32.2 %copy-start.2 = (f32[256]{0:T(256)S(1)}, f32[256]{0:T(256)}, u32[]{:S(2)}) copy-start(f32[256]{0:T(256)} %param.41) | copy-start | bytes 3076
  339.7 32.8 %copy-start.3 = (f32[256]{0:T(256)S(1)}, f32[256]{0:T(256)}, u32[]{:S(2)}) copy-start(f32[256]{0:T(256)} %param.42) | copy-start | bytes 3076
  371.9 22.9 %copy-start = (f32[1,256]{1,0:T(1,128)}, f32[1,256]{1,0:T(1,128)S(1)}, u32[]{:S(2)}) copy-start(f32[1,256]{1,0:T(1,128)S(1)} %get-tuple-element.123) | copy-start | bytes 3076
  371.9 22.9 %copy-start.1 = (f32[1,256]{1,0:T(1,128)}, f32[1,256]{1,0:T(1,128)S(1)}, u32[]{:S(2)}) copy-start(f32[1,256]{1,0:T(1,128)S(1)} %get-tuple-element.124) | copy-start | bytes 3076
  373.0 0.8 copy-start.5
  373.0 1.2 copy-start.4

commit v8 on v7

--- a/solution.py
+++ b/solution.py
@@ -86,11 +86,12 @@
     return jnp.where(lane_low((half, rows.shape[1])), rows[:half], rows[half:])
 
 
-def allowed_pairs(start_column, start_row):
-    shape = (start_column.shape[0], start_row.shape[1])
+def allowed_pairs(start_row):
+    shape = (start_row.shape[1], start_row.shape[1])
+    keys = jnp.broadcast_to(start_row.astype(jnp.float32), shape)
     query_places = lax.broadcasted_iota(jnp.int32, shape, 0)
     key_places = lax.broadcasted_iota(jnp.int32, shape, 1)
-    one = (start_column == start_row) & (key_places <= query_places)
+    one = (keys.T == keys) & (key_places <= query_places)
     return jnp.where(jnp.concatenate([one, one], axis=0), 0.0, masked_score)
 
 
@@ -496,6 +497,8 @@
         back_recv,
         sum_send,
         sum_recv,
+        core_send,
+        core_recv,
     ) = rest[1 + 2 * len(bits) :]
     rep = lax.axis_index("rep")
     me = lax.axis_index("shard")
@@ -677,9 +680,17 @@
             device_id_type=MESH,
         )
 
+    def core_copy(e, kind):
+        return pltpu.make_async_remote_copy(
+            src_ref=mats.at[e, kind, rows_of((1 - core) * half, half)],
+            dst_ref=landing[0].at[e, kind],
+            send_sem=core_send.at[e, kind],
+            recv_sem=core_recv.at[e, kind],
+            device_id=(flip(rep, 1), me),
+            device_id_type=MESH,
+        )
+
     def copies(stage, e):
-        if stage == 0:
-            return [(sum_copy(0, 0, e, (1 - core) * half, half, 1), 0, core * half, half)]
         return [
             (
                 sum_copy(stage, 1 + 2 * (stage - 1) + stream, e, send, size, bit),
@@ -691,6 +702,15 @@
         ]
 
     def finish(stage, e):
+        if stage == 0:
+            place = rows_of(core * half, half)
+            for kind in range(3):
+                core_copy(e, kind).wait_recv()
+                mats[e, kind, place] = (
+                    mats[e, kind, place].astype(jnp.float32)
+                    + landing[0][e, kind].astype(jnp.float32)
+                ).astype(jnp.bfloat16)
+            return
         for copy, slot, keep, size in copies(stage, e):
             copy.wait_recv()
             place = rows_of(keep, size)
@@ -705,12 +725,15 @@
         if turn < experts:
             e = turn
             sums(last, e, factors(e, last), (sum_back, sum_out))
-            for side in range(2):
-                part = slice(side * half, (side + 1) * half)
-                mats[e, 0, part] = dot(turned[part], gate_delta[e]).astype(jnp.bfloat16)
-                mats[e, 1, part] = dot(turned[part], up_delta[e]).astype(jnp.bfloat16)
-                mats[e, 2, part] = dot(hid[e], cot_ref[:, :, part].reshape(count * tokens, half)).astype(jnp.bfloat16)
-            copies(0, e)[0][0].start()
+            for kind in range(3):
+                for side in range(2):
+                    part = slice(side * half, (side + 1) * half)
+                    if kind == 2:
+                        values = dot(hid[e], cot_ref[:, :, part].reshape(count * tokens, half))
+                    else:
+                        values = dot(turned[part], (gate_delta, up_delta)[kind][e])
+                    mats[e, kind, part] = values.astype(jnp.bfloat16)
+                core_copy(e, kind).start()
             if e == experts - 1:
                 stage_back[last] = sum_back[...].astype(jnp.bfloat16)
                 stage_out[last] = sum_out[...].astype(jnp.bfloat16)
@@ -743,7 +766,9 @@
         block = lax.rem(me + k, count)
         returning(stage_back, got_back, back_send, back_recv, block).wait_send()
     for e in range(experts):
-        for stage in range(stages):
+        for kind in range(3):
+            core_copy(e, kind).wait_send()
+        for stage in range(1, stages):
             for copy, _, _, _ in copies(stage, e):
                 copy.wait_send()
     for block in range(count):
@@ -802,6 +827,8 @@
             dma((count,)),
             dma((slots, experts)),
             dma((slots, experts)),
+            dma((experts, 3)),
+            dma((experts, 3)),
         ],
         compiler_params=pltpu.CompilerParams(
             collective_id=1, has_side_effects=True, vmem_limit_bytes=63 * 1024 * 1024
@@ -839,7 +866,6 @@
     pair_ref,
     total_ref,
     table_ref,
-    column_ref,
     row_ref,
     query_moment,
     key_moment,
@@ -1010,7 +1036,7 @@
     tokens_out[...] = grad_middle
     branch_ref[...] = grad_middle.astype(jnp.bfloat16)
     heads_ref[...] = dot_nt(branch_ref[...], whole(2)).astype(jnp.bfloat16)
-    bias = allowed_pairs(column_ref[...], row_ref[...])
+    bias = allowed_pairs(row_ref[...])
     attend_backward(query_ref, pair_ref, bias, total_ref, heads_ref, table_ref, delta_ref)
 
     part = dense_ref.shape[3] // 3
@@ -1378,7 +1404,7 @@
     dma = pltpu.SemaphoreType.DMA
     return pl.pallas_call(
         functools.partial(spread_kernel, count, bits),
-        in_specs=[vmem] * 16 + [pl.BlockSpec(memory_space=pl.ANY)] * 4,
+        in_specs=[vmem] * 15 + [pl.BlockSpec(memory_space=pl.ANY)] * 4,
         out_specs=[pl.BlockSpec(memory_space=pl.ANY)] + [vmem] * 5,
         out_shape=[
             jax.ShapeDtypeStruct((experts, 3, 4 * (final << steps), hidden), low),
@@ -1454,7 +1480,6 @@
         pair,
         log_total,
         tables,
-        starts[:, None],
         starts[None, :],
         *moments,
     )
@@ -1471,7 +1496,6 @@
     tokens_ref,
     cot_ref,
     table_ref,
-    column_ref,
     row_ref,
     weights_hbm,
     small_out,
@@ -1677,7 +1701,7 @@
         return weights_out[index].reshape(count * rows, width)
 
     project_inputs(first_out[...], whole, query_out, pair_out, table_ref)
-    bias = allowed_pairs(column_ref[...], row_ref[...])
+    bias = allowed_pairs(row_ref[...])
     if count > 2:
         line_step(2)
     attend_forward(range(KVHEADS // 2), query_out, pair_out, bias, head_out, total_out)
@@ -1722,7 +1746,7 @@
     features = jax.ShapeDtypeStruct((token_count, width), low)
     return pl.pallas_call(
         functools.partial(gather_kernel, count, bits),
-        in_specs=[vmem] * 10,
+        in_specs=[vmem] * 9,
         out_specs=[pl.BlockSpec(memory_space=pl.ANY)] + [vmem] * 9,
         out_shape=[
             whole,
@@ -1762,7 +1786,6 @@
         tokens,
         cotangent,
         tables,
-        starts[:, None],
         starts[None, :],
     )
 

time: 402 us -> 399 us (level)
  the two profiles are of different devices: /device:TPU:0 before, /device:TPU:9 now
where the time goes in v8:
time: 399 us; the launch traced here: 392 us
  Pallas kernels  379 us (95%)
  other arithmetic  5.48 us (1%)
  local copies, waits for them, and re-layouts  5.43 us (1%)
    pallas_call x1, Pallas kernels, spread(): pl.pallas_call(functools.partial(spread_kernel, count, bits), in_specs=[v...  139 us
    pallas_call x1, Pallas kernels, moe(): pl.pallas_call(functools.partial(moe_kernel, count, bits), in_specs=[vmem...  103 us
    pallas_call x1, Pallas kernels, gather(): pl.pallas_call(functools.partial(gather_kernel, count, bits), in_specs=[v...  62.8 us
    pallas_call x2, Pallas kernels, expert_update(): pl.pallas_call(functools.partial(expert_update_kernel, kinds, scale, len(...  51.9 us
    pallas_call x1, Pallas kernels, dense_update(): pl.pallas_call(functools.partial(dense_update_kernel, layout), grid=(1,),...  22.6 us
  transfers between devices with their start and end apart: 2, of which 0 were waited for; matrix products, arithmetic and copies ran while one was open for 1% of the time, Pallas kernels for 8%

profile of v8, /device:TPU:9, one launch (start us, length us, event | category | flops | bytes accessed | tf_op | source)
XLA Modules:
  0.0 391.7 jit_solution(9813539977965368695)
XLA Ops:
  0.7 0.7 stack.30
  1.4 0.7 stack.31
  2.0 0.7 subtract_convert_fusion
  2.7 0.8 select_reduce_fusion
  3.5 0.6 pad_maximum_fusion.1.small_ref
  4.1 0.5 multiply_cosine_fusion
  4.6 0.4 maximum_bitcast_fusion.1
  5.0 0.8 pad_maximum_fusion.table_ref
  5.8 62.8 %gather.1 = (bf16[3,4,256,1024]{3,2,1,0:T(8,128)(2,1)}, f32[4,24,256]{2,1,0:T(8,128)}, bf16[4,256,1024]{2,1,0:T(8,128)(2,1)}, f32[256,1024]{1,0:T(8,128)}, bf16[...) custom-call(bf16[256,1024]{1,0:T(8,128)(2,1)} %query_weight.1, ...), custom_call_target="tpu_custom_call" | custom-call | tf_op jit(solution)/shard_map/gather/pallas_call | solution.py:1747
  68.6 1.1 copy.53
  69.7 0.6 pad_add_fusion.place_ref
  70.2 1.0 dynamic-slice_bitcast_fusion.weight_ref
  71.2 102.7 %moe.1 = (bf16[4,256,1024]{2,1,0:T(8,128)(2,1)}, f32[256,1024]{1,0:T(8,128)}, bf16[4,3,2,64,512]{4,3,2,1,0:T(8,128)(2,1)}) custom-call(bf16[256,1024]{1,0:T(8,128)(2,1)} %get-tuple-element.73.own_ref, bf16[4,256,1024]{2,1,0:T(8,128)(2,1)} %get-tuple-element.74.cot_ref, f32[4,256,4]{2,1,0:T(8,128)} %dynamic-slice_bitcast_fusion.weight_ref, ...), custom_call_target="tpu_custom_call" | custom-call | flops 38999998464 | bytes 20000000 | tf_op jit(solution)/shard_map/moe/pallas_call | solution.py:799
  173.9 139.3 %spread.1 = (bf16[4,3,1024,512]{3,2,1,0:T(8,128)(2,1)}, bf16[8,4,256,384]{3,2,1,0:T(8,128)(2,1)}, bf16[8,256,384]{2,1,0:T(8,128)(2,1)}, f32[8,1024]{1,0:T(8,128)...) custom-call(bf16[4,3,2,64,512]{4,3,2,1,0:T(8,128)(2,1)} %get-tuple-element.76.share_ref, ...), custom_call_target="tpu_custom_call" | custom-call | tf_op jit(solution)/shard_map/spread/pallas_call | solution.py:1405
  313.3 22.6 %dense_update.1 = (f32[256,1024]{1,0:T(8,128)}, f32[256,1024]{1,0:T(8,128)}, f32[256,512]{1,0:T(8,128)}, f32[256,512]{1,0:T(8,128)}, f32[256,512]{1,0:T(8,128)},...) custom-call(s32[2]{0:T(128)} %pad_add_fusion.place_ref, ...), custom_call_target="tpu_custom_call" | custom-call | flops 14000000000 | bytes 25165824 | tf_op jit(solution)/shard_map/dense_update/pallas_call | solution.py:406
  335.8 0.2 collective-permute-start.1
  336.1 0.4 collective-permute-start
  336.4 0.0 copy-start.2
  336.4 0.0 copy-start.3
  336.4 31.3 %expert_update.3 = (f32[4,1024,512]{2,1,0:T(8,128)}, f32[4,1024,512]{2,1,0:T(8,128)}, f32[4,1024,512]{2,1,0:T(8,128)}, f32[4,1024,512]{2,1,0:T(8,128)}, f32[4,10...) custom-call(bf16[4,3,1024,512]{3,2,1,0:T(8,128)(2,1)} %get-tuple-element.86.refs_0_, f32[4,1024,512]{2,1,0:T(8,128)} %refs_1_.5, ...), custom_call_target="tpu_custom_call" | custom-call | flops 20000000000 | bytes 75497472 | tf_op jit(solution)/shard_map/expert_update/pallas_call | solution.py:300
  367.8 0.8 fusion.5
  368.6 0.0 copy-start
  368.6 0.0 copy-start.1
  368.6 0.0 copy-done.2
  368.6 0.6 broadcast_multiply_fusion.1
  369.2 0.0 copy-done.3
  369.2 0.6 broadcast_multiply_fusion
  369.8 0.0 collective-permute-done.1.refs_5_
  369.8 0.0 copy-start.5
  369.8 0.0 collective-permute-done.refs_3_
  369.8 0.0 copy-start.4
  369.8 0.8 copy-done.5
  370.6 0.4 copy-done.4
  370.9 20.5 %expert_update.2 = (f32[4,512,1024]{2,1,0:T(8,128)}, f32[4,512,1024]{2,1,0:T(8,128)}, f32[4,512,1024]{2,1,0:T(8,128)}, f32[256,1024]{1,0:T(8,128)}, f32[256,1024...) custom-call(bf16[4,3,1024,512]{3,2,1,0:T(8,128)(2,1)} %get-tuple-elem, ...), custom_call_target="tpu_custom_call" | custom-call | flops 10000000000 | bytes 37748736 | tf_op jit(solution)/shard_map/expert_update/pallas_call | solution.py:300
  391.5 0.0 copy-done
  391.5 0.0 copy-done.1
  (3 shorter events, 0.0 us)
Async XLA Ops:
  335.8 33.9 %collective-permute-start.1 = (f32[256,512]{1,0:T(8,128)}, f32[256,512]{1,0:T(8,128)S(1)}, u32[]{:S(2)}, u32[]{:S(2)}) collective-permute-start(f32[256,512]{1,0:T(8,128)} %get-tuple-element.90.refs_4_), channel_id=1, source_target_pairs={{0,4},{4,0},{8,12},{12,8},{16,20},{20,16},{24,28},{28,24},{1,5},{5... | collective-permute-start | bytes 1572872 | tf_op jit(solution)/shard_map/ppermute | solution.py:1921
  336.1 33.7 %collective-permute-start = (f32[256,1024]{1,0:T(8,128)}, f32[256,1024]{1,0:T(8,128)S(1)}, u32[]{:S(2)}, u32[]{:S(2)}) collective-permute-start(f32[256,1024]{1,0:T(8,128)} %get-tuple-element.89.refs_2_), channel_id=1, source_target_pairs={{0,4},{4,0},{8,12},{12,8},{16,20},{20,16},{24,28},{28,24},{1,5},{5... | collective-permute-start | bytes 3145736 | tf_op jit(solution)/shard_map/ppermute | solution.py:1920
  336.4 32.2 %copy-start.2 = (f32[256]{0:T(256)S(1)}, f32[256]{0:T(256)}, u32[]{:S(2)}) copy-start(f32[256]{0:T(256)} %param.41) | copy-start | bytes 3076
  336.4 32.8 %copy-start.3 = (f32[256]{0:T(256)S(1)}, f32[256]{0:T(256)}, u32[]{:S(2)}) copy-start(f32[256]{0:T(256)} %param.42) | copy-start | bytes 3076
  368.6 22.9 %copy-start = (f32[1,256]{1,0:T(1,128)}, f32[1,256]{1,0:T(1,128)S(1)}, u32[]{:S(2)}) copy-start(f32[1,256]{1,0:T(1,128)S(1)} %get-tuple-element.123) | copy-start | bytes 3076
  368.6 22.9 %copy-start.1 = (f32[1,256]{1,0:T(1,128)}, f32[1,256]{1,0:T(1,128)S(1)}, u32[]{:S(2)}) copy-start(f32[1,256]{1,0:T(1,128)S(1)} %get-tuple-element.124) | copy-start | bytes 3076
  369.8 0.8 copy-start.5
  369.8 1.2 copy-start.4

commit v9 on v8

--- a/solution.py
+++ b/solution.py
@@ -856,7 +856,7 @@
     returned_ref,
     normed_ref,
     head_ref,
-    weights_ref,
+    weights_hbm,
     small_ref,
     tokens_ref,
     cot_ref,
@@ -878,6 +878,7 @@
     tokens_out,
     mixed_out,
     experts_out,
+    weights_ref,
     got_ref,
     moment_piece,
     delta_ref,
@@ -924,6 +925,7 @@
         own_recv,
         own_join_send,
         own_join_recv,
+        weights_sem,
     ) = rest[later:]
     rep = lax.axis_index("rep")
     me = lax.axis_index("shard")
@@ -982,6 +984,8 @@
             local_sem.at[stream],
         )
 
+    weights_load = pltpu.make_async_copy(weights_hbm, weights_ref, weights_sem.at[0])
+    weights_load.start()
     for stream in streams:
         own_copy(stream).start()
     peers = [(rep, lax.rem(me + k, count)) for k in range(1, count)]
@@ -1035,6 +1039,7 @@
     grad_middle = cot_ref[...].astype(jnp.float32) + middle_extra
     tokens_out[...] = grad_middle
     branch_ref[...] = grad_middle.astype(jnp.bfloat16)
+    weights_load.wait()
     heads_ref[...] = dot_nt(branch_ref[...], whole(2)).astype(jnp.bfloat16)
     bias = allowed_pairs(row_ref[...])
     attend_backward(query_ref, pair_ref, bias, total_ref, heads_ref, table_ref, delta_ref)
@@ -1404,7 +1409,10 @@
     dma = pltpu.SemaphoreType.DMA
     return pl.pallas_call(
         functools.partial(spread_kernel, count, bits),
-        in_specs=[vmem] * 15 + [pl.BlockSpec(memory_space=pl.ANY)] * 4,
+        in_specs=[vmem] * 4
+        + [pl.BlockSpec(memory_space=pl.ANY)]
+        + [vmem] * 10
+        + [pl.BlockSpec(memory_space=pl.ANY)] * 4,
         out_specs=[pl.BlockSpec(memory_space=pl.ANY)] + [vmem] * 5,
         out_shape=[
             jax.ShapeDtypeStruct((experts, 3, 4 * (final << steps), hidden), low),
@@ -1416,6 +1424,7 @@
         ],
         scratch_shapes=[
             pltpu.VMEM((experts, 3, 4 * (final << steps), hidden), low),
+            pltpu.VMEM(weights.shape, low),
             pltpu.VMEM((count, token_count, features), low),
             pltpu.VMEM((2, last, width), jnp.float32),
             pltpu.VMEM((token_count, 2 * features), low),
@@ -1460,6 +1469,7 @@
             dma((steps, 2)),
             dma((2,)),
             dma((2,)),
+            dma((1,)),
         ],
         compiler_params=pltpu.CompilerParams(
             collective_id=2, has_side_effects=True, vmem_limit_bytes=63 * 1024 * 1024

time: 399 us -> 397 us (level)
  no operation moved by 1% of the time
where the time goes in v9:
time: 397 us; the launch traced here: 390 us
  Pallas kernels  377 us (95%)
  other arithmetic  5.48 us (1%)
  local copies, waits for them, and re-layouts  5.43 us (1%)
    pallas_call x1, Pallas kernels, spread(): pl.pallas_call(functools.partial(spread_kernel, count, bits), in_specs=[v...  137 us
    pallas_call x1, Pallas kernels, moe(): pl.pallas_call(functools.partial(moe_kernel, count, bits), in_specs=[vmem...  103 us
    pallas_call x1, Pallas kernels, gather(): pl.pallas_call(functools.partial(gather_kernel, count, bits), in_specs=[v...  62.8 us
    pallas_call x2, Pallas kernels, expert_update(): pl.pallas_call(functools.partial(expert_update_kernel, kinds, scale, len(...  51.9 us
    pallas_call x1, Pallas kernels, dense_update(): pl.pallas_call(functools.partial(dense_update_kernel, layout), grid=(1,),...  22.6 us
  transfers between devices with their start and end apart: 2, of which 0 were waited for; matrix products, arithmetic and copies ran while one was open for 1% of the time, Pallas kernels for 8%

profile of v9, /device:TPU:9, one launch (start us, length us, event | category | flops | bytes accessed | tf_op | source)
XLA Modules:
  0.0 389.7 jit_solution(16514320871075861508)
XLA Ops:
  0.7 0.7 stack.30
  1.4 0.7 stack.31
  2.0 0.7 subtract_convert_fusion
  2.7 0.8 select_reduce_fusion
  3.5 0.6 pad_maximum_fusion.1.small_ref
  4.1 0.5 multiply_cosine_fusion
  4.6 0.4 maximum_bitcast_fusion.1
  5.0 0.8 pad_maximum_fusion.table_ref
  5.8 62.8 %gather.1 = (bf16[3,4,256,1024]{3,2,1,0:T(8,128)(2,1)}, f32[4,24,256]{2,1,0:T(8,128)}, bf16[4,256,1024]{2,1,0:T(8,128)(2,1)}, f32[256,1024]{1,0:T(8,128)}, bf16[...) custom-call(bf16[256,1024]{1,0:T(8,128)(2,1)} %query_weight.1, ...), custom_call_target="tpu_custom_call" | custom-call | tf_op jit(solution)/shard_map/gather/pallas_call | solution.py:1757
  68.6 1.1 copy.53
  69.7 0.6 pad_add_fusion.place_ref
  70.2 1.0 dynamic-slice_bitcast_fusion.weight_ref
  71.2 102.7 %moe.1 = (bf16[4,256,1024]{2,1,0:T(8,128)(2,1)}, f32[256,1024]{1,0:T(8,128)}, bf16[4,3,2,64,512]{4,3,2,1,0:T(8,128)(2,1)}) custom-call(bf16[256,1024]{1,0:T(8,128)(2,1)} %get-tuple-element.73.own_ref, bf16[4,256,1024]{2,1,0:T(8,128)(2,1)} %get-tuple-element.74.cot_ref, f32[4,256,4]{2,1,0:T(8,128)} %dynamic-slice_bitcast_fusion.weight_ref, ...), custom_call_target="tpu_custom_call" | custom-call | flops 38999998464 | bytes 20000000 | tf_op jit(solution)/shard_map/moe/pallas_call | solution.py:799
  173.9 137.3 %spread.1 = (bf16[4,3,1024,512]{3,2,1,0:T(8,128)(2,1)}, bf16[8,4,256,384]{3,2,1,0:T(8,128)(2,1)}, bf16[8,256,384]{2,1,0:T(8,128)(2,1)}, f32[8,1024]{1,0:T(8,128)...) custom-call(bf16[4,3,2,64,512]{4,3,2,1,0:T(8,128)(2,1)} %get-tuple-element.76.share_ref, ...), custom_call_target="tpu_custom_call" | custom-call | tf_op jit(solution)/shard_map/spread/pallas_call | solution.py:1410
  311.2 22.6 %dense_update.1 = (f32[256,1024]{1,0:T(8,128)}, f32[256,1024]{1,0:T(8,128)}, f32[256,512]{1,0:T(8,128)}, f32[256,512]{1,0:T(8,128)}, f32[256,512]{1,0:T(8,128)},...) custom-call(s32[2]{0:T(128)} %pad_add_fusion.place_ref, ...), custom_call_target="tpu_custom_call" | custom-call | flops 14000000000 | bytes 25165824 | tf_op jit(solution)/shard_map/dense_update/pallas_call | solution.py:406
  333.8 0.2 collective-permute-start.1
  334.0 0.4 collective-permute-start
  334.4 0.0 copy-start.2
  334.4 0.0 copy-start.3
  334.4 31.3 %expert_update.3 = (f32[4,1024,512]{2,1,0:T(8,128)}, f32[4,1024,512]{2,1,0:T(8,128)}, f32[4,1024,512]{2,1,0:T(8,128)}, f32[4,1024,512]{2,1,0:T(8,128)}, f32[4,10...) custom-call(bf16[4,3,1024,512]{3,2,1,0:T(8,128)(2,1)} %get-tuple-element.86.refs_0_, f32[4,1024,512]{2,1,0:T(8,128)} %refs_1_.5, ...), custom_call_target="tpu_custom_call" | custom-call | flops 20000000000 | bytes 75497472 | tf_op jit(solution)/shard_map/expert_update/pallas_call | solution.py:300
  365.7 0.8 fusion.5
  366.6 0.0 copy-start
  366.6 0.0 copy-start.1
  366.6 0.0 copy-done.2
  366.6 0.6 broadcast_multiply_fusion.1
  367.2 0.0 copy-done.3
  367.2 0.6 broadcast_multiply_fusion
  367.7 0.0 collective-permute-done.1.refs_5_
  367.7 0.0 copy-start.5
  367.8 0.0 collective-permute-done.refs_3_
  367.8 0.0 copy-start.4
  367.8 0.8 copy-done.5
  368.5 0.4 copy-done.4
  368.9 20.5 %expert_update.2 = (f32[4,512,1024]{2,1,0:T(8,128)}, f32[4,512,1024]{2,1,0:T(8,128)}, f32[4,512,1024]{2,1,0:T(8,128)}, f32[256,1024]{1,0:T(8,128)}, f32[256,1024...) custom-call(bf16[4,3,1024,512]{3,2,1,0:T(8,128)(2,1)} %get-tuple-elem, ...), custom_call_target="tpu_custom_call" | custom-call | flops 10000000000 | bytes 37748736 | tf_op jit(solution)/shard_map/expert_update/pallas_call | solution.py:300
  389.5 0.0 copy-done
  389.5 0.0 copy-done.1
  (3 shorter events, 0.0 us)
Async XLA Ops:
  333.8 33.9 %collective-permute-start.1 = (f32[256,512]{1,0:T(8,128)}, f32[256,512]{1,0:T(8,128)S(1)}, u32[]{:S(2)}, u32[]{:S(2)}) collective-permute-start(f32[256,512]{1,0:T(8,128)} %get-tuple-element.90.refs_4_), channel_id=1, source_target_pairs={{0,4},{4,0},{8,12},{12,8},{16,20},{20,16},{24,28},{28,24},{1,5},{5... | collective-permute-start | bytes 1572872 | tf_op jit(solution)/shard_map/ppermute | solution.py:1931
  334.0 33.7 %collective-permute-start = (f32[256,1024]{1,0:T(8,128)}, f32[256,1024]{1,0:T(8,128)S(1)}, u32[]{:S(2)}, u32[]{:S(2)}) collective-permute-start(f32[256,1024]{1,0:T(8,128)} %get-tuple-element.89.refs_2_), channel_id=1, source_target_pairs={{0,4},{4,0},{8,12},{12,8},{16,20},{20,16},{24,28},{28,24},{1,5},{5... | collective-permute-start | bytes 3145736 | tf_op jit(solution)/shard_map/ppermute | solution.py:1930
  334.4 32.2 %copy-start.2 = (f32[256]{0:T(256)S(1)}, f32[256]{0:T(256)}, u32[]{:S(2)}) copy-start(f32[256]{0:T(256)} %param.41) | copy-start | bytes 3076
  334.4 32.8 %copy-start.3 = (f32[256]{0:T(256)S(1)}, f32[256]{0:T(256)}, u32[]{:S(2)}) copy-start(f32[256]{0:T(256)} %param.42) | copy-start | bytes 3076
  366.6 22.9 %copy-start = (f32[1,256]{1,0:T(1,128)}, f32[1,256]{1,0:T(1,128)S(1)}, u32[]{:S(2)}) copy-start(f32[1,256]{1,0:T(1,128)S(1)} %get-tuple-element.123) | copy-start | bytes 3076
  366.6 22.9 %copy-start.1 = (f32[1,256]{1,0:T(1,128)}, f32[1,256]{1,0:T(1,128)S(1)}, u32[]{:S(2)}) copy-start(f32[1,256]{1,0:T(1,128)S(1)} %get-tuple-element.124) | copy-start | bytes 3076
  367.7 0.8 copy-start.5
  367.8 1.2 copy-start.4
